TPU v7x, 512 devices: a whole 4x4x16 slice. The times are simulated.
512 devices in a mesh: row: 16 (over z), col: 32 (over x, y, core).
Axes of the slice: x: 4, y: 4, z: 16, core: 2. Of those that a mesh axis runs over, the one named last changes fastest.
Arguments:
- coords: float32 [3, 65536], P(None, ('row', 'col')), may hold values from -1 to 1
- residual_in: float32 [65536, 512], P(('row', 'col')), may hold values from -6 to 6
- link_mask: int32 [512, 2], P(('row', 'col')), may hold values 0 or 1
- compress: float32 [65536, 256], P(('row', 'col')), may hold values from -0.5 to 0.5
- expand: float32 [65536, 256], P(('row', 'col')), may hold values from -0.375 to 0.375
- level_gain: float32 [512, 1280], P(('row', 'col')), may hold values from 0.5 to 1.5
- level_couple: float32 [131072, 1280], P(('row', 'col')), may hold values from -0.1875 to 0.1875
- partner_perm: int32 [512, 5, 256], P(('row', 'col')), may hold values from 0 to 255, each once within a row
Outputs:
- new_residual: float32 [65536, 512], P(('row', 'col'))
- res_norms: float32 [512], replicated
Inputs may be any that keep to these rules, and one draw needn't show every extreme that they name: `partner_perm`: each row of 256 entries names every number once.
All inputs are finite; a program needn't handle non-finite values. No bound on the sum of `link_mask` on one device may be relied on, other than what follows from the above.
Results may differ from a plain program's by a relative error of at most 0.0003.
Values sent between devices are 32-bit elements; how exact they have to be, the bound alone decides.
No kernel may reach another device: no remote copies, remote signals or barrier semaphores. Data moves between devices by JAX's collectives and lax.ppermute only.
A program may use at most 64 MiB of HBM per device.

v0:
```python
import jax
import jax.numpy as jnp
from jax import lax
from jax.sharding import PartitionSpec as P

ROW_LEVELS = 2
COL_LEVELS = 3


WAVENUM = 6.0
SOFTEN = 0.01


def in_blocks(shard, dim, length):
    shape = shard.shape
    tiles = shard.reshape(*shape[:dim], length, shape[dim] // length, *shape[dim + 1 :])
    return jnp.moveaxis(tiles, dim, 0)


def sent_and_summed(shard, axis, dim):
    length = lax.axis_size(axis)
    tiles = lax.all_to_all(in_blocks(shard, dim, length), axis, 0, 0, tiled=True)
    return jnp.sum(tiles, axis=0)


def side_by_side(arrays, axis, dim, along):
    widths = [a.shape[along] for a in arrays]
    both = jnp.concatenate(arrays, axis=along)
    whole = sent_and_summed(both, axis, dim)
    return tuple(jnp.split(whole, [sum(widths[:k]) for k in range(1, len(widths))], axis=along))


def from_everyone(shard, axis):
    length = lax.axis_size(axis)
    return lax.all_to_all(
        jnp.broadcast_to(shard[None], (length, *shard.shape)), axis, 0, 0, tiled=True
    )


def over_copies(shard, axis):
    return from_everyone(shard, axis).sum(axis=0)


def packed_total(arrays, axis):
    ends = [0]
    for a in arrays:
        ends.append(ends[-1] + a.size)
    so_far = over_copies(jnp.concatenate([a.ravel() for a in arrays]), axis)
    return tuple((so_far[b:e].reshape(a.shape) for a, b, e in zip(arrays, ends, ends[1:])))


def gather_turned(arrays, axis, dims):
    turned = [jnp.moveaxis(a, dim, 0) for a, dim in zip(arrays, dims)]
    both = jnp.concatenate([t.reshape(len(t), -1) for t in turned], axis=1)
    whole, at, finished = (lax.all_gather(both, axis, axis=0, tiled=True), 0, [])
    for t, dim in zip(turned, dims):
        piece = whole[:, at : at + t[0].size].reshape(-1, *t.shape[1:])
        finished.append(jnp.moveaxis(piece, 0, dim))
        at += t[0].size
    return tuple(finished)


def from_behind(block, axis, distance):
    devices = range(lax.axis_size(axis))
    route = [(i - distance, i) for i in devices if i - distance in devices]
    return lax.ppermute(block, axis, route)


def from_partner(block, axis, distance):
    count = lax.axis_size(axis)
    route = []
    for low in range(count):
        high = low | 1 << distance
        if high != low and high < count:
            route += [(low, high), (high, low)]
    return lax.ppermute(block, axis, route)


def kernel_tile(own_xyz, other_xyz):
    dist_sq = (own_xyz[0][:, None] - other_xyz[0][None, :]) ** 2
    dist_sq = dist_sq + (own_xyz[1][:, None] - other_xyz[1][None, :]) ** 2
    dist_sq = dist_sq + (own_xyz[2][:, None] - other_xyz[2][None, :]) ** 2
    return jnp.cos(WAVENUM * jnp.sqrt(dist_sq)) / jnp.sqrt(dist_sq + SOFTEN)


def matmul_hi(left, right):
    return jnp.dot(left, right, precision=lax.Precision.HIGHEST)


def inner_cols(left, right):
    return lax.dot_general(left, right, (((0,), (0,)), ((), ())), precision=lax.Precision.HIGHEST)


def chol_solve(gram_mat, cross_mat):
    factor = jnp.linalg.cholesky(gram_mat)
    middle = lax.linalg.triangular_solve(factor, cross_mat, left_side=True, lower=True)
    return lax.linalg.triangular_solve(factor, middle, left_side=True, lower=True, transpose_a=True)


def global_sum(members):
    shares = side_by_side((members[0], members[1], members[2]), "col", 1, 0)
    shares = packed_total((shares[0], shares[1], shares[2]), "row")
    return gather_turned((shares[0], shares[1], shares[2]), "col", (1, 1, 1))


def shards(
    coords, residual_in, link_mask, compress, expand, level_gain, level_couple, partner_perm
):
    below_xyz, below_rhs = from_behind((coords, residual_in), ("row", "col"), 1)
    above_xyz, above_rhs = from_behind((coords, residual_in), ("row", "col"), -1)
    rank_width = compress.shape[1]
    coeffs = inner_cols(compress, residual_in)

    def mix_level(current, partner, level_at):
        taken_rows = partner_perm[0, level_at]
        picked = jnp.take(partner, taken_rows, axis=0)
        gain_col = level_gain[0, level_at * rank_width : (level_at + 1) * rank_width][:, None]
        couple = level_couple[:, level_at * rank_width : (level_at + 1) * rank_width]
        return gain_col * current + matmul_hi(couple, picked)

    row_top = lax.axis_size("row").bit_length() - 2
    for index_row in range(ROW_LEVELS):
        partner = from_partner(coeffs, "row", row_top - index_row)
        coeffs = mix_level(coeffs, partner, index_row)
    col_top = lax.axis_size("col").bit_length() - 2
    for index_col in range(COL_LEVELS):
        partner = from_partner(coeffs, "col", col_top - index_col)
        coeffs = mix_level(coeffs, partner, ROW_LEVELS + index_col)
    far_field = matmul_hi(expand, coeffs)
    weights = link_mask.astype(jnp.float32)
    near_scale = (3.0 * coords.shape[1]) ** (-0.5)
    near_field = matmul_hi(kernel_tile(coords, coords), residual_in)
    near_field = near_field + weights[0, 0] * matmul_hi(kernel_tile(coords, below_xyz), below_rhs)
    near_field = near_field + weights[0, 1] * matmul_hi(kernel_tile(coords, above_xyz), above_rhs)
    near_field = near_scale * near_field
    image = 2.0 * residual_in + near_field + far_field
    gram_mat = inner_cols(image, image)
    cross_mat = inner_cols(image, residual_in)
    points_total = coords.shape[1] * lax.axis_size("row") * lax.axis_size("col")
    self_squares = jnp.sum(residual_in * residual_in, axis=0)[None, :]
    gram_mat, cross_mat, self_total = global_sum((gram_mat, cross_mat, self_squares))
    alpha_mix = chol_solve(gram_mat, cross_mat)
    new_residual = residual_in - matmul_hi(image, alpha_mix)
    col_total = self_total[0] - jnp.sum(alpha_mix * cross_mat, axis=0)
    res_norms = jnp.sqrt(col_total / points_total)
    return (new_residual, res_norms)


def solution(mesh):
    return jax.shard_map(
        shards,
        mesh=mesh,
        in_specs=(
            P(None, ("row", "col")),
            P(("row", "col"), None),
            P(("row", "col"), None),
            P(("row", "col"), None),
            P(("row", "col"), None),
            P(("row", "col"), None),
            P(("row", "col"), None),
            P(("row", "col"), None, None),
        ),
        out_specs=(P(("row", "col"), None), P()),
        check_vma=False,
    )
```

profile of v0, /device:TPU:1, one launch (start us, length us, event | category | flops | bytes accessed | tf_op | source)
XLA Modules:
  0.0 550.0 jit_solution(8922406250387740012)
XLA Ops:
  7.2 4.6 collective-permute-start
  11.8 6.0 %collective-permute-start.2 = (f32[3,128]{1,0:T(4,128)}, f32[3,128]{1,0:T(4,128)}, u32[]{:S(2)}, u32[]{:S(2)}) collective-permute-start(f32[3,128]{1,0:T(4,128)} %param.10), channel_id=1, source_target_pairs={{1,0},{2,1},{3,2},{4,3},{5,4},{6,5},{7,6},{8,7},{9,8},{10,9},{11,1... | collective-permute-start | bytes 4616 | tf_op jit(solution)/shard_map/ppermute | solution.py:66
  17.9 1.9 collective-permute-start.1
  19.8 2.4 collective-permute-start.3
  22.2 1.6 fusion.166
  23.8 16.8 %collective-permute-start.4 = (f32[256,512]{1,0:T(8,128)S(1)}, f32[256,512]{1,0:T(8,128)S(1)}, u32[]{:S(2)}, u32[]{:S(2)}) collective-permute-start(f32[256,512]{1,0:T(8,128)S(1)} %fusion.166), channel_id=1, source_target_pairs={{0,256},{256,0},{32,288},{288,32},{64,320},{320,64},{96,352},{352,... | collective-permute-start | bytes 1572872 | tf_op jit(solution)/shard_map/ppermute | solution.py:76
  45.5 8.0 %collective-permute-done.4 = f32[256,512]{1,0:T(8,128)S(1)} collective-permute-done((f32[256,512]{1,0:T(8,128)S(1)}, f32[256,512]{1,0:T(8,128)S(1)}, u32[]{:S(2)}, u32[]{:S(2)}) %collective-permute-start.4) | collective-permute-done | bytes 524320 | tf_op jit(solution)/shard_map/ppermute | solution.py:76
  54.5 1.7 fusion
  56.2 36.6 %collective-permute-start.5 = (f32[256,512]{1,0:T(8,128)S(1)}, f32[256,512]{1,0:T(8,128)S(1)}, u32[]{:S(2)}, u32[]{:S(2)}) collective-permute-start(f32[256,512]{1,0:T(8,128)S(1)} %fusion), channel_id=1, source_target_pairs={{0,128},{128,0},{32,160},{160,32},{64,192},{192,64},{96,224},{224,... | collective-permute-start | bytes 1572872 | tf_op jit(solution)/shard_map/ppermute | solution.py:76
  92.8 42.3 %collective-permute-done.5 = f32[256,512]{1,0:T(8,128)S(1)} collective-permute-done((f32[256,512]{1,0:T(8,128)S(1)}, f32[256,512]{1,0:T(8,128)S(1)}, u32[]{:S(2)}, u32[]{:S(2)}) %collective-permute-start.5) | collective-permute-done | bytes 524320 | tf_op jit(solution)/shard_map/ppermute | solution.py:76
  136.2 1.7 multiply_add_fusion.2
  137.9 1.9 collective-permute-start.6
  141.2 13.2 %collective-permute-done.6 = f32[256,512]{1,0:T(8,128)S(1)} collective-permute-done((f32[256,512]{1,0:T(8,128)S(1)}, f32[256,512]{1,0:T(8,128)S(1)}, u32[]{:S(2)}, u32[]{:S(2)}) %collective-permute-start.6) | collective-permute-done | bytes 524320 | tf_op jit(solution)/shard_map/ppermute | solution.py:76
  155.3 1.7 multiply_add_fusion.1
  157.0 1.9 collective-permute-start.7
  161.7 9.3 %collective-permute-done.7 = f32[256,512]{1,0:T(8,128)S(1)} collective-permute-done((f32[256,512]{1,0:T(8,128)S(1)}, f32[256,512]{1,0:T(8,128)S(1)}, u32[]{:S(2)}, u32[]{:S(2)}) %collective-permute-start.7) | collective-permute-done | bytes 524320 | tf_op jit(solution)/shard_map/ppermute | solution.py:76
  172.1 1.7 multiply_add_fusion
  173.8 2.4 collective-permute-start.8
  179.7 8.7 %collective-permute-done.8 = f32[256,512]{1,0:T(8,128)S(1)} collective-permute-done((f32[256,512]{1,0:T(8,128)S(1)}, f32[256,512]{1,0:T(8,128)S(1)}, u32[]{:S(2)}, u32[]{:S(2)}) %collective-permute-start.8) | collective-permute-done | bytes 524320 | tf_op jit(solution)/shard_map/ppermute | solution.py:76
  189.5 1.7 convolution_bitcast_fusion
  194.2 37.4 %all_to_all.11 = f32[32,1025,16]{1,2,0:T(8,128)S(1)} all-to-all(f32[32,1025,16]{1,2,0:T(8,128)S(1)} %maximum_bitcast_fusion), channel_id=1, replica_groups=mesh['row'=16,'col'=32] {'col'}, dimensions={0} | all-to-all | bytes 4198400 | tf_op jit(solution)/shard_map/all_to_all | solution.py:22
  232.9 66.3 %all_to_all.12 = f32[16,1,16400]{2,1,0:T(1,128)S(1)} all-to-all(f32[16,1,16400]{2,1,0:T(1,128)S(1)} %broadcast_in_dim.18), channel_id=1, replica_groups=mesh['row'=16,'col'=32] {'row'}, dimensions={0} | all-to-all | bytes 2099200 | tf_op jit(solution)/shard_map/all_to_all | solution.py:35
  301.2 48.2 %all-gather.2.cloned.1.call-done = f32[512,1025]{1,0:T(8,128)} async-done(((f32[16,1025]{1,0:T(8,128)}), f32[512,1025]{1,0:T(8,128)}) %all-gather.2.cloned.1.call-update) | async-done | bytes 2099216 | tf_op jit(solution)/shard_map/all_gather | solution.py:55
  349.4 2.4 slice_bitcast_fusion.1
  351.8 1.6 copy.108
  355.6 12.3 %cholesky.104 = f32[128,128]{1,0:T(8,128)} custom-call(f32[128,128]{1,0:T(8,128)S(1)} %cholesky.266), custom_call_target="Cholesky" | custom-call | tf_op jit(solution)/shard_map/jit(cholesky)/cholesky | solution.py:95
  368.9 1.5 select_reduce_fusion.3
  370.4 11.3 %custom-call.32 = f32[1,128,128]{1,2,0:T(8,128)} custom-call(f32[1,128,128]{2,1,0:T(8,128)} %get-tuple-element.36), custom_call_target="InvertDiagBlocksLowerTriangular" | custom-call | tf_op jit(solution)/shard_map/jit(cholesky)/cholesky | solution.py:95
  385.5 13.2 %cholesky.217 = f32[128,128]{1,0:T(8,128)} custom-call(f32[128,128]{1,0:T(8,128)} %cholesky.270), custom_call_target="Cholesky" | custom-call | tf_op jit(solution)/shard_map/jit(cholesky)/cholesky | solution.py:95
  398.6 1.5 select_reduce_fusion.2
  400.1 11.5 %custom-call.33 = f32[1,128,128]{1,2,0:T(8,128)} custom-call(f32[1,128,128]{2,1,0:T(8,128)} %get-tuple-element.33), custom_call_target="InvertDiagBlocksLowerTriangular" | custom-call | tf_op jit(solution)/shard_map/jit(cholesky)/cholesky | solution.py:95
  415.3 13.2 %cholesky.238 = f32[128,128]{1,0:T(8,128)} custom-call(f32[128,128]{1,0:T(8,128)} %cholesky.275), custom_call_target="Cholesky" | custom-call | tf_op jit(solution)/shard_map/jit(cholesky)/cholesky | solution.py:95
  430.6 11.3 %custom-call.34 = f32[1,128,128]{1,2,0:T(8,128)} custom-call(f32[1,128,128]{2,1,0:T(8,128)} %get-tuple-element.30), custom_call_target="InvertDiagBlocksLowerTriangular" | custom-call | tf_op jit(solution)/shard_map/jit(cholesky)/cholesky | solution.py:95
  443.0 1.9 convolution_subtract_fusion.9
  444.8 13.4 %cholesky.255 = f32[128,128]{1,0:T(8,128)} custom-call(f32[128,128]{1,0:T(8,128)} %convolution_subtract_fusion.9), custom_call_target="Cholesky" | custom-call | tf_op jit(solution)/shard_map/jit(cholesky)/cholesky | solution.py:95
  464.1 14.2 %while.1 = (s32[]{:T(128)}, f32[512,512]{1,0:T(8,128)}, s32[4,2]{0,1:T(2,128)S(1)}, f32[4,128,128]{2,1,0:T(8,128)}, s32[]{:T(128)}) while((s32[]{:T(128)}, f32[512,512]{1,0:T(8,128)}, s32[4,2]{0,1:T(2,128)S(1)}, f32[4,128,128]{2,1,0:T(8,128)}, s32[]{:T(128)}) %tuple.50), condition=%wide.while_cond, body=%wide.while_body.sunk | while | flops 2 | bytes 132705 | solution.py:97
  464.8 2.9 bitcast_dynamic-update-slice_fusion.2
  468.3 2.9 bitcast_dynamic-update-slice_fusion.2
  471.9 2.9 bitcast_dynamic-update-slice_fusion.2
  475.4 2.8 bitcast_dynamic-update-slice_fusion.2
  478.3 40.7 %custom-call.35 = f32[4,128,128]{1,2,0:T(8,128)} custom-call(f32[4,128,128]{2,1,0:T(8,128)} %get-tuple-element.10), custom_call_target="InvertDiagBlocksLowerTriangular" | custom-call | tf_op jit(solution)/shard_map/triangular_solve | solution.py:97
  520.5 1.6 convolution_subtract_fusion.3
  522.5 1.9 convolution_subtract_fusion.2
  524.8 2.4 convolution_subtract_fusion.5
  532.1 2.3 convolution_subtract_fusion.4
  534.4 1.8 copy.113
  537.2 1.6 fusion.113
  538.9 2.9 convolution_subtract_fusion.6
  (145 shorter events, 52.4 us)
Async XLA Ops:
  7.2 15.1 %copy-start = (f32[128,256]{1,0:T(8,128)S(1)}, f32[128,256]{1,0:T(8,128)}, u32[]{:S(2)}) copy-start(f32[128,256]{1,0:T(8,128)} %param.13) | copy-start | bytes 393220
  7.2 342.2 %all-gather.2.cloned.1.call-start = ((), (), s32[]{:S(2)}) async-start(), calls=%async_computation.2 | async-start | bytes 2433024 | tf_op jit(solution)/shard_map/all_gather | solution.py:55
  7.2 153.1 %collective-permute-start = (f32[3,128]{1,0:T(4,128)}, f32[3,128]{1,0:T(4,128)}, u32[]{:S(2)}, u32[]{:S(2)}) collective-permute-start(f32[3,128]{1,0:T(4,128)} %param.10), channel_id=1, source_target_pairs={{0,1},{1,2},{2,3},{3,4},{4,5},{5,6},{6,7},{7,8},{8,9},{9,10},{10,1... | collective-permute-start | bytes 4616 | tf_op jit(solution)/shard_map/ppermute | solution.py:66
  11.8 164.4 %collective-permute-start.2 = (f32[3,128]{1,0:T(4,128)}, f32[3,128]{1,0:T(4,128)}, u32[]{:S(2)}, u32[]{:S(2)}) collective-permute-start(f32[3,128]{1,0:T(4,128)} %param.10), channel_id=1, source_target_pairs={{1,0},{2,1},{3,2},{4,3},{5,4},{6,5},{7,6},{8,7},{9,8},{10,9},{11,1... | collective-permute-start | bytes 4616 | tf_op jit(solution)/shard_map/ppermute | solution.py:66
  17.9 159.1 %collective-permute-start.1 = (f32[128,512]{1,0:T(8,128)}, f32[128,512]{1,0:T(8,128)S(1)}, u32[]{:S(2)}, u32[]{:S(2)}) collective-permute-start(f32[128,512]{1,0:T(8,128)} %param.11), channel_id=1, source_target_pairs={{0,1},{1,2},{2,3},{3,4},{4,5},{5,6},{6,7},{7,8},{8,9},{9,10},{10,1... | collective-permute-start | bytes 786440 | tf_op jit(solution)/shard_map/ppermute | solution.py:66
  19.8 158.6 %collective-permute-start.3 = (f32[128,512]{1,0:T(8,128)}, f32[128,512]{1,0:T(8,128)S(1)}, u32[]{:S(2)}, u32[]{:S(2)}) collective-permute-start(f32[128,512]{1,0:T(8,128)} %param.11), channel_id=1, source_target_pairs={{1,0},{2,1},{3,2},{4,3},{5,4},{6,5},{7,6},{8,7},{9,8},{10,9},{11,1... | collective-permute-start | bytes 786440 | tf_op jit(solution)/shard_map/ppermute | solution.py:66
  23.8 29.7 %collective-permute-start.4 = (f32[256,512]{1,0:T(8,128)S(1)}, f32[256,512]{1,0:T(8,128)S(1)}, u32[]{:S(2)}, u32[]{:S(2)}) collective-permute-start(f32[256,512]{1,0:T(8,128)S(1)} %fusion.166), channel_id=1, source_target_pairs={{0,256},{256,0},{32,288},{288,32},{64,320},{320,64},{96,352},{352,... | collective-permute-start | bytes 1572872 | tf_op jit(solution)/shard_map/ppermute | solution.py:76
  56.2 79.0 %collective-permute-start.5 = (f32[256,512]{1,0:T(8,128)S(1)}, f32[256,512]{1,0:T(8,128)S(1)}, u32[]{:S(2)}, u32[]{:S(2)}) collective-permute-start(f32[256,512]{1,0:T(8,128)S(1)} %fusion), channel_id=1, source_target_pairs={{0,128},{128,0},{32,160},{160,32},{64,192},{192,64},{96,224},{224,... | collective-permute-start | bytes 1572872 | tf_op jit(solution)/shard_map/ppermute | solution.py:76
  136.1 4.3 copy-start.20
  136.2 4.3 copy-start.2
  137.9 16.4 %collective-permute-start.6 = (f32[256,512]{1,0:T(8,128)S(1)}, f32[256,512]{1,0:T(8,128)S(1)}, u32[]{:S(2)}, u32[]{:S(2)}) collective-permute-start(f32[256,512]{1,0:T(8,128)S(1)} %multiply_add_fusion.2), channel_id=1, source_target_pairs={{0,16},{16,0},{1,17},{17,1},{2,18},{18,2},{3,19},{19,3},{4,20},{20... | collective-permute-start | bytes 1572872 | tf_op jit(solution)/shard_map/ppermute | solution.py:76
  157.0 14.0 %collective-permute-start.7 = (f32[256,512]{1,0:T(8,128)S(1)}, f32[256,512]{1,0:T(8,128)S(1)}, u32[]{:S(2)}, u32[]{:S(2)}) collective-permute-start(f32[256,512]{1,0:T(8,128)S(1)} %multiply_add_fusion.1), channel_id=1, source_target_pairs={{0,8},{8,0},{1,9},{9,1},{2,10},{10,2},{3,11},{11,3},{4,12},{12,4},... | collective-permute-start | bytes 1572872 | tf_op jit(solution)/shard_map/ppermute | solution.py:76
  161.7 10.4 %copy-start.16 = (f32[1,256]{1,0:T(1,128)S(1)}, f32[1,256]{1,0:T(1,128)}, u32[]{:S(2)}) copy-start(f32[1,256]{1,0:T(1,128)} %get-tuple-element.39) | copy-start | bytes 3076
  172.1 4.9 copy-start.17
  172.1 4.9 copy-start.18
  172.1 4.9 copy-start.19
  173.8 14.6 %collective-permute-start.8 = (f32[256,512]{1,0:T(8,128)S(1)}, f32[256,512]{1,0:T(8,128)S(1)}, u32[]{:S(2)}, u32[]{:S(2)}) collective-permute-start(f32[256,512]{1,0:T(8,128)S(1)} %multiply_add_fusion), channel_id=1, source_target_pairs={{0,4},{4,0},{1,5},{5,1},{2,6},{6,2},{3,7},{7,3},{8,12},{12,8},{9,1... | collective-permute-start | bytes 1572872 | tf_op jit(solution)/shard_map/ppermute | solution.py:76
  179.7 9.8 %copy-start.21 = (pred[256]{0:T(512)(128)(4,1)S(1)}, pred[256]{0:T(512)(128)(4,1)}, u32[]{:S(2)}) copy-start(pred[256]{0:T(512)(128)(4,1)} %compare_and_fusion) | copy-start | bytes 772
  189.5 1.8 copy-start.14
  189.5 1.8 copy-start.15
  191.8 2.1 copy-start.5
  349.4 4.0 copy-start.1
  354.6 1.0 copy-start.7
  384.2 0.7 copy-start.12
  414.0 0.7 copy-start.13
  464.1 58.4 %copy-start.4 = (f32[512,512]{0,1:T(8,128)S(1)}, f32[512,512]{0,1:T(8,128)}, u32[]{:S(2)}) copy-start(f32[512,512]{0,1:T(8,128)} %get-tuple-element.22) | copy-start | bytes 3145732
  519.0 3.0 copy-start.9
  531.4 0.7 copy-start.8
  534.4 4.5 copy-start.3
  534.4 4.5 copy-start.6
  537.2 4.6 copy-start.10
  537.2 4.6 copy-start.11
Sparse Core Ops, SparseCore 0:
  301.3 48.0 all-gather.1
where the time goes:
time: 557 us; the launch traced here: 550 us
  other arithmetic  143 us (26%)
  waiting for transfers between devices  130 us (23%)
  blocking collectives  104 us (19%)
  starting transfers between devices  74.7 us (13%)
  matrix products  43 us (8%)
  local copies, waits for them, and re-layouts  38.3 us (7%)
  between operations  17.8 us (3%)
    another operation x14, other arithmetic, chol_solve(): factor = jnp.linalg.cholesky(gram_mat)  93.4 us
    ppermute x5, waiting for transfers between devices, from_partner(): return lax.ppermute(block, axis, route)  81.4 us
    all_to_all x1, blocking collectives, from_everyone(): lax.all_to_all(jnp.broadcast_to(shard[None], (length, *shard.shape)), axi...  66.3 us
    ppermute x5, starting transfers between devices, from_partner(): return lax.ppermute(block, axis, route)  59.6 us
    all_gather x1, waiting for transfers between devices, gather_turned(): lax.all_gather(both, axis, axis=0, tiled=True)  48.2 us
    another operation x3, other arithmetic, chol_solve(): lax.linalg.triangular_solve(factor, middle, left_side=True, lower=True, t...  41.9 us
    all_to_all x1, blocking collectives, sent_and_summed(): lax.all_to_all(in_blocks(shard, dim, length), axis, 0, 0, tiled=True)  37.4 us
    dot_general x10, matrix products, matmul_hi(): return jnp.dot(left, right, precision=lax.Precision.HIGHEST)  15.4 us
  transfers between devices with their start and end apart: 10, of which 6 were waited for; matrix products, arithmetic and copies ran while one was open for 5% of the time, Pallas kernels for 0%

commit v1 on v0

--- a/solution.py
+++ b/solution.py
@@ -1,6 +1,10 @@
+import functools
+
 import jax
 import jax.numpy as jnp
 from jax import lax
+from jax.experimental import pallas as pl
+from jax.experimental.pallas import tpu as pltpu
 from jax.sharding import PartitionSpec as P
 
 ROW_LEVELS = 2
@@ -9,6 +13,8 @@
 
 WAVENUM = 6.0
 SOFTEN = 0.01
+PIVOT = 128
+SLAB = 8
 
 
 def in_blocks(shard, dim, length):
@@ -91,10 +97,123 @@
     return lax.dot_general(left, right, (((0,), (0,)), ((), ())), precision=lax.Precision.HIGHEST)
 
 
-def chol_solve(gram_mat, cross_mat):
-    factor = jnp.linalg.cholesky(gram_mat)
-    middle = lax.linalg.triangular_solve(factor, cross_mat, left_side=True, lower=True)
-    return lax.linalg.triangular_solve(factor, middle, left_side=True, lower=True, transpose_a=True)
+def dot_f32(left, right, left_dim, right_dim):
+    return lax.dot_general(
+        left,
+        right,
+        (((left_dim,), (right_dim,)), ((), ())),
+        precision=lax.Precision.HIGHEST,
+        preferred_element_type=jnp.float32,
+    )
+
+
+def three_parts(value):
+    high = value.astype(jnp.bfloat16).astype(jnp.float32)
+    middle = (value - high).astype(jnp.bfloat16).astype(jnp.float32)
+    return high, middle, (value - high) - middle
+
+
+def self_product(rows, first, count):
+    high, middle, low = three_parts(rows)
+    right = jnp.concatenate([high, middle, high, low, high, middle], axis=0)
+    left = jnp.concatenate([high, high, middle, high, low, middle], axis=0)[:, first:count]
+    return lax.dot_general(
+        left.astype(jnp.bfloat16),
+        right.astype(jnp.bfloat16),
+        (((0,), (0,)), ((), ())),
+        preferred_element_type=jnp.float32,
+    )
+
+
+def slab_factor_inverse(slab, at):
+    spread = (8, 128)
+    block, beside, found = {}, {}, {}
+    for i in range(SLAB):
+        beside[i, i] = jnp.ones(spread, jnp.float32)
+        for j in range(i, SLAB):
+            block[i, j] = jnp.broadcast_to(slab[i : i + 1, at + j : at + j + 1], spread)
+    for k in range(SLAB):
+        pivot = 1.0 / block[k, k]
+        for i in range(k + 1, SLAB):
+            ratio = block[k, i] * pivot
+            for j in range(i, SLAB):
+                block[i, j] = block[i, j] - ratio * block[k, j]
+            for j in range(k + 1):
+                term = ratio * beside[k, j] if j < k else ratio
+                beside[i, j] = beside[i, j] - term if (i, j) in beside else -term
+    for i in range(SLAB):
+        scale = lax.rsqrt(block[i, i])
+        for j in range(i + 1):
+            found[i, j] = beside[i, j] * scale if j < i else scale
+    return found
+
+
+def slab_rows(found, slab, count):
+    row_at = lax.broadcasted_iota(jnp.int32, (SLAB, count), 0)
+    left, right = 0.0, 0.0
+    for j in range(SLAB):
+        column = jnp.zeros((SLAB, count), jnp.float32)
+        for i in range(j, SLAB):
+            column = jnp.where(row_at == i, found[i, j], column)
+        left = left + column * jnp.broadcast_to(slab[j : j + 1, :count], (SLAB, count))
+        right = right + column * jnp.broadcast_to(slab[j : j + 1, count:], (SLAB, count))
+    return jnp.concatenate([left, right], axis=1)
+
+
+def factor_inverse(block):
+    count = block.shape[0]
+    row_at = lax.broadcasted_iota(jnp.int32, block.shape, 0)
+    col_at = lax.broadcasted_iota(jnp.int32, block.shape, 1)
+    rest = jnp.concatenate([block, jnp.where(row_at == col_at, 1.0, 0.0)], axis=1)
+    done = []
+    for at in range(0, count, SLAB):
+        slab = rest[:SLAB]
+        rows = slab_rows(slab_factor_inverse(slab, at), slab, count)
+        done.append(rows[:, count:])
+        if at + SLAB < count:
+            rest = rest[SLAB:] - self_product(rows, at + SLAB, count)
+    return jnp.concatenate(done, axis=0)
+
+
+def eliminate(points_total, gram_in, cross_in, image_in, own_in, total_in, new, norms, gram, cross, image):
+    gram[...] = gram_in[...]
+    cross[...] = cross_in[...]
+    image[...] = image_in[...]
+    new[...] = own_in[...]
+    left_over = total_in[...]
+    size = gram.shape[0]
+    for at in range(0, size, PIVOT):
+        end = at + PIVOT
+        inverse = factor_inverse(gram[at:end, at:end])
+        cross_rows = dot_f32(inverse, cross[at:end, :], 1, 0)
+        image_cols = dot_f32(image[:, at:end], inverse, 1, 1)
+        left_over = left_over - jnp.sum(cross_rows * cross_rows, axis=0, keepdims=True)
+        new[...] -= dot_f32(image_cols, cross_rows, 1, 0)
+        if end < size:
+            gram_rows = dot_f32(inverse, gram[at:end, end:], 1, 0)
+            image[:, end:] -= dot_f32(image_cols, gram_rows, 1, 0)
+            cross[end:, :] -= dot_f32(gram_rows, cross_rows, 0, 0)
+            for row in range(end, size, PIVOT):
+                part = gram_rows[:, row - end : row - end + PIVOT]
+                gram[row : row + PIVOT, row:] -= dot_f32(part, gram_rows[:, row - end :], 0, 0)
+    norms[...] = jnp.sqrt(left_over / points_total)
+
+
+def project_out(gram_mat, cross_mat, image, own, total, points_total):
+    return pl.pallas_call(
+        functools.partial(eliminate, points_total),
+        out_shape=(
+            jax.ShapeDtypeStruct(own.shape, jnp.float32),
+            jax.ShapeDtypeStruct(total.shape, jnp.float32),
+        ),
+        scratch_shapes=[
+            pltpu.VMEM(gram_mat.shape, jnp.float32),
+            pltpu.VMEM(cross_mat.shape, jnp.float32),
+            pltpu.VMEM(image.shape, jnp.float32),
+        ],
+        compiler_params=pltpu.CompilerParams(vmem_limit_bytes=40 * 2**20),
+        name="eliminate",
+    )(gram_mat, cross_mat, image, own, total)
 
 
 def global_sum(members):
@@ -139,11 +258,10 @@
     points_total = coords.shape[1] * lax.axis_size("row") * lax.axis_size("col")
     self_squares = jnp.sum(residual_in * residual_in, axis=0)[None, :]
     gram_mat, cross_mat, self_total = global_sum((gram_mat, cross_mat, self_squares))
-    alpha_mix = chol_solve(gram_mat, cross_mat)
-    new_residual = residual_in - matmul_hi(image, alpha_mix)
-    col_total = self_total[0] - jnp.sum(alpha_mix * cross_mat, axis=0)
-    res_norms = jnp.sqrt(col_total / points_total)
-    return (new_residual, res_norms)
+    new_residual, res_norms = project_out(
+        gram_mat, cross_mat, image, residual_in, self_total, points_total
+    )
+    return (new_residual, res_norms[0])
 
 
 def solution(mesh):

time: 557 us -> 395 us (0.71); the launches traced: 550 us -> 394 us
  other arithmetic: 143 us -> 4.57 us
  Pallas kernels: 0 us -> 34.2 us
  matrix products: 43 us -> 14.6 us
  local copies, waits for them, and re-layouts: 38.3 us -> 16.4 us
    another operation x17 -> x0, other arithmetic: 135 us -> none  [the longest x14 93.4 us: chol_solve(): factor = jnp.linalg.cholesky(gram_mat)]
    pallas_call x0 -> x1, Pallas kernels: none -> 34.2 us  [project_out(): pl.pallas_call(functools.partial(eliminate, points_total), out_shape=(jax...]
    another operation x20 -> x0, matrix products: 24 us -> none  [the longest x7 8.55 us: chol_solve(): lax.linalg.triangular_solve(factor, cross_mat, left_side=True, lower=True)]
    another operation x20 -> x0, local copies, waits for them, and re-layouts: 19.2 us -> none
    dot_general x10 -> x9, matrix products: 15.4 us -> 11 us  [matmul_hi(): return jnp.dot(left, right, precision=lax.Precision.HIGHEST)]
  transfers between devices with their start and end apart: 10 -> 10, of which waited for: 6 -> 6; matrix products, arithmetic and copies ran while one was open for 5% -> 6% of each run, Pallas kernels for 0% -> 0%
where the time goes in v1:
time: 395 us; the launch traced here: 394 us
  waiting for transfers between devices  125 us (32%)
  blocking collectives  107 us (27%)
  starting transfers between devices  77.5 us (20%)
  Pallas kernels  34.2 us (9%)
  local copies, waits for them, and re-layouts  16.4 us (4%)
  matrix products  14.6 us (4%)
  between operations  14.5 us (4%)
  other arithmetic  4.57 us (1%)
    ppermute x5, waiting for transfers between devices, from_partner(): return lax.ppermute(block, axis, route)  76.5 us
    all_to_all x1, blocking collectives, from_everyone(): lax.all_to_all(jnp.broadcast_to(shard[None], (length, *shard.shape)), axi...  68 us
    ppermute x5, starting transfers between devices, from_partner(): return lax.ppermute(block, axis, route)  61.2 us
    all_gather x1, waiting for transfers between devices, gather_turned(): lax.all_gather(both, axis, axis=0, tiled=True)  48.2 us
    all_to_all x1, blocking collectives, sent_and_summed(): lax.all_to_all(in_blocks(shard, dim, length), axis, 0, 0, tiled=True)  39.3 us
    pallas_call x1, Pallas kernels, project_out(): pl.pallas_call(functools.partial(eliminate, points_total), out_shape=(jax...  34.2 us
    ppermute x4, starting transfers between devices, from_behind(): return lax.ppermute(block, axis, route)  16.3 us
    dot_general x9, matrix products, matmul_hi(): return jnp.dot(left, right, precision=lax.Precision.HIGHEST)  11 us
  transfers between devices with their start and end apart: 10, of which 6 were waited for; matrix products, arithmetic and copies ran while one was open for 6% of the time, Pallas kernels for 0%

profile of v1, /device:TPU:1, one launch (start us, length us, event | category | flops | bytes accessed | tf_op | source)
XLA Modules:
  0.0 393.8 jit_solution(16672529515293305461)
XLA Ops:
  7.2 8.8 %collective-permute-start.2 = (f32[3,128]{1,0:T(4,128)}, f32[3,128]{1,0:T(4,128)S(1)}, u32[]{:S(2)}, u32[]{:S(2)}) collective-permute-start(f32[3,128]{1,0:T(4,128)} %param.10), channel_id=1, source_target_pairs={{1,0},{2,1},{3,2},{4,3},{5,4},{6,5},{7,6},{8,7},{9,8},{10,9},{11,1... | collective-permute-start | bytes 4616 | tf_op jit(solution)/shard_map/ppermute | solution.py:72
  16.0 1.9 collective-permute-start
  18.0 2.4 collective-permute-start.3
  20.4 3.2 collective-permute-start.1
  23.5 1.6 fusion.119
  25.2 12.5 %collective-permute-start.4 = (f32[256,512]{1,0:T(8,128)S(1)}, f32[256,512]{1,0:T(8,128)S(1)}, u32[]{:S(2)}, u32[]{:S(2)}) collective-permute-start(f32[256,512]{1,0:T(8,128)S(1)} %fusion.119), channel_id=1, source_target_pairs={{0,256},{256,0},{32,288},{288,32},{64,320},{320,64},{96,352},{352,... | collective-permute-start | bytes 1572872 | tf_op jit(solution)/shard_map/ppermute | solution.py:82
  37.7 1.0 multiply_reduce_fusion
  38.7 0.7 fusion.117
  39.5 0.7 convert_element_type.3
  40.1 0.7 fusion.118
  40.8 0.6 pad_clamp_fusion.1
  41.4 1.3 fusion.116
  42.8 1.8 collective-permute-done.4
  44.6 1.0 gather_fusion
  45.5 0.7 fusion
  46.3 42.7 %collective-permute-start.5 = (f32[256,512]{1,0:T(8,128)S(1)}, f32[256,512]{1,0:T(8,128)S(1)}, u32[]{:S(2)}, u32[]{:S(2)}) collective-permute-start(f32[256,512]{1,0:T(8,128)S(1)} %fusion), channel_id=1, source_target_pairs={{0,128},{128,0},{32,160},{160,32},{64,192},{192,64},{96,224},{224,... | collective-permute-start | bytes 1572872 | tf_op jit(solution)/shard_map/ppermute | solution.py:82
  89.0 44.1 %collective-permute-done.5 = f32[256,512]{1,0:T(8,128)S(1)} collective-permute-done((f32[256,512]{1,0:T(8,128)S(1)}, f32[256,512]{1,0:T(8,128)S(1)}, u32[]{:S(2)}, u32[]{:S(2)}) %collective-permute-start.5) | collective-permute-done | bytes 524320 | tf_op jit(solution)/shard_map/ppermute | solution.py:82
  133.1 1.0 gather_fusion.1
  134.1 0.7 multiply_add_fusion.2
  134.9 1.9 collective-permute-start.6
  136.9 1.4 fusion.63
  138.3 13.0 %collective-permute-done.6 = f32[256,512]{1,0:T(8,128)S(1)} collective-permute-done((f32[256,512]{1,0:T(8,128)S(1)}, f32[256,512]{1,0:T(8,128)S(1)}, u32[]{:S(2)}, u32[]{:S(2)}) %collective-permute-start.6) | collective-permute-done | bytes 524320 | tf_op jit(solution)/shard_map/ppermute | solution.py:82
  151.3 1.0 gather_fusion.2
  152.2 0.7 multiply_add_fusion.1
  153.0 1.9 collective-permute-start.7
  154.9 0.6 pad_clamp_fusion
  155.5 0.9 concatenate.22
  156.4 10.5 %collective-permute-done.7 = f32[256,512]{1,0:T(8,128)S(1)} collective-permute-done((f32[256,512]{1,0:T(8,128)S(1)}, f32[256,512]{1,0:T(8,128)S(1)}, u32[]{:S(2)}, u32[]{:S(2)}) %collective-permute-start.7) | collective-permute-done | bytes 524320 | tf_op jit(solution)/shard_map/ppermute | solution.py:82
  167.0 1.1 gather_fusion.3
  168.1 0.7 multiply_add_fusion
  168.8 2.1 collective-permute-start.8
  171.0 2.3 fusion.4
  173.3 3.1 fusion.5
  176.4 7.0 %collective-permute-done.8 = f32[256,512]{1,0:T(8,128)S(1)} collective-permute-done((f32[256,512]{1,0:T(8,128)S(1)}, f32[256,512]{1,0:T(8,128)S(1)}, u32[]{:S(2)}, u32[]{:S(2)}) %collective-permute-start.8) | collective-permute-done | bytes 524320 | tf_op jit(solution)/shard_map/ppermute | solution.py:82
  183.4 1.1 gather_fusion.4
  184.5 0.7 convolution_bitcast_fusion
  185.5 0.6 fusion.1.image_in
  186.1 1.0 fusion.121
  187.1 1.0 fusion.120
  188.3 39.3 %all_to_all.11 = f32[32,1025,16]{1,2,0:T(8,128)S(1)} all-to-all(f32[32,1025,16]{1,2,0:T(8,128)S(1)} %maximum_bitcast_fusion), channel_id=1, replica_groups=mesh['row'=16,'col'=32] {'col'}, dimensions={0} | all-to-all | bytes 4198400 | tf_op jit(solution)/shard_map/all_to_all | solution.py:28
  229.0 68.0 %all_to_all.12 = f32[16,1,16400]{2,1,0:T(1,128)S(1)} all-to-all(f32[16,1,16400]{2,1,0:T(1,128)S(1)} %broadcast_in_dim.16), channel_id=1, replica_groups=mesh['row'=16,'col'=32] {'row'}, dimensions={0} | all-to-all | bytes 2099200 | tf_op jit(solution)/shard_map/all_to_all | solution.py:41
  297.0 0.7 reduce_sum.29
  298.2 0.7 pad_maximum_fusion
  298.9 48.2 %all-gather.2.cloned.1.call-done = f32[512,1025]{1,0:T(8,128)} async-done(((f32[16,1025]{1,0:T(8,128)}), f32[512,1025]{1,0:T(8,128)}) %all-gather.2.cloned.1.call-update) | async-done | bytes 2099216 | tf_op jit(solution)/shard_map/all_gather | solution.py:61
  347.1 2.7 fusion.113
  350.1 1.6 copy.88
  351.7 1.1 slice_reduce_fusion
  352.8 34.2 %eliminate.1 = (f32[128,512]{1,0:T(8,128)}, f32[1,512]{1,0:T(1,128)}) custom-call(f32[512,512]{1,0:T(8,128)S(1)} %bitcast.75, f32[512,512]{1,0:T(8,128)S(1)} %bitcast.74, f32[128,512]{1,0:T(8,128)S(1)} %fusion.1.image_in, f32[128,512]{1,0:T(8,128)S(1)} %copy-done.1, f32[1,512]{1,0:T(1,128)S(1)} %bitcast.76), custom_call_target="tpu_custom_call" | custom-call | tf_op jit(solution)/shard_map/eliminate/pallas_call | solution.py:203
  (60 shorter events, 2.8 us)
Async XLA Ops:
  7.2 16.4 %copy-start = (f32[128,256]{1,0:T(8,128)S(1)}, f32[128,256]{1,0:T(8,128)}, u32[]{:S(2)}) copy-start(f32[128,256]{1,0:T(8,128)} %param.13) | copy-start | bytes 393220
  7.2 339.9 %all-gather.2.cloned.1.call-start = ((), (), s32[]{:S(2)}) async-start(), calls=%async_computation.2 | async-start | bytes 2433024 | tf_op jit(solution)/shard_map/all_gather | solution.py:61
  7.2 149.2 %collective-permute-start.2 = (f32[3,128]{1,0:T(4,128)}, f32[3,128]{1,0:T(4,128)S(1)}, u32[]{:S(2)}, u32[]{:S(2)}) collective-permute-start(f32[3,128]{1,0:T(4,128)} %param.10), channel_id=1, source_target_pairs={{1,0},{2,1},{3,2},{4,3},{5,4},{6,5},{7,6},{8,7},{9,8},{10,9},{11,1... | collective-permute-start | bytes 4616 | tf_op jit(solution)/shard_map/ppermute | solution.py:72
  16.0 154.9 %collective-permute-start = (f32[3,128]{1,0:T(4,128)}, f32[3,128]{1,0:T(4,128)S(1)}, u32[]{:S(2)}, u32[]{:S(2)}) collective-permute-start(f32[3,128]{1,0:T(4,128)} %param.10), channel_id=1, source_target_pairs={{0,1},{1,2},{2,3},{3,4},{4,5},{5,6},{6,7},{7,8},{8,9},{9,10},{10,1... | collective-permute-start | bytes 4616 | tf_op jit(solution)/shard_map/ppermute | solution.py:72
  18.0 155.3 %collective-permute-start.3 = (f32[128,512]{1,0:T(8,128)}, f32[128,512]{1,0:T(8,128)}, u32[]{:S(2)}, u32[]{:S(2)}) collective-permute-start(f32[128,512]{1,0:T(8,128)} %own_in.1), channel_id=1, source_target_pairs={{1,0},{2,1},{3,2},{4,3},{5,4},{6,5},{7,6},{8,7},{9,8},{10,9},{11,1... | collective-permute-start | bytes 786440 | tf_op jit(solution)/shard_map/ppermute | solution.py:72
  20.4 150.6 %collective-permute-start.1 = (f32[128,512]{1,0:T(8,128)}, f32[128,512]{1,0:T(8,128)}, u32[]{:S(2)}, u32[]{:S(2)}) collective-permute-start(f32[128,512]{1,0:T(8,128)} %own_in.1), channel_id=1, source_target_pairs={{0,1},{1,2},{2,3},{3,4},{4,5},{5,6},{6,7},{7,8},{8,9},{9,10},{10,1... | collective-permute-start | bytes 786440 | tf_op jit(solution)/shard_map/ppermute | solution.py:72
  25.2 19.4 %collective-permute-start.4 = (f32[256,512]{1,0:T(8,128)S(1)}, f32[256,512]{1,0:T(8,128)S(1)}, u32[]{:S(2)}, u32[]{:S(2)}) collective-permute-start(f32[256,512]{1,0:T(8,128)S(1)} %fusion.119), channel_id=1, source_target_pairs={{0,256},{256,0},{32,288},{288,32},{64,320},{320,64},{96,352},{352,... | collective-permute-start | bytes 1572872 | tf_op jit(solution)/shard_map/ppermute | solution.py:82
  42.8 2.8 copy-start.2
  46.3 86.8 %collective-permute-start.5 = (f32[256,512]{1,0:T(8,128)S(1)}, f32[256,512]{1,0:T(8,128)S(1)}, u32[]{:S(2)}, u32[]{:S(2)}) collective-permute-start(f32[256,512]{1,0:T(8,128)S(1)} %fusion), channel_id=1, source_target_pairs={{0,128},{128,0},{32,160},{160,32},{64,192},{192,64},{96,224},{224,... | collective-permute-start | bytes 1572872 | tf_op jit(solution)/shard_map/ppermute | solution.py:82
  134.1 2.7 copy-start.9
  134.1 2.7 copy-start.1
  134.9 16.4 %collective-permute-start.6 = (f32[256,512]{1,0:T(8,128)S(1)}, f32[256,512]{1,0:T(8,128)S(1)}, u32[]{:S(2)}, u32[]{:S(2)}) collective-permute-start(f32[256,512]{1,0:T(8,128)S(1)} %multiply_add_fusion.2), channel_id=1, source_target_pairs={{0,16},{16,0},{1,17},{17,1},{2,18},{18,2},{3,19},{19,3},{4,20},{20... | collective-permute-start | bytes 1572872 | tf_op jit(solution)/shard_map/ppermute | solution.py:82
  153.0 14.0 %collective-permute-start.7 = (f32[256,512]{1,0:T(8,128)S(1)}, f32[256,512]{1,0:T(8,128)S(1)}, u32[]{:S(2)}, u32[]{:S(2)}) collective-permute-start(f32[256,512]{1,0:T(8,128)S(1)} %multiply_add_fusion.1), channel_id=1, source_target_pairs={{0,8},{8,0},{1,9},{9,1},{2,10},{10,2},{3,11},{11,3},{4,12},{12,4},... | collective-permute-start | bytes 1572872 | tf_op jit(solution)/shard_map/ppermute | solution.py:82
  156.4 11.6 %copy-start.8 = (f32[1,256]{1,0:T(1,128)S(1)}, f32[1,256]{1,0:T(1,128)}, u32[]{:S(2)}) copy-start(f32[1,256]{1,0:T(1,128)} %get-tuple-element.15) | copy-start | bytes 3076
  168.1 2.9 copy-start.4
  168.8 14.6 %collective-permute-start.8 = (f32[256,512]{1,0:T(8,128)S(1)}, f32[256,512]{1,0:T(8,128)S(1)}, u32[]{:S(2)}, u32[]{:S(2)}) collective-permute-start(f32[256,512]{1,0:T(8,128)S(1)} %multiply_add_fusion), channel_id=1, source_target_pairs={{0,4},{4,0},{1,5},{5,1},{2,6},{6,2},{3,7},{7,3},{8,12},{12,8},{9,1... | collective-permute-start | bytes 1572872 | tf_op jit(solution)/shard_map/ppermute | solution.py:82
  184.5 1.0 copy-start.5
  184.5 1.0 copy-start.6
  184.5 1.0 copy-start.7
  186.0 2.1 copy-start.3
Sparse Core Ops, SparseCore 0:
  299.0 48.0 all-gather.1

commit v2 on v1

v2 whole, which is shorter than its diff:
```python
import functools

import jax
import jax.numpy as jnp
from jax import lax
from jax.experimental import pallas as pl
from jax.experimental.pallas import tpu as pltpu
from jax.sharding import PartitionSpec as P

LEVELS = 5
CHUNKS = 2


WAVENUM = 6.0
SOFTEN = 0.01
PIVOT = 128
SLAB = 8


def swapped(block, axis, bits):
    return lax.ppermute(block, axis, [(i, i ^ bits) for i in range(lax.axis_size(axis))])


def from_behind(block, axis, distance):
    devices = range(lax.axis_size(axis))
    route = [(i - distance, i) for i in devices if i - distance in devices]
    return lax.ppermute(block, axis, route)


def kernel_tile(own_xyz, other_xyz):
    dist_sq = (own_xyz[0][:, None] - other_xyz[0][None, :]) ** 2
    dist_sq = dist_sq + (own_xyz[1][:, None] - other_xyz[1][None, :]) ** 2
    dist_sq = dist_sq + (own_xyz[2][:, None] - other_xyz[2][None, :]) ** 2
    return jnp.cos(WAVENUM * jnp.sqrt(dist_sq)) / jnp.sqrt(dist_sq + SOFTEN)


def matmul_hi(left, right, left_dim=1, right_dim=0):
    dims = (((left_dim,), (right_dim,)), ((), ()))
    return lax.dot_general(left, right, dims, precision=lax.Precision.HIGHEST)


def dot_f32(left, right, left_dim, right_dim):
    return lax.dot_general(
        left,
        right,
        (((left_dim,), (right_dim,)), ((), ())),
        precision=lax.Precision.HIGHEST,
        preferred_element_type=jnp.float32,
    )


def three_parts(value):
    high = value.astype(jnp.bfloat16).astype(jnp.float32)
    middle = (value - high).astype(jnp.bfloat16).astype(jnp.float32)
    return high, middle, (value - high) - middle


def self_product(rows, first, count):
    high, middle, low = three_parts(rows)
    right = jnp.concatenate([high, middle, high, low, high, middle], axis=0)
    left = jnp.concatenate([high, high, middle, high, low, middle], axis=0)[:, first:count]
    return lax.dot_general(
        left.astype(jnp.bfloat16),
        right.astype(jnp.bfloat16),
        (((0,), (0,)), ((), ())),
        preferred_element_type=jnp.float32,
    )


def slab_factor_inverse(slab, at):
    spread = (8, 128)
    block, beside, found = {}, {}, {}
    for i in range(SLAB):
        beside[i, i] = jnp.ones(spread, jnp.float32)
        for j in range(i, SLAB):
            block[i, j] = jnp.broadcast_to(slab[i : i + 1, at + j : at + j + 1], spread)
    for k in range(SLAB):
        pivot = 1.0 / block[k, k]
        for i in range(k + 1, SLAB):
            ratio = block[k, i] * pivot
            for j in range(i, SLAB):
                block[i, j] = block[i, j] - ratio * block[k, j]
            for j in range(k + 1):
                term = ratio * beside[k, j] if j < k else ratio
                beside[i, j] = beside[i, j] - term if (i, j) in beside else -term
    for i in range(SLAB):
        scale = lax.rsqrt(block[i, i])
        for j in range(i + 1):
            found[i, j] = beside[i, j] * scale if j < i else scale
    return found


def slab_rows(found, slab, count):
    row_at = lax.broadcasted_iota(jnp.int32, (SLAB, count), 0)
    left, right = 0.0, 0.0
    for j in range(SLAB):
        column = jnp.zeros((SLAB, count), jnp.float32)
        for i in range(j, SLAB):
            column = jnp.where(row_at == i, found[i, j], column)
        left = left + column * jnp.broadcast_to(slab[j : j + 1, :count], (SLAB, count))
        right = right + column * jnp.broadcast_to(slab[j : j + 1, count:], (SLAB, count))
    return jnp.concatenate([left, right], axis=1)


def factor_inverse(block):
    count = block.shape[0]
    row_at = lax.broadcasted_iota(jnp.int32, block.shape, 0)
    col_at = lax.broadcasted_iota(jnp.int32, block.shape, 1)
    rest = jnp.concatenate([block, jnp.where(row_at == col_at, 1.0, 0.0)], axis=1)
    done = []
    for at in range(0, count, SLAB):
        slab = rest[:SLAB]
        rows = slab_rows(slab_factor_inverse(slab, at), slab, count)
        done.append(rows[:, count:])
        if at + SLAB < count:
            rest = rest[SLAB:] - self_product(rows, at + SLAB, count)
    return jnp.concatenate(done, axis=0)


def eliminate(
    points_total, core, mine, theirs, image_in, own_in, new, norms, gram, cross, image, total
):
    size = gram.shape[0]
    image[...] = image_in[...]
    new[...] = own_in[...]

    def unpack(first, second):
        gram[0:128, 0:512] = first[:, 0:512]
        gram[384:512, 384:512] = first[:, 512:640]
        gram[128:256, 128:512] = second[:, 0:384]
        gram[256:384, 256:512] = second[:, 384:640]
        cross[0:128, :] = first[:, 640:1152]
        cross[128:256, :] = first[:, 1152:1664]
        cross[256:384, :] = second[:, 640:1152]
        cross[384:512, :] = second[:, 1152:1664]
        for piece in range(4):
            total[:, piece * 128 : piece * 128 + 128] = first[piece : piece + 1, 1664:1792]

    @pl.when(core[0] == 0)
    def _():
        unpack(mine, theirs)

    @pl.when(core[0] == 1)
    def _():
        unpack(theirs, mine)

    left_over = total[...]
    for at in range(0, size, PIVOT):
        end = at + PIVOT
        inverse = factor_inverse(gram[at:end, at:end])
        cross_rows = dot_f32(inverse, cross[at:end, :], 1, 0)
        image_cols = dot_f32(image[:, at:end], inverse, 1, 1)
        left_over = left_over - jnp.sum(cross_rows * cross_rows, axis=0, keepdims=True)
        new[...] -= dot_f32(image_cols, cross_rows, 1, 0)
        if end < size:
            gram_rows = dot_f32(inverse, gram[at:end, end:], 1, 0)
            image[:, end:] -= dot_f32(image_cols, gram_rows, 1, 0)
            cross[end:, :] -= dot_f32(gram_rows, cross_rows, 0, 0)
            for row in range(end, size, PIVOT):
                part = gram_rows[:, row - end : row - end + PIVOT]
                gram[row : row + PIVOT, row:] -= dot_f32(part, gram_rows[:, row - end :], 0, 0)
    norms[...] = jnp.sqrt(left_over / points_total)


def project_out(core, mine, theirs, image, own, points_total):
    size = own.shape[1]
    whole = pl.BlockSpec(memory_space=pltpu.VMEM)
    return pl.pallas_call(
        functools.partial(eliminate, points_total),
        in_specs=[pl.BlockSpec(memory_space=pltpu.SMEM), whole, whole, whole, whole],
        out_specs=(whole, whole),
        out_shape=(
            jax.ShapeDtypeStruct(own.shape, jnp.float32),
            jax.ShapeDtypeStruct((1, size), jnp.float32),
        ),
        scratch_shapes=[
            pltpu.VMEM((size, size), jnp.float32),
            pltpu.VMEM((size, size), jnp.float32),
            pltpu.VMEM(image.shape, jnp.float32),
            pltpu.VMEM((1, size), jnp.float32),
        ],
        compiler_params=pltpu.CompilerParams(vmem_limit_bytes=40 * 2**20),
        name="eliminate",
    )(core[None], mine, theirs, image, own)


def plane_groups():
    return [[2 * chip + core for chip in range(lax.axis_size("col") // 2)] for core in range(2)]


def within_plane(tiles):
    return lax.all_to_all(tiles, "col", 0, 0, axis_index_groups=plane_groups(), tiled=True)


def quad_sum(share, unit):
    one, two, three = (swapped(share, "row", unit * k) for k in (1, 2, 3))
    return (share + one) + (two + three)


def global_sum(half):
    chips = lax.axis_size("col") // 2
    rows = half.shape[0] // chips
    share = jnp.sum(within_plane(half.reshape(chips, rows, -1)), axis=0)
    share = quad_sum(quad_sum(share, 1), 4)
    return within_plane(jnp.broadcast_to(share[None], (chips, *share.shape))).reshape(half.shape)


def half_of_sums(core, image, own, pair_image, pair_own, own_squares):
    odd = core == 1
    images = jnp.concatenate([image, pair_image], axis=0)
    owns = jnp.concatenate([own, pair_own], axis=0)
    blocks = [images[:, k * 128 : k * 128 + 128] for k in range(4)]
    wide = matmul_hi(jnp.where(odd, blocks[1], blocks[0]), images, 0, 0)
    narrow = matmul_hi(jnp.where(odd, blocks[2], blocks[3]), images[:, 256:], 0, 0)
    gram_part = jnp.where(
        odd,
        jnp.concatenate([wide[:, 128:], narrow], axis=1),
        jnp.concatenate([wide, narrow[:, 128:]], axis=1),
    )
    cross_part = matmul_hi(jnp.where(odd, images[:, 256:], images[:, :256]), owns, 0, 0)
    squares = jnp.pad(own_squares.reshape(4, 128), ((0, 124), (0, 0)))
    return jnp.concatenate([gram_part, cross_part[:128], cross_part[128:], squares], axis=1)


def shards(
    coords, residual_in, link_mask, compress, expand, level_gain, level_couple, partner_perm
):
    rank = compress.shape[1]
    chunks = jnp.split(residual_in, CHUNKS, axis=1)
    core = lax.axis_index("col") & 1

    by_three = [swapped(chunk, "row", 12) for chunk in chunks]
    compress_two = swapped(compress, "row", 8)
    by_two = [swapped(chunk, "row", 4) for chunk in by_three]
    by_one = [swapped(chunk, "row", 12) for chunk in by_two]

    below_xyz, below_rhs = from_behind((coords, residual_in), ("row", "col"), 1)
    above_xyz, above_rhs = from_behind((coords, residual_in), ("row", "col"), -1)

    gains = [level_gain[0, k * rank : (k + 1) * rank][:, None] for k in range(LEVELS)]
    numbers = jnp.arange(rank, dtype=jnp.int32)[None, :]

    def couple_of(level_at):
        couple = level_couple[:, level_at * rank : (level_at + 1) * rank]
        place = (partner_perm[0, level_at][:, None] == numbers).astype(jnp.float32)
        return matmul_hi(couple, place)

    couples = [couple_of(k) for k in range(LEVELS)]
    last_partner = swapped(matmul_hi(expand, couples[4]), "col", 4)
    last_own = expand * level_gain[:, 4 * rank :]

    low_map = jnp.concatenate(
        [gains[0] * compress.T, matmul_hi(couples[0], compress_two, 1, 1)], axis=1
    )
    low_map_one = matmul_hi(couples[1], swapped(low_map, "row", 4))
    low_map_own = gains[1] * low_map

    near_scale = (3.0 * coords.shape[1]) ** (-0.5)
    weights = link_mask.astype(jnp.float32)
    near_field = matmul_hi(kernel_tile(coords, coords), residual_in)
    near_field = near_field + weights[0, 0] * matmul_hi(kernel_tile(coords, below_xyz), below_rhs)
    near_field = near_field + weights[0, 1] * matmul_hi(kernel_tile(coords, above_xyz), above_rhs)
    base = 2.0 * residual_in + near_scale * near_field
    own_squares = jnp.sum(residual_in * residual_in, axis=0)
    pair_own = jnp.where(core == 1, below_rhs, above_rhs)
    pair_squares = jnp.sum(pair_own * pair_own, axis=0)

    far_parts = []
    for own, one, two, three in zip(chunks, by_one, by_two, by_three):
        coeffs = matmul_hi(low_map_own, jnp.concatenate([own, two], axis=0))
        coeffs = coeffs + matmul_hi(low_map_one, jnp.concatenate([one, three], axis=0))
        coeffs = gains[2] * coeffs + matmul_hi(couples[2], swapped(coeffs, "col", 16))
        coeffs = gains[3] * coeffs + matmul_hi(couples[3], swapped(coeffs, "col", 8))
        sent = swapped(matmul_hi(last_partner, coeffs), "col", 4)
        far_parts.append(matmul_hi(last_own, coeffs) + sent)
    image = base + jnp.concatenate(far_parts, axis=1)

    half = half_of_sums(
        core, image, residual_in, swapped(image, "col", 1), pair_own, own_squares + pair_squares
    )
    mine = global_sum(half)
    theirs = swapped(mine, "col", 1)
    points_total = coords.shape[1] * lax.axis_size("row") * lax.axis_size("col")
    new_residual, res_norms = project_out(core, mine, theirs, image, residual_in, points_total)
    return (new_residual, res_norms[0])


def solution(mesh):
    return jax.shard_map(
        shards,
        mesh=mesh,
        in_specs=(
            P(None, ("row", "col")),
            P(("row", "col"), None),
            P(("row", "col"), None),
            P(("row", "col"), None),
            P(("row", "col"), None),
            P(("row", "col"), None),
            P(("row", "col"), None),
            P(("row", "col"), None, None),
        ),
        out_specs=(P(("row", "col"), None), P()),
        check_vma=False,
    )
```

time: 395 us -> 300 us (0.76)
  blocking collectives: 107 us -> 37.1 us
  starting transfers between devices: 77.5 us -> 133 us
  waiting for transfers between devices: 125 us -> 70.8 us
  between operations: 14.5 us -> 1.32 us
  local copies, waits for them, and re-layouts: 16.4 us -> 4.02 us
    all_to_all x2, blocking collectives: 107 us -> 37.1 us  [within_plane(): lax.all_to_all(tiles, 'col', 0, 0, axis_index_groups=plane_groups(), tile...]
    ppermute x5 -> x23, starting transfers between devices: 61.2 us -> 116 us  [swapped(): lax.ppermute(block, axis, [(i, i ^ bits) for i in range(lax.axis_size(axi...]
    all_gather x1 -> x0, waiting for transfers between devices: 48.2 us -> none  [gather_turned(): lax.all_gather(both, axis, axis=0, tiled=True)]
    ppermute x5 -> x23, waiting for transfers between devices: 76.5 us -> 70.8 us  [swapped(): lax.ppermute(block, axis, [(i, i ^ bits) for i in range(lax.axis_size(axi...]
    gather x5 -> x0, local copies, waits for them, and re-layouts: 5.13 us -> none  [mix_level(): picked = jnp.take(partner, taken_rows, axis=0)]
    slice x5, local copies, waits for them, and re-layouts: 5.87 us -> 1.55 us  [the longest x1 0.75 us: couple_of(): place = (partner_perm[0, level_at][:, None] == numbers).astype(jnp.float32)]
    dot_general x12 -> x26, matrix products: 14.6 us -> 15.2 us  [matmul_hi(): return lax.dot_general(left, right, dims, precision=lax.Precision.HIGHEST)]
  transfers between devices with their start and end apart: 10 -> 27, of which waited for: 6 -> 13; matrix products, arithmetic and copies ran while one was open for 6% -> 6% of each run, Pallas kernels for 0% -> 0%
where the time goes in v2:
time: 300 us; the launch traced here: 297 us
  starting transfers between devices  133 us (44%)
  waiting for transfers between devices  70.8 us (24%)
  blocking collectives  37.1 us (12%)
  Pallas kernels  34.3 us (11%)
  matrix products  15.2 us (5%)
  local copies, waits for them, and re-layouts  4.02 us (1%)
    ppermute x23, starting transfers between devices, swapped(): lax.ppermute(block, axis, [(i, i ^ bits) for i in range(lax.axis_size(axi...  116 us
    ppermute x23, waiting for transfers between devices, swapped(): lax.ppermute(block, axis, [(i, i ^ bits) for i in range(lax.axis_size(axi...  70.8 us
    all_to_all x2, blocking collectives, within_plane(): lax.all_to_all(tiles, 'col', 0, 0, axis_index_groups=plane_groups(), tile...  37.1 us
    pallas_call x1, Pallas kernels, project_out(): pl.pallas_call(functools.partial(eliminate, points_total), in_specs=[pl.B...  34.3 us
    ppermute x4, starting transfers between devices, from_behind(): return lax.ppermute(block, axis, route)  17.1 us
    dot_general x26, matrix products, matmul_hi(): return lax.dot_general(left, right, dims, precision=lax.Precision.HIGHEST)  15.2 us
  transfers between devices with their start and end apart: 27, of which 13 were waited for; matrix products, arithmetic and copies ran while one was open for 6% of the time, Pallas kernels for 0%

profile of v2, /device:TPU:1, one launch (start us, length us, event | category | flops | bytes accessed | tf_op | source)
XLA Modules:
  0.0 297.5 jit_solution(13304148628272139505)
XLA Ops:
  0.6 4.7 %collective-permute-start = (f32[3,128]{1,0:T(4,128)}, f32[3,128]{1,0:T(4,128)S(1)}, u32[]{:S(2)}, u32[]{:S(2)}) collective-permute-start(f32[3,128]{1,0:T(4,128)} %param.8), channel_id=1, source_target_pairs={{0,1},{1,2},{2,3},{3,4},{4,5},{5,6},{6,7},{7,8},{8,9},{9,10},{10,1... | collective-permute-start | bytes 4616 | tf_op jit(solution)/shard_map/ppermute | solution.py:27
  5.4 5.5 %collective-permute-start.2 = (f32[3,128]{1,0:T(4,128)}, f32[3,128]{1,0:T(4,128)S(1)}, u32[]{:S(2)}, u32[]{:S(2)}) collective-permute-start(f32[3,128]{1,0:T(4,128)} %param.8), channel_id=1, source_target_pairs={{1,0},{2,1},{3,2},{4,3},{5,4},{6,5},{7,6},{8,7},{9,8},{10,9},{11,1... | collective-permute-start | bytes 4616 | tf_op jit(solution)/shard_map/ppermute | solution.py:27
  10.9 11.9 %collective-permute-start.4 = (f32[128,256]{1,0:T(8,128)}, f32[128,256]{1,0:T(8,128)S(1)}, u32[]{:S(2)}, u32[]{:S(2)}) collective-permute-start(f32[128,256]{1,0:T(8,128)} %param.11), channel_id=1, source_target_pairs={{0,256},{32,288},{64,320},{96,352},{128,384},{160,416},{192,448},{... | collective-permute-start | bytes 393224 | tf_op jit(solution)/shard_map/ppermute | solution.py:21
  22.8 3.9 %collective-permute-start.1 = (f32[128,512]{1,0:T(8,128)}, f32[128,512]{1,0:T(8,128)S(1)}, u32[]{:S(2)}, u32[]{:S(2)}) collective-permute-start(f32[128,512]{1,0:T(8,128)} %own_in.1), channel_id=1, source_target_pairs={{0,1},{1,2},{2,3},{3,4},{4,5},{5,6},{6,7},{7,8},{8,9},{9,10},{10,1... | collective-permute-start | bytes 786440 | tf_op jit(solution)/shard_map/ppermute | solution.py:27
  26.7 1.0 fusion.163
  27.7 1.9 collective-permute-start.13
  29.6 0.8 slice_bitcast_fusion.8
  30.4 0.7 fusion.164
  31.9 0.9 multiply_bitcast_fusion
  32.8 1.4 fusion.37
  37.6 7.3 %collective-permute-start.5 = (f32[128,256]{1,0:T(8,128)S(1)}, f32[128,256]{1,0:T(8,128)S(1)}, u32[]{:S(2)}, u32[]{:S(2)}) collective-permute-start(f32[128,256]{1,0:T(8,128)S(1)} %get-tuple-element.10), channel_id=1, source_target_pairs={{0,384},{32,416},{64,448},{96,480},{128,256},{160,288},{192,320},{... | collective-permute-start | bytes 393224 | tf_op jit(solution)/shard_map/ppermute | solution.py:21
  44.9 1.2 collective-permute-done.13
  46.2 15.2 %collective-permute-start.14 = (f32[128,256]{1,0:T(8,128)S(1)}, f32[128,256]{1,0:T(8,128)S(1)}, u32[]{:S(2)}, u32[]{:S(2)}) collective-permute-start(f32[128,256]{1,0:T(8,128)S(1)} %collective-permute-done.13), channel_id=1, source_target_pairs={{0,128},{32,160},{64,192},{96,224},{128,0},{160,32},{192,64},{224,... | collective-permute-start | bytes 393224 | tf_op jit(solution)/shard_map/ppermute | solution.py:21
  61.7 2.5 collective-permute-start.7
  64.1 29.2 %collective-permute-done.14 = f32[128,256]{1,0:T(8,128)S(1)} collective-permute-done((f32[128,256]{1,0:T(8,128)S(1)}, f32[128,256]{1,0:T(8,128)S(1)}, u32[]{:S(2)}, u32[]{:S(2)}) %collective-permute-start.14) | collective-permute-done | bytes 131104 | tf_op jit(solution)/shard_map/ppermute | solution.py:21
  93.3 1.9 collective-permute-start.6
  95.8 8.6 %collective-permute-done.6 = f32[128,256]{1,0:T(8,128)S(1)} collective-permute-done((f32[128,256]{1,0:T(8,128)S(1)}, f32[128,256]{1,0:T(8,128)S(1)}, u32[]{:S(2)}, u32[]{:S(2)}) %collective-permute-start.6) | collective-permute-done | bytes 131104 | tf_op jit(solution)/shard_map/ppermute | solution.py:21
  104.4 2.9 collective-permute-start.3
  107.9 1.9 collective-permute-start.15
  110.5 8.5 %collective-permute-done.15 = f32[128,256]{1,0:T(8,128)S(1)} collective-permute-done((f32[128,256]{1,0:T(8,128)S(1)}, f32[128,256]{1,0:T(8,128)S(1)}, u32[]{:S(2)}, u32[]{:S(2)}) %collective-permute-start.15) | collective-permute-done | bytes 131104 | tf_op jit(solution)/shard_map/ppermute | solution.py:21
  118.9 1.9 collective-permute-start.8
  121.2 7.3 %collective-permute-done.8 = f32[128,256]{1,0:T(8,128)S(1)} collective-permute-done((f32[128,256]{1,0:T(8,128)S(1)}, f32[128,256]{1,0:T(8,128)S(1)}, u32[]{:S(2)}, u32[]{:S(2)}) %collective-permute-start.8) | collective-permute-done | bytes 131104 | tf_op jit(solution)/shard_map/ppermute | solution.py:21
  128.5 3.0 %collective-permute-start.16 = (f32[256,256]{1,0:T(8,128)S(1)}, f32[256,256]{1,0:T(8,128)S(1)}, u32[]{:S(2)}, u32[]{:S(2)}) collective-permute-start(f32[256,256]{1,0:T(8,128)S(1)} %convolution_add_fusion), channel_id=1, source_target_pairs={{0,16},{1,17},{2,18},{3,19},{4,20},{5,21},{6,22},{7,23},{8,24},{9,... | collective-permute-start | bytes 786440 | tf_op jit(solution)/shard_map/ppermute | solution.py:21
  132.0 3.7 %collective-permute-start.9 = (f32[256,256]{1,0:T(8,128)S(1)}, f32[256,256]{1,0:T(8,128)S(1)}, u32[]{:S(2)}, u32[]{:S(2)}) collective-permute-start(f32[256,256]{1,0:T(8,128)S(1)} %convolution_add_fusion.1), channel_id=1, source_target_pairs={{0,16},{1,17},{2,18},{3,19},{4,20},{5,21},{6,22},{7,23},{8,24},{9,... | collective-permute-start | bytes 786440 | tf_op jit(solution)/shard_map/ppermute | solution.py:21
  135.8 1.4 collective-permute-done.16
  137.2 9.1 %collective-permute-start.11 = (f32[128,256]{0,1:T(8,128)S(1)}, f32[128,256]{0,1:T(8,128)S(1)}, u32[]{:S(2)}, u32[]{:S(2)}) collective-permute-start(f32[128,256]{0,1:T(8,128)S(1)} %convolution_bitcast_fusion), channel_id=1, source_target_pairs={{0,4},{1,5},{2,6},{3,7},{4,0},{5,1},{6,2},{7,3},{8,12},{9,13},{10,... | collective-permute-start | bytes 393224 | tf_op jit(solution)/shard_map/ppermute | solution.py:21
  147.5 1.9 collective-permute-start.10
  149.4 1.4 fusion.2
  150.8 3.4 %collective-permute-start.17 = (f32[256,256]{1,0:T(8,128)S(1)}, f32[256,256]{1,0:T(8,128)S(1)}, u32[]{:S(2)}, u32[]{:S(2)}) collective-permute-start(f32[256,256]{1,0:T(8,128)S(1)} %get-tuple-element.32), channel_id=1, source_target_pairs={{0,8},{1,9},{2,10},{3,11},{4,12},{5,13},{6,14},{7,15},{8,0},{9,1},... | collective-permute-start | bytes 786440 | tf_op jit(solution)/shard_map/ppermute | solution.py:21
  155.7 5.5 %collective-permute-start.12 = (f32[128,256]{1,0:T(8,128)S(1)}, f32[128,256]{1,0:T(8,128)S(1)}, u32[]{:S(2)}, u32[]{:S(2)}) collective-permute-start(f32[128,256]{1,0:T(8,128)S(1)} %fusion.121), channel_id=1, source_target_pairs={{0,4},{1,5},{2,6},{3,7},{4,0},{5,1},{6,2},{7,3},{8,12},{9,13},{10,... | collective-permute-start | bytes 393224 | tf_op jit(solution)/shard_map/ppermute | solution.py:21
  162.6 4.4 %collective-permute-start.18 = (f32[128,256]{1,0:T(8,128)S(1)}, f32[128,256]{1,0:T(8,128)S(1)}, u32[]{:S(2)}, u32[]{:S(2)}) collective-permute-start(f32[128,256]{1,0:T(8,128)S(1)} %fusion.122), channel_id=1, source_target_pairs={{0,4},{1,5},{2,6},{3,7},{4,0},{5,1},{6,2},{7,3},{8,12},{9,13},{10,... | collective-permute-start | bytes 393224 | tf_op jit(solution)/shard_map/ppermute | solution.py:21
  167.4 3.5 %collective-permute-done.18 = f32[128,256]{1,0:T(8,128)S(1)} collective-permute-done((f32[128,256]{1,0:T(8,128)S(1)}, f32[128,256]{1,0:T(8,128)S(1)}, u32[]{:S(2)}, u32[]{:S(2)}) %collective-permute-start.18) | collective-permute-done | bytes 131104 | tf_op jit(solution)/shard_map/ppermute | solution.py:21
  170.9 1.4 fusion.4.image_in
  172.3 7.3 %collective-permute-start.19 = (f32[128,512]{1,0:T(8,128)S(1)}, f32[128,512]{1,0:T(8,128)S(1)}, u32[]{:S(2)}, u32[]{:S(2)}) collective-permute-start(f32[128,512]{1,0:T(8,128)S(1)} %fusion.4.image_in), channel_id=1, source_target_pairs={{0,1},{1,0},{2,3},{3,2},{4,5},{5,4},{6,7},{7,6},{8,9},{9,8},{10,11... | collective-permute-start | bytes 786440 | tf_op jit(solution)/shard_map/ppermute | solution.py:21
  179.7 1.1 collective-permute-done.19
  182.5 18.8 %all_to_all.10 = f32[16,8,1792]{2,1,0:T(8,128)S(1)} all-to-all(f32[16,8,1792]{2,1,0:T(8,128)S(1)} %fusion.5), channel_id=1, replica_groups={{0,2,4,6,8,10,12,14,16,18,20,22,24,26,28,30},{1,3,5,7,9,11,13,15,17,19,..., dimensions={0} | all-to-all | bytes 1835008 | tf_op jit(solution)/shard_map/all_to_all | solution.py:192
  201.4 1.9 collective-permute-start.20
  203.3 7.6 %collective-permute-start.21 = (f32[8,1792]{1,0:T(8,128)S(1)}, f32[8,1792]{1,0:T(8,128)S(1)}, u32[]{:S(2)}, u32[]{:S(2)}) collective-permute-start(f32[8,1792]{1,0:T(8,128)S(1)} %reduce_sum.29), channel_id=1, source_target_pairs={{0,64},{32,96},{64,0},{96,32},{128,192},{160,224},{192,128},{224,1... | collective-permute-start | bytes 172040 | tf_op jit(solution)/shard_map/ppermute | solution.py:21
  210.9 1.9 collective-permute-start.22
  212.9 4.8 %collective-permute-done.22 = f32[8,1792]{1,0:T(8,128)S(1)} collective-permute-done((f32[8,1792]{1,0:T(8,128)S(1)}, f32[8,1792]{1,0:T(8,128)S(1)}, u32[]{:S(2)}, u32[]{:S(2)}) %collective-permute-start.22) | collective-permute-done | bytes 57376 | tf_op jit(solution)/shard_map/ppermute | solution.py:21
  217.7 3.9 %collective-permute-start.23 = (f32[8,1792]{1,0:T(8,128)S(1)}, f32[8,1792]{1,0:T(8,128)S(1)}, u32[]{:S(2)}, u32[]{:S(2)}) collective-permute-start(f32[8,1792]{1,0:T(8,128)S(1)} %add_add_fusion.1), channel_id=1, source_target_pairs={{0,128},{32,160},{64,192},{96,224},{128,0},{160,32},{192,64},{224,... | collective-permute-start | bytes 172040 | tf_op jit(solution)/shard_map/ppermute | solution.py:21
  221.5 6.1 %collective-permute-start.24 = (f32[8,1792]{1,0:T(8,128)S(1)}, f32[8,1792]{1,0:T(8,128)S(1)}, u32[]{:S(2)}, u32[]{:S(2)}) collective-permute-start(f32[8,1792]{1,0:T(8,128)S(1)} %add_add_fusion.1), channel_id=1, source_target_pairs={{0,256},{32,288},{64,320},{96,352},{128,384},{160,416},{192,448},{... | collective-permute-start | bytes 172040 | tf_op jit(solution)/shard_map/ppermute | solution.py:21
  227.7 6.2 %collective-permute-start.25 = (f32[8,1792]{1,0:T(8,128)S(1)}, f32[8,1792]{1,0:T(8,128)S(1)}, u32[]{:S(2)}, u32[]{:S(2)}) collective-permute-start(f32[8,1792]{1,0:T(8,128)S(1)} %add_add_fusion.1), channel_id=1, source_target_pairs={{0,384},{32,416},{64,448},{96,480},{128,256},{160,288},{192,320},{... | collective-permute-start | bytes 172040 | tf_op jit(solution)/shard_map/ppermute | solution.py:21
  233.9 2.1 collective-permute-done.24
  236.8 18.3 %all_to_all.11 = f32[16,8,1792]{2,1,0:T(8,128)S(1)} all-to-all(f32[16,8,1792]{2,1,0:T(8,128)S(1)} %broadcast_in_dim.5), channel_id=1, replica_groups={{0,2,4,6,8,10,12,14,16,18,20,22,24,26,28,30},{1,3,5,7,9,11,13,15,17,19,..., dimensions={0} | all-to-all | bytes 1835008 | tf_op jit(solution)/shard_map/all_to_all | solution.py:192
  255.1 5.9 %collective-permute-start.26 = (f32[128,1792]{1,0:T(8,128)S(1)}, f32[128,1792]{1,0:T(8,128)S(1)}, u32[]{:S(2)}, u32[]{:S(2)}) collective-permute-start(f32[128,1792]{1,0:T(8,128)S(1)} %bitcast.62), channel_id=1, source_target_pairs={{0,1},{1,0},{2,3},{3,2},{4,5},{5,4},{6,7},{7,6},{8,9},{9,8},{10,11... | collective-permute-start | bytes 2752520 | tf_op jit(solution)/shard_map/ppermute | solution.py:21
  261.0 2.1 collective-permute-done.26.theirs
  263.1 34.3 %eliminate.1 = (f32[128,512]{1,0:T(8,128)}, f32[1,512]{1,0:T(1,128)}) custom-call(s32[1]{0:T(128)} %bitcast.core, f32[128,1792]{1,0:T(8,128)S(1)} %bitcast.63, f32[128,1792]{1,0:T(8,128)S(1)} %collective-permute-done.26.theirs, f32[128,512]{1,0:T(8,128)S(1)} %fusion.4.image_in, f32[128,512]{1,0:T(8,128)S(1)} %copy-done), custom_call_target="tpu_custom_call" | custom-call | tf_op jit(solution)/shard_map/eliminate/pallas_call | solution.py:168
  (67 shorter events, 14.1 us)
Async XLA Ops:
  0.6 33.6 %copy-start.1 = (f32[256,1280]{1,0:T(8,128)S(1)}, f32[256,1280]{1,0:T(8,128)}, u32[]{:S(2)}) copy-start(f32[256,1280]{1,0:T(8,128)} %param.14) | copy-start | bytes 3932164
  0.6 131.3 %collective-permute-start = (f32[3,128]{1,0:T(4,128)}, f32[3,128]{1,0:T(4,128)S(1)}, u32[]{:S(2)}, u32[]{:S(2)}) collective-permute-start(f32[3,128]{1,0:T(4,128)} %param.8), channel_id=1, source_target_pairs={{0,1},{1,2},{2,3},{3,4},{4,5},{5,6},{6,7},{7,8},{8,9},{9,10},{10,1... | collective-permute-start | bytes 4616 | tf_op jit(solution)/shard_map/ppermute | solution.py:27
  5.4 144.0 %collective-permute-start.2 = (f32[3,128]{1,0:T(4,128)}, f32[3,128]{1,0:T(4,128)S(1)}, u32[]{:S(2)}, u32[]{:S(2)}) collective-permute-start(f32[3,128]{1,0:T(4,128)} %param.8), channel_id=1, source_target_pairs={{1,0},{2,1},{3,2},{4,3},{5,4},{6,5},{7,6},{8,7},{9,8},{10,9},{11,1... | collective-permute-start | bytes 4616 | tf_op jit(solution)/shard_map/ppermute | solution.py:27
  10.9 26.8 %collective-permute-start.4 = (f32[128,256]{1,0:T(8,128)}, f32[128,256]{1,0:T(8,128)S(1)}, u32[]{:S(2)}, u32[]{:S(2)}) collective-permute-start(f32[128,256]{1,0:T(8,128)} %param.11), channel_id=1, source_target_pairs={{0,256},{32,288},{64,320},{96,352},{128,384},{160,416},{192,448},{... | collective-permute-start | bytes 393224 | tf_op jit(solution)/shard_map/ppermute | solution.py:21
  22.8 126.7 %collective-permute-start.1 = (f32[128,512]{1,0:T(8,128)}, f32[128,512]{1,0:T(8,128)S(1)}, u32[]{:S(2)}, u32[]{:S(2)}) collective-permute-start(f32[128,512]{1,0:T(8,128)} %own_in.1), channel_id=1, source_target_pairs={{0,1},{1,2},{2,3},{3,4},{4,5},{5,6},{6,7},{7,8},{8,9},{9,10},{10,1... | collective-permute-start | bytes 786440 | tf_op jit(solution)/shard_map/ppermute | solution.py:27
  27.7 18.5 %collective-permute-start.13 = (f32[128,256]{1,0:T(8,128)S(1)}, f32[128,256]{1,0:T(8,128)S(1)}, u32[]{:S(2)}, u32[]{:S(2)}) collective-permute-start(f32[128,256]{1,0:T(8,128)S(1)} %get-tuple-element.11), channel_id=1, source_target_pairs={{0,384},{32,416},{64,448},{96,480},{128,256},{160,288},{192,320},{... | collective-permute-start | bytes 393224 | tf_op jit(solution)/shard_map/ppermute | solution.py:21
  32.8 3.1 %copy-start.3 = (s32[1,2]{1,0:T(1,128)S(1)}, s32[1,2]{1,0:T(1,128)}, u32[]{:S(2)}) copy-start(s32[1,2]{1,0:T(1,128)} %param.10) | copy-start | bytes 28
  32.8 3.1 %copy-start.2 = (f32[128,256]{1,0:T(8,128)S(1)}, f32[128,256]{1,0:T(8,128)}, u32[]{:S(2)}) copy-start(f32[128,256]{1,0:T(8,128)} %param.12) | copy-start | bytes 393220
  34.2 2.0 copy-start
  37.6 24.0 %collective-permute-start.5 = (f32[128,256]{1,0:T(8,128)S(1)}, f32[128,256]{1,0:T(8,128)S(1)}, u32[]{:S(2)}, u32[]{:S(2)}) collective-permute-start(f32[128,256]{1,0:T(8,128)S(1)} %get-tuple-element.10), channel_id=1, source_target_pairs={{0,384},{32,416},{64,448},{96,480},{128,256},{160,288},{192,320},{... | collective-permute-start | bytes 393224 | tf_op jit(solution)/shard_map/ppermute | solution.py:21
  46.2 47.1 %collective-permute-start.14 = (f32[128,256]{1,0:T(8,128)S(1)}, f32[128,256]{1,0:T(8,128)S(1)}, u32[]{:S(2)}, u32[]{:S(2)}) collective-permute-start(f32[128,256]{1,0:T(8,128)S(1)} %collective-permute-done.13), channel_id=1, source_target_pairs={{0,128},{32,160},{64,192},{96,224},{128,0},{160,32},{192,64},{224,... | collective-permute-start | bytes 393224 | tf_op jit(solution)/shard_map/ppermute | solution.py:21
  61.7 46.3 %collective-permute-start.7 = (f32[256,256]{0,1:T(8,128)S(1)}, f32[256,256]{0,1:T(8,128)S(1)}, u32[]{:S(2)}, u32[]{:S(2)}) collective-permute-start(f32[256,256]{0,1:T(8,128)S(1)} %pad_maximum_fusion.2), channel_id=1, source_target_pairs={{0,128},{32,160},{64,192},{96,224},{128,0},{160,32},{192,64},{224,... | collective-permute-start | bytes 786440 | tf_op jit(solution)/shard_map/ppermute | solution.py:21
  93.3 11.1 %collective-permute-start.6 = (f32[128,256]{1,0:T(8,128)S(1)}, f32[128,256]{1,0:T(8,128)S(1)}, u32[]{:S(2)}, u32[]{:S(2)}) collective-permute-start(f32[128,256]{1,0:T(8,128)S(1)} %collective-permute-done.5), channel_id=1, source_target_pairs={{0,128},{32,160},{64,192},{96,224},{128,0},{160,32},{192,64},{224,... | collective-permute-start | bytes 393224 | tf_op jit(solution)/shard_map/ppermute | solution.py:21
  104.4 66.5 %collective-permute-start.3 = (f32[128,512]{1,0:T(8,128)S(1)}, f32[128,512]{1,0:T(8,128)S(1)}, u32[]{:S(2)}, u32[]{:S(2)}) collective-permute-start(f32[128,512]{1,0:T(8,128)S(1)} %copy-done), channel_id=1, source_target_pairs={{1,0},{2,1},{3,2},{4,3},{5,4},{6,5},{7,6},{8,7},{9,8},{10,9},{11,1... | collective-permute-start | bytes 786440 | tf_op jit(solution)/shard_map/ppermute | solution.py:27
  107.9 11.0 %collective-permute-start.15 = (f32[128,256]{1,0:T(8,128)S(1)}, f32[128,256]{1,0:T(8,128)S(1)}, u32[]{:S(2)}, u32[]{:S(2)}) collective-permute-start(f32[128,256]{1,0:T(8,128)S(1)} %collective-permute-done.14), channel_id=1, source_target_pairs={{0,384},{32,416},{64,448},{96,480},{128,256},{160,288},{192,320},{... | collective-permute-start | bytes 393224 | tf_op jit(solution)/shard_map/ppermute | solution.py:21
  118.9 9.6 %collective-permute-start.8 = (f32[128,256]{1,0:T(8,128)S(1)}, f32[128,256]{1,0:T(8,128)S(1)}, u32[]{:S(2)}, u32[]{:S(2)}) collective-permute-start(f32[128,256]{1,0:T(8,128)S(1)} %collective-permute-done.6), channel_id=1, source_target_pairs={{0,384},{32,416},{64,448},{96,480},{128,256},{160,288},{192,320},{... | collective-permute-start | bytes 393224 | tf_op jit(solution)/shard_map/ppermute | solution.py:21
  128.5 8.6 %collective-permute-start.16 = (f32[256,256]{1,0:T(8,128)S(1)}, f32[256,256]{1,0:T(8,128)S(1)}, u32[]{:S(2)}, u32[]{:S(2)}) collective-permute-start(f32[256,256]{1,0:T(8,128)S(1)} %convolution_add_fusion), channel_id=1, source_target_pairs={{0,16},{1,17},{2,18},{3,19},{4,20},{5,21},{6,22},{7,23},{8,24},{9,... | collective-permute-start | bytes 786440 | tf_op jit(solution)/shard_map/ppermute | solution.py:21
  132.0 14.9 %collective-permute-start.9 = (f32[256,256]{1,0:T(8,128)S(1)}, f32[256,256]{1,0:T(8,128)S(1)}, u32[]{:S(2)}, u32[]{:S(2)}) collective-permute-start(f32[256,256]{1,0:T(8,128)S(1)} %convolution_add_fusion.1), channel_id=1, source_target_pairs={{0,16},{1,17},{2,18},{3,19},{4,20},{5,21},{6,22},{7,23},{8,24},{9,... | collective-permute-start | bytes 786440 | tf_op jit(solution)/shard_map/ppermute | solution.py:21
  137.2 18.0 %collective-permute-start.11 = (f32[128,256]{0,1:T(8,128)S(1)}, f32[128,256]{0,1:T(8,128)S(1)}, u32[]{:S(2)}, u32[]{:S(2)}) collective-permute-start(f32[128,256]{0,1:T(8,128)S(1)} %convolution_bitcast_fusion), channel_id=1, source_target_pairs={{0,4},{1,5},{2,6},{3,7},{4,0},{5,1},{6,2},{7,3},{8,12},{9,13},{10,... | collective-permute-start | bytes 393224 | tf_op jit(solution)/shard_map/ppermute | solution.py:21
  147.5 7.1 %collective-permute-start.10 = (f32[256,256]{1,0:T(8,128)S(1)}, f32[256,256]{1,0:T(8,128)S(1)}, u32[]{:S(2)}, u32[]{:S(2)}) collective-permute-start(f32[256,256]{1,0:T(8,128)S(1)} %get-tuple-element.31), channel_id=1, source_target_pairs={{0,8},{1,9},{2,10},{3,11},{4,12},{5,13},{6,14},{7,15},{8,0},{9,1},... | collective-permute-start | bytes 786440 | tf_op jit(solution)/shard_map/ppermute | solution.py:21
  150.8 10.8 %collective-permute-start.17 = (f32[256,256]{1,0:T(8,128)S(1)}, f32[256,256]{1,0:T(8,128)S(1)}, u32[]{:S(2)}, u32[]{:S(2)}) collective-permute-start(f32[256,256]{1,0:T(8,128)S(1)} %get-tuple-element.32), channel_id=1, source_target_pairs={{0,8},{1,9},{2,10},{3,11},{4,12},{5,13},{6,14},{7,15},{8,0},{9,1},... | collective-permute-start | bytes 786440 | tf_op jit(solution)/shard_map/ppermute | solution.py:21
  155.7 11.7 %collective-permute-start.12 = (f32[128,256]{1,0:T(8,128)S(1)}, f32[128,256]{1,0:T(8,128)S(1)}, u32[]{:S(2)}, u32[]{:S(2)}) collective-permute-start(f32[128,256]{1,0:T(8,128)S(1)} %fusion.121), channel_id=1, source_target_pairs={{0,4},{1,5},{2,6},{3,7},{4,0},{5,1},{6,2},{7,3},{8,12},{9,13},{10,... | collective-permute-start | bytes 393224 | tf_op jit(solution)/shard_map/ppermute | solution.py:21
  162.6 8.2 %collective-permute-start.18 = (f32[128,256]{1,0:T(8,128)S(1)}, f32[128,256]{1,0:T(8,128)S(1)}, u32[]{:S(2)}, u32[]{:S(2)}) collective-permute-start(f32[128,256]{1,0:T(8,128)S(1)} %fusion.122), channel_id=1, source_target_pairs={{0,4},{1,5},{2,6},{3,7},{4,0},{5,1},{6,2},{7,3},{8,12},{9,13},{10,... | collective-permute-start | bytes 393224 | tf_op jit(solution)/shard_map/ppermute | solution.py:21
  172.3 8.5 %collective-permute-start.19 = (f32[128,512]{1,0:T(8,128)S(1)}, f32[128,512]{1,0:T(8,128)S(1)}, u32[]{:S(2)}, u32[]{:S(2)}) collective-permute-start(f32[128,512]{1,0:T(8,128)S(1)} %fusion.4.image_in), channel_id=1, source_target_pairs={{0,1},{1,0},{2,3},{3,2},{4,5},{5,4},{6,7},{7,6},{8,9},{9,8},{10,11... | collective-permute-start | bytes 786440 | tf_op jit(solution)/shard_map/ppermute | solution.py:21
  201.4 11.5 %collective-permute-start.20 = (f32[8,1792]{1,0:T(8,128)S(1)}, f32[8,1792]{1,0:T(8,128)S(1)}, u32[]{:S(2)}, u32[]{:S(2)}) collective-permute-start(f32[8,1792]{1,0:T(8,128)S(1)} %reduce_sum.29), channel_id=1, source_target_pairs={{0,32},{32,0},{64,96},{96,64},{128,160},{160,128},{192,224},{224,1... | collective-permute-start | bytes 172040 | tf_op jit(solution)/shard_map/ppermute | solution.py:21
  203.3 9.6 %collective-permute-start.21 = (f32[8,1792]{1,0:T(8,128)S(1)}, f32[8,1792]{1,0:T(8,128)S(1)}, u32[]{:S(2)}, u32[]{:S(2)}) collective-permute-start(f32[8,1792]{1,0:T(8,128)S(1)} %reduce_sum.29), channel_id=1, source_target_pairs={{0,64},{32,96},{64,0},{96,32},{128,192},{160,224},{192,128},{224,1... | collective-permute-start | bytes 172040 | tf_op jit(solution)/shard_map/ppermute | solution.py:21
  210.9 6.7 %collective-permute-start.22 = (f32[8,1792]{1,0:T(8,128)S(1)}, f32[8,1792]{1,0:T(8,128)S(1)}, u32[]{:S(2)}, u32[]{:S(2)}) collective-permute-start(f32[8,1792]{1,0:T(8,128)S(1)} %reduce_sum.29), channel_id=1, source_target_pairs={{0,96},{32,64},{64,32},{96,0},{128,224},{160,192},{192,160},{224,1... | collective-permute-start | bytes 172040 | tf_op jit(solution)/shard_map/ppermute | solution.py:21
  217.7 16.2 %collective-permute-start.23 = (f32[8,1792]{1,0:T(8,128)S(1)}, f32[8,1792]{1,0:T(8,128)S(1)}, u32[]{:S(2)}, u32[]{:S(2)}) collective-permute-start(f32[8,1792]{1,0:T(8,128)S(1)} %add_add_fusion.1), channel_id=1, source_target_pairs={{0,128},{32,160},{64,192},{96,224},{128,0},{160,32},{192,64},{224,... | collective-permute-start | bytes 172040 | tf_op jit(solution)/shard_map/ppermute | solution.py:21
  221.5 14.5 %collective-permute-start.24 = (f32[8,1792]{1,0:T(8,128)S(1)}, f32[8,1792]{1,0:T(8,128)S(1)}, u32[]{:S(2)}, u32[]{:S(2)}) collective-permute-start(f32[8,1792]{1,0:T(8,128)S(1)} %add_add_fusion.1), channel_id=1, source_target_pairs={{0,256},{32,288},{64,320},{96,352},{128,384},{160,416},{192,448},{... | collective-permute-start | bytes 172040 | tf_op jit(solution)/shard_map/ppermute | solution.py:21
  227.7 9.0 %collective-permute-start.25 = (f32[8,1792]{1,0:T(8,128)S(1)}, f32[8,1792]{1,0:T(8,128)S(1)}, u32[]{:S(2)}, u32[]{:S(2)}) collective-permute-start(f32[8,1792]{1,0:T(8,128)S(1)} %add_add_fusion.1), channel_id=1, source_target_pairs={{0,384},{32,416},{64,448},{96,480},{128,256},{160,288},{192,320},{... | collective-permute-start | bytes 172040 | tf_op jit(solution)/shard_map/ppermute | solution.py:21
  255.1 8.0 %collective-permute-start.26 = (f32[128,1792]{1,0:T(8,128)S(1)}, f32[128,1792]{1,0:T(8,128)S(1)}, u32[]{:S(2)}, u32[]{:S(2)}) collective-permute-start(f32[128,1792]{1,0:T(8,128)S(1)} %bitcast.62), channel_id=1, source_target_pairs={{0,1},{1,0},{2,3},{3,2},{4,5},{5,4},{6,7},{7,6},{8,9},{9,8},{10,11... | collective-permute-start | bytes 2752520 | tf_op jit(solution)/shard_map/ppermute | solution.py:21

commit v3 on v2

--- a/solution.py
+++ b/solution.py
@@ -8,7 +8,6 @@
 from jax.sharding import PartitionSpec as P
 
 LEVELS = 5
-CHUNKS = 2
 
 
 WAVENUM = 6.0
@@ -192,17 +191,30 @@
     return lax.all_to_all(tiles, "col", 0, 0, axis_index_groups=plane_groups(), tiled=True)
 
 
-def quad_sum(share, unit):
-    one, two, three = (swapped(share, "row", unit * k) for k in (1, 2, 3))
-    return (share + one) + (two + three)
+def in_quads(tiles, groups):
+    return lax.all_to_all(tiles, "row", 0, 0, axis_index_groups=groups, tiled=True)
+
+
+def copies(share, count):
+    return jnp.broadcast_to(share[None], (count, *share.shape))
+
+
+def column_sum(share):
+    quads = lax.axis_size("row") // 4
+    near = [[4 * quad + place for place in range(4)] for quad in range(quads)]
+    far = [list(group) for group in zip(*near)]
+    rows, columns = share.shape
+    parts = jnp.moveaxis(share.reshape(rows, 4, columns // 4), 1, 0)
+    part = jnp.sum(in_quads(parts, near), axis=0)
+    part = jnp.sum(in_quads(copies(part, quads), far), axis=0)
+    return jnp.moveaxis(in_quads(copies(part, 4), near), 0, 1).reshape(rows, columns)
 
 
 def global_sum(half):
     chips = lax.axis_size("col") // 2
     rows = half.shape[0] // chips
-    share = jnp.sum(within_plane(half.reshape(chips, rows, -1)), axis=0)
-    share = quad_sum(quad_sum(share, 1), 4)
-    return within_plane(jnp.broadcast_to(share[None], (chips, *share.shape))).reshape(half.shape)
+    share = column_sum(jnp.sum(within_plane(half.reshape(chips, rows, -1)), axis=0))
+    return within_plane(copies(share, chips)).reshape(half.shape)
 
 
 def half_of_sums(core, image, own, pair_image, pair_own, own_squares):
@@ -226,16 +238,8 @@
     coords, residual_in, link_mask, compress, expand, level_gain, level_couple, partner_perm
 ):
     rank = compress.shape[1]
-    chunks = jnp.split(residual_in, CHUNKS, axis=1)
+    columns = residual_in.shape[1]
     core = lax.axis_index("col") & 1
-
-    by_three = [swapped(chunk, "row", 12) for chunk in chunks]
-    compress_two = swapped(compress, "row", 8)
-    by_two = [swapped(chunk, "row", 4) for chunk in by_three]
-    by_one = [swapped(chunk, "row", 12) for chunk in by_two]
-
-    below_xyz, below_rhs = from_behind((coords, residual_in), ("row", "col"), 1)
-    above_xyz, above_rhs = from_behind((coords, residual_in), ("row", "col"), -1)
 
     gains = [level_gain[0, k * rank : (k + 1) * rank][:, None] for k in range(LEVELS)]
     numbers = jnp.arange(rank, dtype=jnp.int32)[None, :]
@@ -246,14 +250,40 @@
         return matmul_hi(couple, place)
 
     couples = [couple_of(k) for k in range(LEVELS)]
-    last_partner = swapped(matmul_hi(expand, couples[4]), "col", 4)
-    last_own = expand * level_gain[:, 4 * rank :]
-
+
+    by_one = swapped(residual_in, "row", 4)
+    by_three = swapped(residual_in, "row", 12)
+    compress_two = swapped(compress, "row", 8)
+    rows = residual_in.shape[0]
+    placed = jnp.pad(coords, ((0, 5), (0, columns - coords.shape[1])))
+    near_points = jnp.concatenate([residual_in, placed], axis=0)
+    below = from_behind(near_points, ("row", "col"), 1)
+    above = from_behind(near_points, ("row", "col"), -1)
+    below_rhs, above_rhs = below[:rows], above[:rows]
+    below_xyz, above_xyz = below[rows : rows + 3, :rows], above[rows : rows + 3, :rows]
+
+    points = expand.shape[0]
+    expand_own = expand * level_gain[:, 4 * rank :]
+    from_last = swapped(matmul_hi(expand, couples[4]), "col", 4)
+
+    by_one, compress_two, from_last = lax.optimization_barrier((by_one, compress_two, from_last))
+    by_two = swapped(by_one, "row", 12)
     low_map = jnp.concatenate(
         [gains[0] * compress.T, matmul_hi(couples[0], compress_two, 1, 1)], axis=1
     )
-    low_map_one = matmul_hi(couples[1], swapped(low_map, "row", 4))
-    low_map_own = gains[1] * low_map
+    low_map_one = swapped(low_map, "row", 4)
+    from_both = swapped(
+        matmul_hi(jnp.concatenate([expand_own, from_last], axis=0), couples[3]), "col", 8
+    )
+    by_two, low_map_one, by_three, from_both = lax.optimization_barrier(
+        (by_two, low_map_one, by_three, from_both)
+    )
+
+    maps = [expand_own * gains[3][:, 0], from_last * gains[3][:, 0]]
+    maps += [from_both[:points], from_both[points:]]
+    last_bit, next_bit = (lax.axis_index("col") & 4) > 0, (lax.axis_index("col") & 8) > 0
+    maps = [jnp.where(last_bit, maps[k ^ 1], maps[k]) for k in range(4)]
+    maps = jnp.concatenate([jnp.where(next_bit, maps[k ^ 2], maps[k]) for k in range(4)], axis=0)
 
     near_scale = (3.0 * coords.shape[1]) ** (-0.5)
     weights = link_mask.astype(jnp.float32)
@@ -265,15 +295,14 @@
     pair_own = jnp.where(core == 1, below_rhs, above_rhs)
     pair_squares = jnp.sum(pair_own * pair_own, axis=0)
 
-    far_parts = []
-    for own, one, two, three in zip(chunks, by_one, by_two, by_three):
-        coeffs = matmul_hi(low_map_own, jnp.concatenate([own, two], axis=0))
-        coeffs = coeffs + matmul_hi(low_map_one, jnp.concatenate([one, three], axis=0))
-        coeffs = gains[2] * coeffs + matmul_hi(couples[2], swapped(coeffs, "col", 16))
-        coeffs = gains[3] * coeffs + matmul_hi(couples[3], swapped(coeffs, "col", 8))
-        sent = swapped(matmul_hi(last_partner, coeffs), "col", 4)
-        far_parts.append(matmul_hi(last_own, coeffs) + sent)
-    image = base + jnp.concatenate(far_parts, axis=1)
+    coeffs = gains[1] * matmul_hi(low_map, jnp.concatenate([residual_in, by_two], axis=0))
+    low_map_one = matmul_hi(couples[1], low_map_one)
+    coeffs = coeffs + matmul_hi(low_map_one, jnp.concatenate([by_one, by_three], axis=0))
+    coeffs = gains[2] * coeffs + matmul_hi(couples[2], swapped(coeffs, "col", 16))
+    given = matmul_hi(maps, coeffs).reshape(4, points, columns)
+    quads = [[16 * x + 2 * y + e + 4 * k for k in range(4)] for x in range(2) for y in range(2) for e in range(2)]
+    taken = lax.all_to_all(given, "col", 0, 0, axis_index_groups=quads, tiled=True)
+    image = base + jnp.sum(taken, axis=0)
 
     half = half_of_sums(
         core, image, residual_in, swapped(image, "col", 1), pair_own, own_squares + pair_squares

time: 300 us -> 252 us (0.84)
  starting transfers between devices: 133 us -> 72.1 us
  blocking collectives: 37.1 us -> 67.5 us
  waiting for transfers between devices: 70.8 us -> 55.9 us
    ppermute x23 -> x10, starting transfers between devices: 116 us -> 61.2 us  [swapped(): lax.ppermute(block, axis, [(i, i ^ bits) for i in range(lax.axis_size(axi...]
    all_to_all x0 -> x3, blocking collectives: none -> 33.8 us  [in_quads(): lax.all_to_all(tiles, 'row', 0, 0, axis_index_groups=groups, tiled=True)]
    ppermute x23 -> x10, waiting for transfers between devices: 70.8 us -> 43.3 us  [swapped(): lax.ppermute(block, axis, [(i, i ^ bits) for i in range(lax.axis_size(axi...]
    all_to_all x0 -> x1, waiting for transfers between devices: none -> 12.6 us  [shards(): lax.all_to_all(given, 'col', 0, 0, axis_index_groups=quads, tiled=True)]
    ppermute x4 -> x2, starting transfers between devices: 17.1 us -> 6.94 us  [from_behind(): return lax.ppermute(block, axis, route)]
    all_to_all x0 -> x1, starting transfers between devices: none -> 3.95 us  [shards(): lax.all_to_all(given, 'col', 0, 0, axis_index_groups=quads, tiled=True)]
    all_to_all x2, blocking collectives: 37.1 us -> 33.8 us  [within_plane(): lax.all_to_all(tiles, 'col', 0, 0, axis_index_groups=plane_groups(), tile...]
    dot_general x26 -> x19, matrix products: 15.2 us -> 15.4 us  [matmul_hi(): return lax.dot_general(left, right, dims, precision=lax.Precision.HIGHEST)]
  transfers between devices with their start and end apart: 27 -> 13, of which waited for: 13 -> 6; matrix products, arithmetic and copies ran while one was open for 6% -> 6% of each run, Pallas kernels for 0% -> 0%
where the time goes in v3:
time: 252 us; the launch traced here: 251 us
  starting transfers between devices  72.1 us (29%)
  blocking collectives  67.5 us (27%)
  waiting for transfers between devices  55.9 us (22%)
  Pallas kernels  34.5 us (14%)
  matrix products  15.4 us (6%)
    ppermute x10, starting transfers between devices, swapped(): lax.ppermute(block, axis, [(i, i ^ bits) for i in range(lax.axis_size(axi...  61.2 us
    ppermute x10, waiting for transfers between devices, swapped(): lax.ppermute(block, axis, [(i, i ^ bits) for i in range(lax.axis_size(axi...  43.3 us
    pallas_call x1, Pallas kernels, project_out(): pl.pallas_call(functools.partial(eliminate, points_total), in_specs=[pl.B...  34.5 us
    all_to_all x3, blocking collectives, in_quads(): lax.all_to_all(tiles, 'row', 0, 0, axis_index_groups=groups, tiled=True)  33.8 us
    all_to_all x2, blocking collectives, within_plane(): lax.all_to_all(tiles, 'col', 0, 0, axis_index_groups=plane_groups(), tile...  33.8 us
    dot_general x19, matrix products, matmul_hi(): return lax.dot_general(left, right, dims, precision=lax.Precision.HIGHEST)  15.4 us
    all_to_all x1, waiting for transfers between devices, shards(): lax.all_to_all(given, 'col', 0, 0, axis_index_groups=quads, tiled=True)  12.6 us
    ppermute x2, starting transfers between devices, from_behind(): return lax.ppermute(block, axis, route)  6.94 us
  transfers between devices with their start and end apart: 13, of which 6 were waited for; matrix products, arithmetic and copies ran while one was open for 6% of the time, Pallas kernels for 0%

profile of v3, /device:TPU:1, one launch (start us, length us, event | category | flops | bytes accessed | tf_op | source)
XLA Modules:
  0.0 250.9 jit_solution(13730955240116133470)
XLA Ops:
  0.7 9.8 %collective-permute-start.2 = (f32[128,512]{1,0:T(8,128)}, f32[128,512]{1,0:T(8,128)}, u32[]{:S(2)}, u32[]{:S(2)}) collective-permute-start(f32[128,512]{1,0:T(8,128)} %own_in.1), channel_id=1, source_target_pairs={{0,128},{32,160},{64,192},{96,224},{128,0},{160,32},{192,64},{224,... | collective-permute-start | bytes 786440 | tf_op jit(solution)/shard_map/ppermute | solution.py:20
  10.4 8.8 %collective-permute-start.7 = (f32[128,512]{1,0:T(8,128)}, f32[128,512]{1,0:T(8,128)}, u32[]{:S(2)}, u32[]{:S(2)}) collective-permute-start(f32[128,512]{1,0:T(8,128)} %own_in.1), channel_id=1, source_target_pairs={{0,384},{32,416},{64,448},{96,480},{128,256},{160,288},{192,320},{... | collective-permute-start | bytes 786440 | tf_op jit(solution)/shard_map/ppermute | solution.py:20
  19.3 0.7 fusion.154
  20.0 1.3 fusion.37
  21.4 1.3 convolution_bitcast_fusion
  22.7 5.0 %collective-permute-start.4 = (f32[128,256]{0,1:T(8,128)S(1)}, f32[128,256]{0,1:T(8,128)S(1)}, u32[]{:S(2)}, u32[]{:S(2)}) collective-permute-start(f32[128,256]{0,1:T(8,128)S(1)} %convolution_bitcast_fusion), channel_id=1, source_target_pairs={{0,4},{1,5},{2,6},{3,7},{4,0},{5,1},{6,2},{7,3},{8,12},{9,13},{10,... | collective-permute-start | bytes 393224 | tf_op jit(solution)/shard_map/ppermute | solution.py:20
  27.7 3.7 %collective-permute-start.3 = (f32[128,256]{1,0:T(8,128)}, f32[128,256]{1,0:T(8,128)S(1)}, u32[]{:S(2)}, u32[]{:S(2)}) collective-permute-start(f32[128,256]{1,0:T(8,128)} %param.11), channel_id=1, source_target_pairs={{0,256},{32,288},{64,320},{96,352},{128,384},{160,416},{192,448},{... | collective-permute-start | bytes 393224 | tf_op jit(solution)/shard_map/ppermute | solution.py:20
  31.4 1.7 select_maximum_fusion.1
  33.1 3.7 %collective-permute-start = (f32[136,512]{1,0:T(8,128)}, f32[136,512]{1,0:T(8,128)S(1)}, u32[]{:S(2)}, u32[]{:S(2)}) collective-permute-start(f32[136,512]{1,0:T(8,128)} %select_maximum_fusion.1), channel_id=1, source_target_pairs={{0,1},{1,2},{2,3},{3,4},{4,5},{5,6},{6,7},{7,8},{8,9},{9,10},{10,1... | collective-permute-start | bytes 835592 | tf_op jit(solution)/shard_map/ppermute | solution.py:26
  36.9 0.4 fusion.33
  37.3 0.4 fusion.35
  37.7 0.4 fusion.31
  38.4 10.7 %collective-permute-done.3 = f32[128,256]{1,0:T(8,128)S(1)} collective-permute-done((f32[128,256]{1,0:T(8,128)}, f32[128,256]{1,0:T(8,128)S(1)}, u32[]{:S(2)}, u32[]{:S(2)}) %collective-permute-start.3) | collective-permute-done | bytes 131104 | tf_op jit(solution)/shard_map/ppermute | solution.py:20
  49.1 0.4 fusion.25
  49.5 3.1 %collective-permute-start.8 = (f32[256,256]{0,1:T(8,128)S(1)}, f32[256,256]{0,1:T(8,128)S(1)}, u32[]{:S(2)}, u32[]{:S(2)}) collective-permute-start(f32[256,256]{0,1:T(8,128)S(1)} %fusion.25), channel_id=1, source_target_pairs={{0,8},{1,9},{2,10},{3,11},{4,12},{5,13},{6,14},{7,15},{8,0},{9,1},... | collective-permute-start | bytes 786440 | tf_op jit(solution)/shard_map/ppermute | solution.py:20
  52.6 0.3 fusion.156
  53.0 8.3 %collective-permute-start.6 = (f32[256,256]{0,1:T(8,128)S(1)}, f32[256,256]{0,1:T(8,128)S(1)}, u32[]{:S(2)}, u32[]{:S(2)}) collective-permute-start(f32[256,256]{0,1:T(8,128)S(1)} %pad_maximum_fusion.6), channel_id=1, source_target_pairs={{0,128},{32,160},{64,192},{96,224},{128,0},{160,32},{192,64},{224,... | collective-permute-start | bytes 786440 | tf_op jit(solution)/shard_map/ppermute | solution.py:20
  61.2 5.8 %collective-permute-start.5 = (f32[128,512]{1,0:T(8,128)}, f32[128,512]{1,0:T(8,128)S(1)}, u32[]{:S(2)}, u32[]{:S(2)}) collective-permute-start(f32[128,512]{1,0:T(8,128)} %collective-permute-done.2), channel_id=1, source_target_pairs={{0,384},{32,416},{64,448},{96,480},{128,256},{160,288},{192,320},{... | collective-permute-start | bytes 786440 | tf_op jit(solution)/shard_map/ppermute | solution.py:20
  67.0 0.4 fusion.29
  67.5 3.2 %collective-permute-start.1 = (f32[136,512]{1,0:T(8,128)}, f32[136,512]{1,0:T(8,128)S(1)}, u32[]{:S(2)}, u32[]{:S(2)}) collective-permute-start(f32[136,512]{1,0:T(8,128)} %select_maximum_fusion.1), channel_id=1, source_target_pairs={{1,0},{2,1},{3,2},{4,3},{5,4},{6,5},{7,6},{8,7},{9,8},{10,9},{11,1... | collective-permute-start | bytes 835592 | tf_op jit(solution)/shard_map/ppermute | solution.py:26
  70.7 18.3 %collective-permute-done.5 = f32[128,512]{1,0:T(8,128)S(1)} collective-permute-done((f32[128,512]{1,0:T(8,128)}, f32[128,512]{1,0:T(8,128)S(1)}, u32[]{:S(2)}, u32[]{:S(2)}) %collective-permute-start.5) | collective-permute-done | bytes 262176 | tf_op jit(solution)/shard_map/ppermute | solution.py:20
  89.0 0.6 convolution_multiply_fusion
  89.7 0.6 fusion.157
  90.3 1.6 convolution_add_fusion.1
  91.9 4.3 %collective-permute-start.9 = (f32[256,512]{1,0:T(8,128)S(1)}, f32[256,512]{1,0:T(8,128)S(1)}, u32[]{:S(2)}, u32[]{:S(2)}) collective-permute-start(f32[256,512]{1,0:T(8,128)S(1)} %convolution_add_fusion.1), channel_id=1, source_target_pairs={{0,16},{1,17},{2,18},{3,19},{4,20},{5,21},{6,22},{7,23},{8,24},{9,... | collective-permute-start | bytes 1572872 | tf_op jit(solution)/shard_map/ppermute | solution.py:20
  96.3 0.7 fusion.96
  97.0 0.1 broadcast_select_fusion.3
  97.2 11.1 %collective-permute-done.9 = f32[256,512]{1,0:T(8,128)S(1)} collective-permute-done((f32[256,512]{1,0:T(8,128)S(1)}, f32[256,512]{1,0:T(8,128)S(1)}, u32[]{:S(2)}, u32[]{:S(2)}) %collective-permute-start.9) | collective-permute-done | bytes 524320 | tf_op jit(solution)/shard_map/ppermute | solution.py:20
  108.3 0.6 convolution_add_fusion
  109.0 2.0 fusion.8
  111.0 4.0 %all-to-all-start = ((f32[4,128,512]{2,1,0:T(8,128)}), f32[4,128,512]{2,1,0:T(8,128)S(1)}, u32[]{:S(2)}, u32[]{:S(2)}) async-start(f32[4,128,512]{2,1,0:T(8,128)} %bitcast.24), calls=%async_computation | async-start | bytes 2097152 | tf_op jit(solution)/shard_map/all_to_all | solution.py:304
  114.9 0.6 fusion.155
  115.6 1.4 fusion.2
  116.9 12.6 %all-to-all-done = f32[4,128,512]{2,1,0:T(8,128)S(1)} async-done(((f32[4,128,512]{2,1,0:T(8,128)}), f32[4,128,512]{2,1,0:T(8,128)S(1)}, u32[]{:S(2)}, u32[]{:S(2)}) %all-to-all-start) | async-done | bytes 1048608 | tf_op jit(solution)/shard_map/all_to_all | solution.py:304
  129.6 1.4 fusion.4.image_in
  131.0 3.4 %collective-permute-start.10 = (f32[128,512]{1,0:T(8,128)S(1)}, f32[128,512]{1,0:T(8,128)S(1)}, u32[]{:S(2)}, u32[]{:S(2)}) collective-permute-start(f32[128,512]{1,0:T(8,128)S(1)} %fusion.4.image_in), channel_id=1, source_target_pairs={{0,1},{1,0},{2,3},{3,2},{4,5},{5,4},{6,7},{7,6},{8,9},{9,8},{10,11... | collective-permute-start | bytes 786440 | tf_op jit(solution)/shard_map/ppermute | solution.py:20
  134.5 1.1 collective-permute-done.10
  135.5 0.5 fusion.7
  136.0 0.4 fusion.58
  136.4 0.6 fusion.6
  137.3 18.9 %all_to_all.30 = f32[16,8,1792]{2,1,0:T(8,128)S(1)} all-to-all(f32[16,8,1792]{2,1,0:T(8,128)S(1)} %fusion.5), channel_id=1, replica_groups={{0,2,4,6,8,10,12,14,16,18,20,22,24,26,28,30},{1,3,5,7,9,11,13,15,17,19,..., dimensions={0} | all-to-all | bytes 1835008 | tf_op jit(solution)/shard_map/all_to_all | solution.py:191
  156.4 8.4 %all_to_all.31 = f32[4,8,448]{2,1,0:T(8,128)S(1)} all-to-all(f32[4,8,448]{2,1,0:T(8,128)S(1)} %copy.20), channel_id=1, replica_groups={{0,32,64,96},{128,160,192,224},{256,288,320,352},{384,416,448,480},{1,3..., dimensions={0} | all-to-all | bytes 114688 | tf_op jit(solution)/shard_map/all_to_all | solution.py:195
  164.8 18.4 %all_to_all.32 = f32[4,8,448]{2,1,0:T(8,128)S(1)} all-to-all(f32[4,8,448]{2,1,0:T(8,128)S(1)} %broadcast_in_dim.11), channel_id=1, replica_groups={{0,128,256,384},{32,160,288,416},{64,192,320,448},{96,224,352,480},{1,1..., dimensions={0} | all-to-all | bytes 114688 | tf_op jit(solution)/shard_map/all_to_all | solution.py:195
  183.2 7.0 %all_to_all.33 = f32[4,8,448]{2,1,0:T(8,128)S(1)} all-to-all(f32[4,8,448]{2,1,0:T(8,128)S(1)} %broadcast_in_dim.12), channel_id=1, replica_groups={{0,32,64,96},{128,160,192,224},{256,288,320,352},{384,416,448,480},{1,3..., dimensions={0} | all-to-all | bytes 114688 | tf_op jit(solution)/shard_map/all_to_all | solution.py:195
  190.4 14.8 %all_to_all.34 = f32[16,8,1792]{2,1,0:T(8,128)S(1)} all-to-all(f32[16,8,1792]{2,1,0:T(8,128)S(1)} %broadcast_in_dim.27), channel_id=1, replica_groups={{0,2,4,6,8,10,12,14,16,18,20,22,24,26,28,30},{1,3,5,7,9,11,13,15,17,19,..., dimensions={0} | all-to-all | bytes 1835008 | tf_op jit(solution)/shard_map/all_to_all | solution.py:191
  205.2 9.0 %collective-permute-start.11 = (f32[128,1792]{1,0:T(8,128)S(1)}, f32[128,1792]{1,0:T(8,128)S(1)}, u32[]{:S(2)}, u32[]{:S(2)}) collective-permute-start(f32[128,1792]{1,0:T(8,128)S(1)} %bitcast.56), channel_id=1, source_target_pairs={{0,1},{1,0},{2,3},{3,2},{4,5},{5,4},{6,7},{7,6},{8,9},{9,8},{10,11... | collective-permute-start | bytes 2752520 | tf_op jit(solution)/shard_map/ppermute | solution.py:20
  214.3 2.1 collective-permute-done.11.theirs
  216.4 34.5 %eliminate.1 = (f32[128,512]{1,0:T(8,128)}, f32[1,512]{1,0:T(1,128)}) custom-call(s32[1]{0:T(128)} %bitcast.core, f32[128,1792]{1,0:T(8,128)S(1)} %bitcast.57, f32[128,1792]{1,0:T(8,128)S(1)} %collective-permute-done.11.theirs, f32[128,512]{1,0:T(8,128)S(1)} %fusion.4.image_in, f32[128,512]{1,0:T(8,128)S(1)} %copy-done), custom_call_target="tpu_custom_call" | custom-call | tf_op jit(solution)/shard_map/eliminate/pallas_call | solution.py:167
  (49 shorter events, 1.1 us)
Async XLA Ops:
  0.6 36.2 %copy-start.1 = (f32[256,1280]{1,0:T(8,128)S(1)}, f32[256,1280]{1,0:T(8,128)}, u32[]{:S(2)}) copy-start(f32[256,1280]{1,0:T(8,128)} %param.14) | copy-start | bytes 3932164
  0.6 36.2 %copy-start.5 = (f32[1,1280]{1,0:T(1,128)S(1)}, f32[1,1280]{1,0:T(1,128)}, u32[]{:S(2)}) copy-start(f32[1,1280]{1,0:T(1,128)} %param.13) | copy-start | bytes 15364
  0.7 48.4 %collective-permute-start.2 = (f32[128,512]{1,0:T(8,128)}, f32[128,512]{1,0:T(8,128)}, u32[]{:S(2)}, u32[]{:S(2)}) collective-permute-start(f32[128,512]{1,0:T(8,128)} %own_in.1), channel_id=1, source_target_pairs={{0,128},{32,160},{64,192},{96,224},{128,0},{160,32},{192,64},{224,... | collective-permute-start | bytes 786440 | tf_op jit(solution)/shard_map/ppermute | solution.py:20
  10.4 57.0 %collective-permute-start.7 = (f32[128,512]{1,0:T(8,128)}, f32[128,512]{1,0:T(8,128)}, u32[]{:S(2)}, u32[]{:S(2)}) collective-permute-start(f32[128,512]{1,0:T(8,128)} %own_in.1), channel_id=1, source_target_pairs={{0,384},{32,416},{64,448},{96,480},{128,256},{160,288},{192,320},{... | collective-permute-start | bytes 786440 | tf_op jit(solution)/shard_map/ppermute | solution.py:20
  21.4 16.7 %copy-start.3 = (f32[128,256]{1,0:T(8,128)S(1)}, f32[128,256]{1,0:T(8,128)}, u32[]{:S(2)}) copy-start(f32[128,256]{1,0:T(8,128)} %param.11) | copy-start | bytes 393220
  22.7 15.4 %copy-start.2 = (f32[128,256]{1,0:T(8,128)S(1)}, f32[128,256]{1,0:T(8,128)}, u32[]{:S(2)}) copy-start(f32[128,256]{1,0:T(8,128)} %param.12) | copy-start | bytes 393220
  22.7 15.6 %collective-permute-start.4 = (f32[128,256]{0,1:T(8,128)S(1)}, f32[128,256]{0,1:T(8,128)S(1)}, u32[]{:S(2)}, u32[]{:S(2)}) collective-permute-start(f32[128,256]{0,1:T(8,128)S(1)} %convolution_bitcast_fusion), channel_id=1, source_target_pairs={{0,4},{1,5},{2,6},{3,7},{4,0},{5,1},{6,2},{7,3},{8,12},{9,13},{10,... | collective-permute-start | bytes 393224 | tf_op jit(solution)/shard_map/ppermute | solution.py:20
  27.7 21.4 %collective-permute-start.3 = (f32[128,256]{1,0:T(8,128)}, f32[128,256]{1,0:T(8,128)S(1)}, u32[]{:S(2)}, u32[]{:S(2)}) collective-permute-start(f32[128,256]{1,0:T(8,128)} %param.11), channel_id=1, source_target_pairs={{0,256},{32,288},{64,320},{96,352},{128,384},{160,416},{192,448},{... | collective-permute-start | bytes 393224 | tf_op jit(solution)/shard_map/ppermute | solution.py:20
  33.1 82.4 %collective-permute-start = (f32[136,512]{1,0:T(8,128)}, f32[136,512]{1,0:T(8,128)S(1)}, u32[]{:S(2)}, u32[]{:S(2)}) collective-permute-start(f32[136,512]{1,0:T(8,128)} %select_maximum_fusion.1), channel_id=1, source_target_pairs={{0,1},{1,2},{2,3},{3,4},{4,5},{5,6},{6,7},{7,8},{8,9},{9,10},{10,1... | collective-permute-start | bytes 835592 | tf_op jit(solution)/shard_map/ppermute | solution.py:26
  38.1 28.9 %copy-start.4 = (f32[3,128]{1,0:T(4,128)S(1)}, f32[3,128]{1,0:T(4,128)}, u32[]{:S(2)}) copy-start(f32[3,128]{1,0:T(4,128)} %param.8) | copy-start | bytes 4612
  38.2 50.8 %copy-start = (f32[128,512]{1,0:T(8,128)S(1)}, f32[128,512]{1,0:T(8,128)}, u32[]{:S(2)}) copy-start(f32[128,512]{1,0:T(8,128)} %own_in.1) | copy-start | bytes 786436
  49.5 21.2 %collective-permute-start.8 = (f32[256,256]{0,1:T(8,128)S(1)}, f32[256,256]{0,1:T(8,128)S(1)}, u32[]{:S(2)}, u32[]{:S(2)}) collective-permute-start(f32[256,256]{0,1:T(8,128)S(1)} %fusion.25), channel_id=1, source_target_pairs={{0,8},{1,9},{2,10},{3,11},{4,12},{5,13},{6,14},{7,15},{8,0},{9,1},... | collective-permute-start | bytes 786440 | tf_op jit(solution)/shard_map/ppermute | solution.py:20
  53.0 17.8 %collective-permute-start.6 = (f32[256,256]{0,1:T(8,128)S(1)}, f32[256,256]{0,1:T(8,128)S(1)}, u32[]{:S(2)}, u32[]{:S(2)}) collective-permute-start(f32[256,256]{0,1:T(8,128)S(1)} %pad_maximum_fusion.6), channel_id=1, source_target_pairs={{0,128},{32,160},{64,192},{96,224},{128,0},{160,32},{192,64},{224,... | collective-permute-start | bytes 786440 | tf_op jit(solution)/shard_map/ppermute | solution.py:20
  61.2 27.8 %collective-permute-start.5 = (f32[128,512]{1,0:T(8,128)}, f32[128,512]{1,0:T(8,128)S(1)}, u32[]{:S(2)}, u32[]{:S(2)}) collective-permute-start(f32[128,512]{1,0:T(8,128)} %collective-permute-done.2), channel_id=1, source_target_pairs={{0,384},{32,416},{64,448},{96,480},{128,256},{160,288},{192,320},{... | collective-permute-start | bytes 786440 | tf_op jit(solution)/shard_map/ppermute | solution.py:20
  67.5 48.1 %collective-permute-start.1 = (f32[136,512]{1,0:T(8,128)}, f32[136,512]{1,0:T(8,128)S(1)}, u32[]{:S(2)}, u32[]{:S(2)}) collective-permute-start(f32[136,512]{1,0:T(8,128)} %select_maximum_fusion.1), channel_id=1, source_target_pairs={{1,0},{2,1},{3,2},{4,3},{5,4},{6,5},{7,6},{8,7},{9,8},{10,9},{11,1... | collective-permute-start | bytes 835592 | tf_op jit(solution)/shard_map/ppermute | solution.py:26
  89.7 6.6 %copy-start.6 = (s32[1,2]{1,0:T(1,128)S(1)}, s32[1,2]{1,0:T(1,128)}, u32[]{:S(2)}) copy-start(s32[1,2]{1,0:T(1,128)} %param.10) | copy-start | bytes 28
  91.9 16.4 %collective-permute-start.9 = (f32[256,512]{1,0:T(8,128)S(1)}, f32[256,512]{1,0:T(8,128)S(1)}, u32[]{:S(2)}, u32[]{:S(2)}) collective-permute-start(f32[256,512]{1,0:T(8,128)S(1)} %convolution_add_fusion.1), channel_id=1, source_target_pairs={{0,16},{1,17},{2,18},{3,19},{4,20},{5,21},{6,22},{7,23},{8,24},{9,... | collective-permute-start | bytes 1572872 | tf_op jit(solution)/shard_map/ppermute | solution.py:20
  111.0 18.5 %all-to-all-start = ((f32[4,128,512]{2,1,0:T(8,128)}), f32[4,128,512]{2,1,0:T(8,128)S(1)}, u32[]{:S(2)}, u32[]{:S(2)}) async-start(f32[4,128,512]{2,1,0:T(8,128)} %bitcast.24), calls=%async_computation | async-start | bytes 2097152 | tf_op jit(solution)/shard_map/all_to_all | solution.py:304
  131.0 4.5 %collective-permute-start.10 = (f32[128,512]{1,0:T(8,128)S(1)}, f32[128,512]{1,0:T(8,128)S(1)}, u32[]{:S(2)}, u32[]{:S(2)}) collective-permute-start(f32[128,512]{1,0:T(8,128)S(1)} %fusion.4.image_in), channel_id=1, source_target_pairs={{0,1},{1,0},{2,3},{3,2},{4,5},{5,4},{6,7},{7,6},{8,9},{9,8},{10,11... | collective-permute-start | bytes 786440 | tf_op jit(solution)/shard_map/ppermute | solution.py:20
  205.2 11.1 %collective-permute-start.11 = (f32[128,1792]{1,0:T(8,128)S(1)}, f32[128,1792]{1,0:T(8,128)S(1)}, u32[]{:S(2)}, u32[]{:S(2)}) collective-permute-start(f32[128,1792]{1,0:T(8,128)S(1)} %bitcast.56), channel_id=1, source_target_pairs={{0,1},{1,0},{2,3},{3,2},{4,5},{5,4},{6,7},{7,6},{8,9},{9,8},{10,11... | collective-permute-start | bytes 2752520 | tf_op jit(solution)/shard_map/ppermute | solution.py:20

commit v4 on v3

--- a/solution.py
+++ b/solution.py
@@ -38,24 +38,30 @@
     return lax.dot_general(left, right, dims, precision=lax.Precision.HIGHEST)
 
 
-def dot_f32(left, right, left_dim, right_dim):
-    return lax.dot_general(
-        left,
-        right,
-        (((left_dim,), (right_dim,)), ((), ())),
-        precision=lax.Precision.HIGHEST,
-        preferred_element_type=jnp.float32,
-    )
-
-
 def three_parts(value):
-    high = value.astype(jnp.bfloat16).astype(jnp.float32)
-    middle = (value - high).astype(jnp.bfloat16).astype(jnp.float32)
-    return high, middle, (value - high) - middle
+    high = value.astype(jnp.bfloat16)
+    rest = value - high.astype(jnp.float32)
+    middle = rest.astype(jnp.bfloat16)
+    return high, middle, (rest - middle.astype(jnp.float32)).astype(jnp.bfloat16)
+
+
+def dot_parts(left, right, left_dim, right_dim):
+    def one_pass(first, second, third, fourth):
+        return lax.dot_general(
+            jnp.concatenate([first, second], axis=left_dim),
+            jnp.concatenate([third, fourth], axis=right_dim),
+            (((left_dim,), (right_dim,)), ((), ())),
+            preferred_element_type=jnp.float32,
+        )
+
+    high, middle, low = left if isinstance(left, tuple) else three_parts(left)
+    top, mid, last = right if isinstance(right, tuple) else three_parts(right)
+    small = one_pass(high, middle, mid, mid) + one_pass(high, low, last, top)
+    return one_pass(high, middle, top, top) + small
 
 
 def self_product(rows, first, count):
-    high, middle, low = three_parts(rows)
+    high, middle, low = (part.astype(jnp.float32) for part in three_parts(rows))
     right = jnp.concatenate([high, middle, high, low, high, middle], axis=0)
     left = jnp.concatenate([high, high, middle, high, low, middle], axis=0)[:, first:count]
     return lax.dot_general(
@@ -76,9 +82,9 @@
     for k in range(SLAB):
         pivot = 1.0 / block[k, k]
         for i in range(k + 1, SLAB):
+            for j in range(i, SLAB):
+                block[i, j] = block[i, j] - (block[k, i] * block[k, j]) * pivot
             ratio = block[k, i] * pivot
-            for j in range(i, SLAB):
-                block[i, j] = block[i, j] - ratio * block[k, j]
             for j in range(k + 1):
                 term = ratio * beside[k, j] if j < k else ratio
                 beside[i, j] = beside[i, j] - term if (i, j) in beside else -term
@@ -89,16 +95,31 @@
     return found
 
 
+def sum_of_rows(columns, rows, count):
+    left, right = 0.0, 0.0
+    for k in range(SLAB):
+        left = left + columns[k] * jnp.broadcast_to(rows[k : k + 1, :count], (SLAB, count))
+        right = right + columns[k] * jnp.broadcast_to(rows[k : k + 1, count:], (SLAB, count))
+    return jnp.concatenate([left, right], axis=1)
+
+
 def slab_rows(found, slab, count):
     row_at = lax.broadcasted_iota(jnp.int32, (SLAB, count), 0)
-    left, right = 0.0, 0.0
+    columns = []
     for j in range(SLAB):
         column = jnp.zeros((SLAB, count), jnp.float32)
         for i in range(j, SLAB):
             column = jnp.where(row_at == i, found[i, j], column)
-        left = left + column * jnp.broadcast_to(slab[j : j + 1, :count], (SLAB, count))
-        right = right + column * jnp.broadcast_to(slab[j : j + 1, count:], (SLAB, count))
-    return jnp.concatenate([left, right], axis=1)
+        columns.append(column)
+    return sum_of_rows(columns, slab, count)
+
+
+def after_slab(found, rows, following, at, count):
+    held = [jnp.broadcast_to(following[:, at + i : at + i + 1], (SLAB, count)) for i in range(SLAB)]
+    columns = []
+    for k in range(SLAB):
+        columns.append(sum(found[k, i] * held[i] for i in range(k + 1)))
+    return following - sum_of_rows(columns, rows, count)
 
 
 def factor_inverse(block):
@@ -106,13 +127,16 @@
     row_at = lax.broadcasted_iota(jnp.int32, block.shape, 0)
     col_at = lax.broadcasted_iota(jnp.int32, block.shape, 1)
     rest = jnp.concatenate([block, jnp.where(row_at == col_at, 1.0, 0.0)], axis=1)
+    slab, rest = rest[:SLAB], rest[SLAB:]
     done = []
     for at in range(0, count, SLAB):
-        slab = rest[:SLAB]
-        rows = slab_rows(slab_factor_inverse(slab, at), slab, count)
+        found = slab_factor_inverse(slab, at)
+        rows = slab_rows(found, slab, count)
         done.append(rows[:, count:])
         if at + SLAB < count:
-            rest = rest[SLAB:] - self_product(rows, at + SLAB, count)
+            slab = after_slab(found, rows, rest[:SLAB], at, count)
+        if at + 2 * SLAB < count:
+            rest = rest[SLAB:] - self_product(rows, at + 2 * SLAB, count)
     return jnp.concatenate(done, axis=0)
 
 
@@ -146,18 +170,20 @@
     left_over = total[...]
     for at in range(0, size, PIVOT):
         end = at + PIVOT
-        inverse = factor_inverse(gram[at:end, at:end])
-        cross_rows = dot_f32(inverse, cross[at:end, :], 1, 0)
-        image_cols = dot_f32(image[:, at:end], inverse, 1, 1)
+        inverse = three_parts(factor_inverse(gram[at:end, at:end]))
+        cross_rows = dot_parts(inverse, cross[at:end, :], 1, 0)
         left_over = left_over - jnp.sum(cross_rows * cross_rows, axis=0, keepdims=True)
-        new[...] -= dot_f32(image_cols, cross_rows, 1, 0)
+        cross_rows = three_parts(cross_rows)
+        image_cols = three_parts(dot_parts(image[:, at:end], inverse, 1, 1))
+        new[...] -= dot_parts(image_cols, cross_rows, 1, 0)
         if end < size:
-            gram_rows = dot_f32(inverse, gram[at:end, end:], 1, 0)
-            image[:, end:] -= dot_f32(image_cols, gram_rows, 1, 0)
-            cross[end:, :] -= dot_f32(gram_rows, cross_rows, 0, 0)
+            gram_rows = three_parts(dot_parts(inverse, gram[at:end, end:], 1, 0))
+            image[:, end:] -= dot_parts(image_cols, gram_rows, 1, 0)
+            cross[end:, :] -= dot_parts(gram_rows, cross_rows, 0, 0)
             for row in range(end, size, PIVOT):
-                part = gram_rows[:, row - end : row - end + PIVOT]
-                gram[row : row + PIVOT, row:] -= dot_f32(part, gram_rows[:, row - end :], 0, 0)
+                own = tuple(part[:, row - end : row - end + PIVOT] for part in gram_rows)
+                right = tuple(part[:, row - end :] for part in gram_rows)
+                gram[row : row + PIVOT, row:] -= dot_parts(own, right, 0, 0)
     norms[...] = jnp.sqrt(left_over / points_total)
 
 

time: 252 us -> 239 us (0.948)
  Pallas kernels: 34.5 us -> 21.4 us
    pallas_call x1, Pallas kernels: 34.5 us -> 21.4 us  [project_out(): pl.pallas_call(functools.partial(eliminate, points_total), in_specs=[pl.B...]
  transfers between devices with their start and end apart: 13 -> 13, of which waited for: 6 -> 6; matrix products, arithmetic and copies ran while one was open for 6% -> 7% of each run, Pallas kernels for 0% -> 0%
where the time goes in v4:
time: 239 us; the launch traced here: 238 us
  starting transfers between devices  72.1 us (30%)
  blocking collectives  67.5 us (28%)
  waiting for transfers between devices  55.9 us (23%)
  Pallas kernels  21.4 us (9%)
  matrix products  15.4 us (6%)
    ppermute x10, starting transfers between devices, swapped(): lax.ppermute(block, axis, [(i, i ^ bits) for i in range(lax.axis_size(axi...  61.2 us
    ppermute x10, waiting for transfers between devices, swapped(): lax.ppermute(block, axis, [(i, i ^ bits) for i in range(lax.axis_size(axi...  43.3 us
    all_to_all x3, blocking collectives, in_quads(): lax.all_to_all(tiles, 'row', 0, 0, axis_index_groups=groups, tiled=True)  33.8 us
    all_to_all x2, blocking collectives, within_plane(): lax.all_to_all(tiles, 'col', 0, 0, axis_index_groups=plane_groups(), tile...  33.8 us
    pallas_call x1, Pallas kernels, project_out(): pl.pallas_call(functools.partial(eliminate, points_total), in_specs=[pl.B...  21.4 us
    dot_general x19, matrix products, matmul_hi(): return lax.dot_general(left, right, dims, precision=lax.Precision.HIGHEST)  15.4 us
    all_to_all x1, waiting for transfers between devices, shards(): lax.all_to_all(given, 'col', 0, 0, axis_index_groups=quads, tiled=True)  12.6 us
    ppermute x2, starting transfers between devices, from_behind(): return lax.ppermute(block, axis, route)  6.94 us
  transfers between devices with their start and end apart: 13, of which 6 were waited for; matrix products, arithmetic and copies ran while one was open for 7% of the time, Pallas kernels for 0%

profile of v4, /device:TPU:1, one launch (start us, length us, event | category | flops | bytes accessed | tf_op | source)
XLA Modules:
  0.0 237.8 jit_solution(6795238339577639283)
XLA Ops:
  0.7 9.8 %collective-permute-start.2 = (f32[128,512]{1,0:T(8,128)}, f32[128,512]{1,0:T(8,128)}, u32[]{:S(2)}, u32[]{:S(2)}) collective-permute-start(f32[128,512]{1,0:T(8,128)} %own_in.1), channel_id=1, source_target_pairs={{0,128},{32,160},{64,192},{96,224},{128,0},{160,32},{192,64},{224,... | collective-permute-start | bytes 786440 | tf_op jit(solution)/shard_map/ppermute | solution.py:20
  10.4 8.8 %collective-permute-start.7 = (f32[128,512]{1,0:T(8,128)}, f32[128,512]{1,0:T(8,128)}, u32[]{:S(2)}, u32[]{:S(2)}) collective-permute-start(f32[128,512]{1,0:T(8,128)} %own_in.1), channel_id=1, source_target_pairs={{0,384},{32,416},{64,448},{96,480},{128,256},{160,288},{192,320},{... | collective-permute-start | bytes 786440 | tf_op jit(solution)/shard_map/ppermute | solution.py:20
  19.3 0.7 fusion.154
  20.0 1.3 fusion.37
  21.4 1.3 convolution_bitcast_fusion
  22.7 5.0 %collective-permute-start.4 = (f32[128,256]{0,1:T(8,128)S(1)}, f32[128,256]{0,1:T(8,128)S(1)}, u32[]{:S(2)}, u32[]{:S(2)}) collective-permute-start(f32[128,256]{0,1:T(8,128)S(1)} %convolution_bitcast_fusion), channel_id=1, source_target_pairs={{0,4},{1,5},{2,6},{3,7},{4,0},{5,1},{6,2},{7,3},{8,12},{9,13},{10,... | collective-permute-start | bytes 393224 | tf_op jit(solution)/shard_map/ppermute | solution.py:20
  27.7 3.7 %collective-permute-start.3 = (f32[128,256]{1,0:T(8,128)}, f32[128,256]{1,0:T(8,128)S(1)}, u32[]{:S(2)}, u32[]{:S(2)}) collective-permute-start(f32[128,256]{1,0:T(8,128)} %param.11), channel_id=1, source_target_pairs={{0,256},{32,288},{64,320},{96,352},{128,384},{160,416},{192,448},{... | collective-permute-start | bytes 393224 | tf_op jit(solution)/shard_map/ppermute | solution.py:20
  31.4 1.7 select_maximum_fusion.1
  33.1 3.7 %collective-permute-start = (f32[136,512]{1,0:T(8,128)}, f32[136,512]{1,0:T(8,128)S(1)}, u32[]{:S(2)}, u32[]{:S(2)}) collective-permute-start(f32[136,512]{1,0:T(8,128)} %select_maximum_fusion.1), channel_id=1, source_target_pairs={{0,1},{1,2},{2,3},{3,4},{4,5},{5,6},{6,7},{7,8},{8,9},{9,10},{10,1... | collective-permute-start | bytes 835592 | tf_op jit(solution)/shard_map/ppermute | solution.py:26
  36.9 0.4 fusion.33
  37.3 0.4 fusion.35
  37.7 0.4 fusion.31
  38.4 10.7 %collective-permute-done.3 = f32[128,256]{1,0:T(8,128)S(1)} collective-permute-done((f32[128,256]{1,0:T(8,128)}, f32[128,256]{1,0:T(8,128)S(1)}, u32[]{:S(2)}, u32[]{:S(2)}) %collective-permute-start.3) | collective-permute-done | bytes 131104 | tf_op jit(solution)/shard_map/ppermute | solution.py:20
  49.1 0.4 fusion.25
  49.5 3.1 %collective-permute-start.8 = (f32[256,256]{0,1:T(8,128)S(1)}, f32[256,256]{0,1:T(8,128)S(1)}, u32[]{:S(2)}, u32[]{:S(2)}) collective-permute-start(f32[256,256]{0,1:T(8,128)S(1)} %fusion.25), channel_id=1, source_target_pairs={{0,8},{1,9},{2,10},{3,11},{4,12},{5,13},{6,14},{7,15},{8,0},{9,1},... | collective-permute-start | bytes 786440 | tf_op jit(solution)/shard_map/ppermute | solution.py:20
  52.6 0.3 fusion.156
  53.0 8.3 %collective-permute-start.6 = (f32[256,256]{0,1:T(8,128)S(1)}, f32[256,256]{0,1:T(8,128)S(1)}, u32[]{:S(2)}, u32[]{:S(2)}) collective-permute-start(f32[256,256]{0,1:T(8,128)S(1)} %pad_maximum_fusion.6), channel_id=1, source_target_pairs={{0,128},{32,160},{64,192},{96,224},{128,0},{160,32},{192,64},{224,... | collective-permute-start | bytes 786440 | tf_op jit(solution)/shard_map/ppermute | solution.py:20
  61.2 5.8 %collective-permute-start.5 = (f32[128,512]{1,0:T(8,128)}, f32[128,512]{1,0:T(8,128)S(1)}, u32[]{:S(2)}, u32[]{:S(2)}) collective-permute-start(f32[128,512]{1,0:T(8,128)} %collective-permute-done.2), channel_id=1, source_target_pairs={{0,384},{32,416},{64,448},{96,480},{128,256},{160,288},{192,320},{... | collective-permute-start | bytes 786440 | tf_op jit(solution)/shard_map/ppermute | solution.py:20
  67.0 0.4 fusion.29
  67.5 3.2 %collective-permute-start.1 = (f32[136,512]{1,0:T(8,128)}, f32[136,512]{1,0:T(8,128)S(1)}, u32[]{:S(2)}, u32[]{:S(2)}) collective-permute-start(f32[136,512]{1,0:T(8,128)} %select_maximum_fusion.1), channel_id=1, source_target_pairs={{1,0},{2,1},{3,2},{4,3},{5,4},{6,5},{7,6},{8,7},{9,8},{10,9},{11,1... | collective-permute-start | bytes 835592 | tf_op jit(solution)/shard_map/ppermute | solution.py:26
  70.7 18.3 %collective-permute-done.5 = f32[128,512]{1,0:T(8,128)S(1)} collective-permute-done((f32[128,512]{1,0:T(8,128)}, f32[128,512]{1,0:T(8,128)S(1)}, u32[]{:S(2)}, u32[]{:S(2)}) %collective-permute-start.5) | collective-permute-done | bytes 262176 | tf_op jit(solution)/shard_map/ppermute | solution.py:20
  89.0 0.6 convolution_multiply_fusion
  89.7 0.6 fusion.157
  90.3 1.6 convolution_add_fusion.1
  91.9 4.3 %collective-permute-start.9 = (f32[256,512]{1,0:T(8,128)S(1)}, f32[256,512]{1,0:T(8,128)S(1)}, u32[]{:S(2)}, u32[]{:S(2)}) collective-permute-start(f32[256,512]{1,0:T(8,128)S(1)} %convolution_add_fusion.1), channel_id=1, source_target_pairs={{0,16},{1,17},{2,18},{3,19},{4,20},{5,21},{6,22},{7,23},{8,24},{9,... | collective-permute-start | bytes 1572872 | tf_op jit(solution)/shard_map/ppermute | solution.py:20
  96.3 0.7 fusion.96
  97.0 0.1 broadcast_select_fusion.3
  97.2 11.1 %collective-permute-done.9 = f32[256,512]{1,0:T(8,128)S(1)} collective-permute-done((f32[256,512]{1,0:T(8,128)S(1)}, f32[256,512]{1,0:T(8,128)S(1)}, u32[]{:S(2)}, u32[]{:S(2)}) %collective-permute-start.9) | collective-permute-done | bytes 524320 | tf_op jit(solution)/shard_map/ppermute | solution.py:20
  108.3 0.6 convolution_add_fusion
  109.0 2.0 fusion.8
  111.0 4.0 %all-to-all-start = ((f32[4,128,512]{2,1,0:T(8,128)}), f32[4,128,512]{2,1,0:T(8,128)S(1)}, u32[]{:S(2)}, u32[]{:S(2)}) async-start(f32[4,128,512]{2,1,0:T(8,128)} %bitcast.24), calls=%async_computation | async-start | bytes 2097152 | tf_op jit(solution)/shard_map/all_to_all | solution.py:330
  114.9 0.6 fusion.155
  115.6 1.4 fusion.2
  116.9 12.6 %all-to-all-done = f32[4,128,512]{2,1,0:T(8,128)S(1)} async-done(((f32[4,128,512]{2,1,0:T(8,128)}), f32[4,128,512]{2,1,0:T(8,128)S(1)}, u32[]{:S(2)}, u32[]{:S(2)}) %all-to-all-start) | async-done | bytes 1048608 | tf_op jit(solution)/shard_map/all_to_all | solution.py:330
  129.6 1.4 fusion.4.image_in
  131.0 3.4 %collective-permute-start.10 = (f32[128,512]{1,0:T(8,128)S(1)}, f32[128,512]{1,0:T(8,128)S(1)}, u32[]{:S(2)}, u32[]{:S(2)}) collective-permute-start(f32[128,512]{1,0:T(8,128)S(1)} %fusion.4.image_in), channel_id=1, source_target_pairs={{0,1},{1,0},{2,3},{3,2},{4,5},{5,4},{6,7},{7,6},{8,9},{9,8},{10,11... | collective-permute-start | bytes 786440 | tf_op jit(solution)/shard_map/ppermute | solution.py:20
  134.5 1.1 collective-permute-done.10
  135.5 0.5 fusion.7
  136.0 0.4 fusion.58
  136.4 0.6 fusion.6
  137.3 18.9 %all_to_all.30 = f32[16,8,1792]{2,1,0:T(8,128)S(1)} all-to-all(f32[16,8,1792]{2,1,0:T(8,128)S(1)} %fusion.5), channel_id=1, replica_groups={{0,2,4,6,8,10,12,14,16,18,20,22,24,26,28,30},{1,3,5,7,9,11,13,15,17,19,..., dimensions={0} | all-to-all | bytes 1835008 | tf_op jit(solution)/shard_map/all_to_all | solution.py:217
  156.4 8.4 %all_to_all.31 = f32[4,8,448]{2,1,0:T(8,128)S(1)} all-to-all(f32[4,8,448]{2,1,0:T(8,128)S(1)} %copy.20), channel_id=1, replica_groups={{0,32,64,96},{128,160,192,224},{256,288,320,352},{384,416,448,480},{1,3..., dimensions={0} | all-to-all | bytes 114688 | tf_op jit(solution)/shard_map/all_to_all | solution.py:221
  164.8 18.4 %all_to_all.32 = f32[4,8,448]{2,1,0:T(8,128)S(1)} all-to-all(f32[4,8,448]{2,1,0:T(8,128)S(1)} %broadcast_in_dim.11), channel_id=1, replica_groups={{0,128,256,384},{32,160,288,416},{64,192,320,448},{96,224,352,480},{1,1..., dimensions={0} | all-to-all | bytes 114688 | tf_op jit(solution)/shard_map/all_to_all | solution.py:221
  183.2 7.0 %all_to_all.33 = f32[4,8,448]{2,1,0:T(8,128)S(1)} all-to-all(f32[4,8,448]{2,1,0:T(8,128)S(1)} %broadcast_in_dim.12), channel_id=1, replica_groups={{0,32,64,96},{128,160,192,224},{256,288,320,352},{384,416,448,480},{1,3..., dimensions={0} | all-to-all | bytes 114688 | tf_op jit(solution)/shard_map/all_to_all | solution.py:221
  190.4 14.8 %all_to_all.34 = f32[16,8,1792]{2,1,0:T(8,128)S(1)} all-to-all(f32[16,8,1792]{2,1,0:T(8,128)S(1)} %broadcast_in_dim.27), channel_id=1, replica_groups={{0,2,4,6,8,10,12,14,16,18,20,22,24,26,28,30},{1,3,5,7,9,11,13,15,17,19,..., dimensions={0} | all-to-all | bytes 1835008 | tf_op jit(solution)/shard_map/all_to_all | solution.py:217
  205.2 9.0 %collective-permute-start.11 = (f32[128,1792]{1,0:T(8,128)S(1)}, f32[128,1792]{1,0:T(8,128)S(1)}, u32[]{:S(2)}, u32[]{:S(2)}) collective-permute-start(f32[128,1792]{1,0:T(8,128)S(1)} %bitcast.56), channel_id=1, source_target_pairs={{0,1},{1,0},{2,3},{3,2},{4,5},{5,4},{6,7},{7,6},{8,9},{9,8},{10,11... | collective-permute-start | bytes 2752520 | tf_op jit(solution)/shard_map/ppermute | solution.py:20
  214.3 2.1 collective-permute-done.11.theirs
  216.4 21.4 %eliminate.1 = (f32[128,512]{1,0:T(8,128)}, f32[1,512]{1,0:T(1,128)}) custom-call(s32[1]{0:T(128)} %bitcast.core, f32[128,1792]{1,0:T(8,128)S(1)} %bitcast.57, f32[128,1792]{1,0:T(8,128)S(1)} %collective-permute-done.11.theirs, f32[128,512]{1,0:T(8,128)S(1)} %fusion.4.image_in, f32[128,512]{1,0:T(8,128)S(1)} %copy-done), custom_call_target="tpu_custom_call" | custom-call | tf_op jit(solution)/shard_map/eliminate/pallas_call | solution.py:193
  (49 shorter events, 1.1 us)
Async XLA Ops:
  0.6 36.2 %copy-start.1 = (f32[256,1280]{1,0:T(8,128)S(1)}, f32[256,1280]{1,0:T(8,128)}, u32[]{:S(2)}) copy-start(f32[256,1280]{1,0:T(8,128)} %param.14) | copy-start | bytes 3932164
  0.6 36.2 %copy-start.5 = (f32[1,1280]{1,0:T(1,128)S(1)}, f32[1,1280]{1,0:T(1,128)}, u32[]{:S(2)}) copy-start(f32[1,1280]{1,0:T(1,128)} %param.13) | copy-start | bytes 15364
  0.7 48.4 %collective-permute-start.2 = (f32[128,512]{1,0:T(8,128)}, f32[128,512]{1,0:T(8,128)}, u32[]{:S(2)}, u32[]{:S(2)}) collective-permute-start(f32[128,512]{1,0:T(8,128)} %own_in.1), channel_id=1, source_target_pairs={{0,128},{32,160},{64,192},{96,224},{128,0},{160,32},{192,64},{224,... | collective-permute-start | bytes 786440 | tf_op jit(solution)/shard_map/ppermute | solution.py:20
  10.4 57.0 %collective-permute-start.7 = (f32[128,512]{1,0:T(8,128)}, f32[128,512]{1,0:T(8,128)}, u32[]{:S(2)}, u32[]{:S(2)}) collective-permute-start(f32[128,512]{1,0:T(8,128)} %own_in.1), channel_id=1, source_target_pairs={{0,384},{32,416},{64,448},{96,480},{128,256},{160,288},{192,320},{... | collective-permute-start | bytes 786440 | tf_op jit(solution)/shard_map/ppermute | solution.py:20
  21.4 16.7 %copy-start.3 = (f32[128,256]{1,0:T(8,128)S(1)}, f32[128,256]{1,0:T(8,128)}, u32[]{:S(2)}) copy-start(f32[128,256]{1,0:T(8,128)} %param.11) | copy-start | bytes 393220
  22.7 15.4 %copy-start.2 = (f32[128,256]{1,0:T(8,128)S(1)}, f32[128,256]{1,0:T(8,128)}, u32[]{:S(2)}) copy-start(f32[128,256]{1,0:T(8,128)} %param.12) | copy-start | bytes 393220
  22.7 15.6 %collective-permute-start.4 = (f32[128,256]{0,1:T(8,128)S(1)}, f32[128,256]{0,1:T(8,128)S(1)}, u32[]{:S(2)}, u32[]{:S(2)}) collective-permute-start(f32[128,256]{0,1:T(8,128)S(1)} %convolution_bitcast_fusion), channel_id=1, source_target_pairs={{0,4},{1,5},{2,6},{3,7},{4,0},{5,1},{6,2},{7,3},{8,12},{9,13},{10,... | collective-permute-start | bytes 393224 | tf_op jit(solution)/shard_map/ppermute | solution.py:20
  27.7 21.4 %collective-permute-start.3 = (f32[128,256]{1,0:T(8,128)}, f32[128,256]{1,0:T(8,128)S(1)}, u32[]{:S(2)}, u32[]{:S(2)}) collective-permute-start(f32[128,256]{1,0:T(8,128)} %param.11), channel_id=1, source_target_pairs={{0,256},{32,288},{64,320},{96,352},{128,384},{160,416},{192,448},{... | collective-permute-start | bytes 393224 | tf_op jit(solution)/shard_map/ppermute | solution.py:20
  33.1 82.4 %collective-permute-start = (f32[136,512]{1,0:T(8,128)}, f32[136,512]{1,0:T(8,128)S(1)}, u32[]{:S(2)}, u32[]{:S(2)}) collective-permute-start(f32[136,512]{1,0:T(8,128)} %select_maximum_fusion.1), channel_id=1, source_target_pairs={{0,1},{1,2},{2,3},{3,4},{4,5},{5,6},{6,7},{7,8},{8,9},{9,10},{10,1... | collective-permute-start | bytes 835592 | tf_op jit(solution)/shard_map/ppermute | solution.py:26
  38.1 28.9 %copy-start.4 = (f32[3,128]{1,0:T(4,128)S(1)}, f32[3,128]{1,0:T(4,128)}, u32[]{:S(2)}) copy-start(f32[3,128]{1,0:T(4,128)} %param.8) | copy-start | bytes 4612
  38.2 50.8 %copy-start = (f32[128,512]{1,0:T(8,128)S(1)}, f32[128,512]{1,0:T(8,128)}, u32[]{:S(2)}) copy-start(f32[128,512]{1,0:T(8,128)} %own_in.1) | copy-start | bytes 786436
  49.5 21.2 %collective-permute-start.8 = (f32[256,256]{0,1:T(8,128)S(1)}, f32[256,256]{0,1:T(8,128)S(1)}, u32[]{:S(2)}, u32[]{:S(2)}) collective-permute-start(f32[256,256]{0,1:T(8,128)S(1)} %fusion.25), channel_id=1, source_target_pairs={{0,8},{1,9},{2,10},{3,11},{4,12},{5,13},{6,14},{7,15},{8,0},{9,1},... | collective-permute-start | bytes 786440 | tf_op jit(solution)/shard_map/ppermute | solution.py:20
  53.0 17.8 %collective-permute-start.6 = (f32[256,256]{0,1:T(8,128)S(1)}, f32[256,256]{0,1:T(8,128)S(1)}, u32[]{:S(2)}, u32[]{:S(2)}) collective-permute-start(f32[256,256]{0,1:T(8,128)S(1)} %pad_maximum_fusion.6), channel_id=1, source_target_pairs={{0,128},{32,160},{64,192},{96,224},{128,0},{160,32},{192,64},{224,... | collective-permute-start | bytes 786440 | tf_op jit(solution)/shard_map/ppermute | solution.py:20
  61.2 27.8 %collective-permute-start.5 = (f32[128,512]{1,0:T(8,128)}, f32[128,512]{1,0:T(8,128)S(1)}, u32[]{:S(2)}, u32[]{:S(2)}) collective-permute-start(f32[128,512]{1,0:T(8,128)} %collective-permute-done.2), channel_id=1, source_target_pairs={{0,384},{32,416},{64,448},{96,480},{128,256},{160,288},{192,320},{... | collective-permute-start | bytes 786440 | tf_op jit(solution)/shard_map/ppermute | solution.py:20
  67.5 48.1 %collective-permute-start.1 = (f32[136,512]{1,0:T(8,128)}, f32[136,512]{1,0:T(8,128)S(1)}, u32[]{:S(2)}, u32[]{:S(2)}) collective-permute-start(f32[136,512]{1,0:T(8,128)} %select_maximum_fusion.1), channel_id=1, source_target_pairs={{1,0},{2,1},{3,2},{4,3},{5,4},{6,5},{7,6},{8,7},{9,8},{10,9},{11,1... | collective-permute-start | bytes 835592 | tf_op jit(solution)/shard_map/ppermute | solution.py:26
  89.7 6.6 %copy-start.6 = (s32[1,2]{1,0:T(1,128)S(1)}, s32[1,2]{1,0:T(1,128)}, u32[]{:S(2)}) copy-start(s32[1,2]{1,0:T(1,128)} %param.10) | copy-start | bytes 28
  91.9 16.4 %collective-permute-start.9 = (f32[256,512]{1,0:T(8,128)S(1)}, f32[256,512]{1,0:T(8,128)S(1)}, u32[]{:S(2)}, u32[]{:S(2)}) collective-permute-start(f32[256,512]{1,0:T(8,128)S(1)} %convolution_add_fusion.1), channel_id=1, source_target_pairs={{0,16},{1,17},{2,18},{3,19},{4,20},{5,21},{6,22},{7,23},{8,24},{9,... | collective-permute-start | bytes 1572872 | tf_op jit(solution)/shard_map/ppermute | solution.py:20
  111.0 18.5 %all-to-all-start = ((f32[4,128,512]{2,1,0:T(8,128)}), f32[4,128,512]{2,1,0:T(8,128)S(1)}, u32[]{:S(2)}, u32[]{:S(2)}) async-start(f32[4,128,512]{2,1,0:T(8,128)} %bitcast.24), calls=%async_computation | async-start | bytes 2097152 | tf_op jit(solution)/shard_map/all_to_all | solution.py:330
  131.0 4.5 %collective-permute-start.10 = (f32[128,512]{1,0:T(8,128)S(1)}, f32[128,512]{1,0:T(8,128)S(1)}, u32[]{:S(2)}, u32[]{:S(2)}) collective-permute-start(f32[128,512]{1,0:T(8,128)S(1)} %fusion.4.image_in), channel_id=1, source_target_pairs={{0,1},{1,0},{2,3},{3,2},{4,5},{5,4},{6,7},{7,6},{8,9},{9,8},{10,11... | collective-permute-start | bytes 786440 | tf_op jit(solution)/shard_map/ppermute | solution.py:20
  205.2 11.1 %collective-permute-start.11 = (f32[128,1792]{1,0:T(8,128)S(1)}, f32[128,1792]{1,0:T(8,128)S(1)}, u32[]{:S(2)}, u32[]{:S(2)}) collective-permute-start(f32[128,1792]{1,0:T(8,128)S(1)} %bitcast.56), channel_id=1, source_target_pairs={{0,1},{1,0},{2,3},{3,2},{4,5},{5,4},{6,7},{7,6},{8,9},{9,8},{10,11... | collective-permute-start | bytes 2752520 | tf_op jit(solution)/shard_map/ppermute | solution.py:20

commit v5 on v4

--- a/solution.py
+++ b/solution.py
@@ -157,7 +157,8 @@
         cross[256:384, :] = second[:, 640:1152]
         cross[384:512, :] = second[:, 1152:1664]
         for piece in range(4):
-            total[:, piece * 128 : piece * 128 + 128] = first[piece : piece + 1, 1664:1792]
+            pair = [first[row : row + 1, 0:64] for row in (120 + 2 * piece, 121 + 2 * piece)]
+            total[:, piece * 128 : piece * 128 + 128] = jnp.concatenate(pair, axis=1)
 
     @pl.when(core[0] == 0)
     def _():
@@ -249,6 +250,7 @@
     owns = jnp.concatenate([own, pair_own], axis=0)
     blocks = [images[:, k * 128 : k * 128 + 128] for k in range(4)]
     wide = matmul_hi(jnp.where(odd, blocks[1], blocks[0]), images, 0, 0)
+    wide = wide.at[120:, :64].set(own_squares.reshape(8, 64))
     narrow = matmul_hi(jnp.where(odd, blocks[2], blocks[3]), images[:, 256:], 0, 0)
     gram_part = jnp.where(
         odd,
@@ -256,8 +258,7 @@
         jnp.concatenate([wide, narrow[:, 128:]], axis=1),
     )
     cross_part = matmul_hi(jnp.where(odd, images[:, 256:], images[:, :256]), owns, 0, 0)
-    squares = jnp.pad(own_squares.reshape(4, 128), ((0, 124), (0, 0)))
-    return jnp.concatenate([gram_part, cross_part[:128], cross_part[128:], squares], axis=1)
+    return jnp.concatenate([gram_part, cross_part[:128], cross_part[128:]], axis=1)
 
 
 def shards(
@@ -293,7 +294,6 @@
     from_last = swapped(matmul_hi(expand, couples[4]), "col", 4)
 
     by_one, compress_two, from_last = lax.optimization_barrier((by_one, compress_two, from_last))
-    by_two = swapped(by_one, "row", 12)
     low_map = jnp.concatenate(
         [gains[0] * compress.T, matmul_hi(couples[0], compress_two, 1, 1)], axis=1
     )
@@ -301,9 +301,8 @@
     from_both = swapped(
         matmul_hi(jnp.concatenate([expand_own, from_last], axis=0), couples[3]), "col", 8
     )
-    by_two, low_map_one, by_three, from_both = lax.optimization_barrier(
-        (by_two, low_map_one, by_three, from_both)
-    )
+    by_two = swapped(by_one, "row", 12)
+    by_two, low_map_one, by_three = lax.optimization_barrier((by_two, low_map_one, by_three))
 
     maps = [expand_own * gains[3][:, 0], from_last * gains[3][:, 0]]
     maps += [from_both[:points], from_both[points:]]

time: 239 us -> 234 us (0.979)
  waiting for transfers between devices: 55.9 us -> 52.8 us
    ppermute x10, waiting for transfers between devices: 43.3 us -> 40.2 us  [swapped(): lax.ppermute(block, axis, [(i, i ^ bits) for i in range(lax.axis_size(axi...]
  transfers between devices with their start and end apart: 13 -> 13, of which waited for: 6 -> 7; matrix products, arithmetic and copies ran while one was open for 7% -> 6% of each run, Pallas kernels for 0% -> 0%
where the time goes in v5:
time: 234 us; the launch traced here: 233 us
  starting transfers between devices  72.4 us (31%)
  blocking collectives  66.1 us (28%)
  waiting for transfers between devices  52.8 us (23%)
  Pallas kernels  21.4 us (9%)
  matrix products  15.1 us (6%)
  local copies, waits for them, and re-layouts  2.42 us (1%)
    ppermute x10, starting transfers between devices, swapped(): lax.ppermute(block, axis, [(i, i ^ bits) for i in range(lax.axis_size(axi...  61.5 us
    ppermute x10, waiting for transfers between devices, swapped(): lax.ppermute(block, axis, [(i, i ^ bits) for i in range(lax.axis_size(axi...  40.2 us
    all_to_all x3, blocking collectives, in_quads(): lax.all_to_all(tiles, 'row', 0, 0, axis_index_groups=groups, tiled=True)  33.7 us
    all_to_all x2, blocking collectives, within_plane(): lax.all_to_all(tiles, 'col', 0, 0, axis_index_groups=plane_groups(), tile...  32.5 us
    pallas_call x1, Pallas kernels, project_out(): pl.pallas_call(functools.partial(eliminate, points_total), in_specs=[pl.B...  21.4 us
    dot_general x19, matrix products, matmul_hi(): return lax.dot_general(left, right, dims, precision=lax.Precision.HIGHEST)  15.1 us
    all_to_all x1, waiting for transfers between devices, shards(): lax.all_to_all(given, 'col', 0, 0, axis_index_groups=quads, tiled=True)  12.6 us
    ppermute x2, starting transfers between devices, from_behind(): return lax.ppermute(block, axis, route)  5.77 us
  transfers between devices with their start and end apart: 13, of which 7 were waited for; matrix products, arithmetic and copies ran while one was open for 6% of the time, Pallas kernels for 0%

profile of v5, /device:TPU:1, one launch (start us, length us, event | category | flops | bytes accessed | tf_op | source)
XLA Modules:
  0.0 233.1 jit_solution(6372999408929812320)
XLA Ops:
  0.6 9.8 %collective-permute-start.2 = (f32[128,512]{1,0:T(8,128)}, f32[128,512]{1,0:T(8,128)S(1)}, u32[]{:S(2)}, u32[]{:S(2)}) collective-permute-start(f32[128,512]{1,0:T(8,128)} %own_in.1), channel_id=1, source_target_pairs={{0,128},{32,160},{64,192},{96,224},{128,0},{160,32},{192,64},{224,... | collective-permute-start | bytes 786440 | tf_op jit(solution)/shard_map/ppermute | solution.py:20
  10.4 8.8 %collective-permute-start.8 = (f32[128,512]{1,0:T(8,128)}, f32[128,512]{1,0:T(8,128)S(1)}, u32[]{:S(2)}, u32[]{:S(2)}) collective-permute-start(f32[128,512]{1,0:T(8,128)} %own_in.1), channel_id=1, source_target_pairs={{0,384},{32,416},{64,448},{96,480},{128,256},{160,288},{192,320},{... | collective-permute-start | bytes 786440 | tf_op jit(solution)/shard_map/ppermute | solution.py:20
  19.3 0.7 fusion.153
  20.0 1.3 fusion.36
  21.4 1.3 convolution_bitcast_fusion
  22.7 5.0 %collective-permute-start.4 = (f32[128,256]{0,1:T(8,128)S(1)}, f32[128,256]{0,1:T(8,128)S(1)}, u32[]{:S(2)}, u32[]{:S(2)}) collective-permute-start(f32[128,256]{0,1:T(8,128)S(1)} %convolution_bitcast_fusion), channel_id=1, source_target_pairs={{0,4},{1,5},{2,6},{3,7},{4,0},{5,1},{6,2},{7,3},{8,12},{9,13},{10,... | collective-permute-start | bytes 393224 | tf_op jit(solution)/shard_map/ppermute | solution.py:20
  27.6 3.7 %collective-permute-start.3 = (f32[128,256]{1,0:T(8,128)}, f32[128,256]{1,0:T(8,128)S(1)}, u32[]{:S(2)}, u32[]{:S(2)}) collective-permute-start(f32[128,256]{1,0:T(8,128)} %param.13), channel_id=1, source_target_pairs={{0,256},{32,288},{64,320},{96,352},{128,384},{160,416},{192,448},{... | collective-permute-start | bytes 393224 | tf_op jit(solution)/shard_map/ppermute | solution.py:20
  31.4 1.0 select_maximum_fusion
  32.4 3.8 %collective-permute-start = (f32[136,512]{1,0:T(8,128)S(1)}, f32[136,512]{1,0:T(8,128)S(1)}, u32[]{:S(2)}, u32[]{:S(2)}) collective-permute-start(f32[136,512]{1,0:T(8,128)S(1)} %select_maximum_fusion), channel_id=1, source_target_pairs={{0,1},{1,2},{2,3},{3,4},{4,5},{5,6},{6,7},{7,8},{8,9},{9,10},{10,1... | collective-permute-start | bytes 835592 | tf_op jit(solution)/shard_map/ppermute | solution.py:26
  36.2 0.4 fusion.32
  36.6 0.4 fusion.30
  37.1 0.4 fusion.28
  37.5 0.4 fusion.34
  38.0 1.9 collective-permute-start.1
  40.0 9.1 %collective-permute-done.3 = f32[128,256]{1,0:T(8,128)S(1)} collective-permute-done((f32[128,256]{1,0:T(8,128)}, f32[128,256]{1,0:T(8,128)S(1)}, u32[]{:S(2)}, u32[]{:S(2)}) %collective-permute-start.3) | collective-permute-done | bytes 131104 | tf_op jit(solution)/shard_map/ppermute | solution.py:20
  49.1 0.3 fusion.155
  49.4 8.3 %collective-permute-start.7 = (f32[256,256]{0,1:T(8,128)S(1)}, f32[256,256]{0,1:T(8,128)S(1)}, u32[]{:S(2)}, u32[]{:S(2)}) collective-permute-start(f32[256,256]{0,1:T(8,128)S(1)} %pad_maximum_fusion.6), channel_id=1, source_target_pairs={{0,128},{32,160},{64,192},{96,224},{128,0},{160,32},{192,64},{224,... | collective-permute-start | bytes 786440 | tf_op jit(solution)/shard_map/ppermute | solution.py:20
  57.7 5.8 %collective-permute-start.6 = (f32[128,512]{1,0:T(8,128)S(1)}, f32[128,512]{1,0:T(8,128)S(1)}, u32[]{:S(2)}, u32[]{:S(2)}) collective-permute-start(f32[128,512]{1,0:T(8,128)S(1)} %collective-permute-done.2), channel_id=1, source_target_pairs={{0,384},{32,416},{64,448},{96,480},{128,256},{160,288},{192,320},{... | collective-permute-start | bytes 786440 | tf_op jit(solution)/shard_map/ppermute | solution.py:20
  63.6 1.1 fusion.24
  64.7 3.1 %collective-permute-start.5 = (f32[256,256]{0,1:T(8,128)}, f32[256,256]{0,1:T(8,128)S(1)}, u32[]{:S(2)}, u32[]{:S(2)}) collective-permute-start(f32[256,256]{0,1:T(8,128)} %fusion.24), channel_id=1, source_target_pairs={{0,8},{1,9},{2,10},{3,11},{4,12},{5,13},{6,14},{7,15},{8,0},{9,1},... | collective-permute-start | bytes 786440 | tf_op jit(solution)/shard_map/ppermute | solution.py:20
  68.0 17.1 %collective-permute-done.6 = f32[128,512]{1,0:T(8,128)S(1)} collective-permute-done((f32[128,512]{1,0:T(8,128)S(1)}, f32[128,512]{1,0:T(8,128)S(1)}, u32[]{:S(2)}, u32[]{:S(2)}) %collective-permute-start.6) | collective-permute-done | bytes 262176 | tf_op jit(solution)/shard_map/ppermute | solution.py:20
  85.1 0.6 convolution_multiply_fusion
  85.8 0.6 fusion.156
  86.4 0.6 convolution_add_fusion.1
  87.0 4.7 %collective-permute-start.9 = (f32[256,512]{1,0:T(8,128)S(1)}, f32[256,512]{1,0:T(8,128)S(1)}, u32[]{:S(2)}, u32[]{:S(2)}) collective-permute-start(f32[256,512]{1,0:T(8,128)S(1)} %convolution_add_fusion.1), channel_id=1, source_target_pairs={{0,16},{1,17},{2,18},{3,19},{4,20},{5,21},{6,22},{7,23},{8,24},{9,... | collective-permute-start | bytes 1572872 | tf_op jit(solution)/shard_map/ppermute | solution.py:20
  91.7 0.7 fusion.95
  92.6 10.8 %collective-permute-done.9 = f32[256,512]{1,0:T(8,128)S(1)} collective-permute-done((f32[256,512]{1,0:T(8,128)S(1)}, f32[256,512]{1,0:T(8,128)S(1)}, u32[]{:S(2)}, u32[]{:S(2)}) %collective-permute-start.9) | collective-permute-done | bytes 524320 | tf_op jit(solution)/shard_map/ppermute | solution.py:20
  103.4 0.6 convolution_add_fusion
  104.1 2.0 fusion.7
  106.1 5.2 %all-to-all-start = ((f32[4,128,512]{2,1,0:T(8,128)}), f32[4,128,512]{2,1,0:T(8,128)S(1)}, u32[]{:S(2)}, u32[]{:S(2)}) async-start(f32[4,128,512]{2,1,0:T(8,128)} %bitcast.24), calls=%async_computation | async-start | bytes 2097152 | tf_op jit(solution)/shard_map/all_to_all | solution.py:329
  111.3 0.6 fusion.154
  111.9 1.4 fusion.2
  113.2 12.6 %all-to-all-done = f32[4,128,512]{2,1,0:T(8,128)S(1)} async-done(((f32[4,128,512]{2,1,0:T(8,128)}), f32[4,128,512]{2,1,0:T(8,128)S(1)}, u32[]{:S(2)}, u32[]{:S(2)}) %all-to-all-start) | async-done | bytes 1048608 | tf_op jit(solution)/shard_map/all_to_all | solution.py:329
  126.0 1.4 fusion.4.image_in
  127.4 3.4 %collective-permute-start.10 = (f32[128,512]{1,0:T(8,128)S(1)}, f32[128,512]{1,0:T(8,128)S(1)}, u32[]{:S(2)}, u32[]{:S(2)}) collective-permute-start(f32[128,512]{1,0:T(8,128)S(1)} %fusion.4.image_in), channel_id=1, source_target_pairs={{0,1},{1,0},{2,3},{3,2},{4,5},{5,4},{6,7},{7,6},{8,9},{9,8},{10,11... | collective-permute-start | bytes 786440 | tf_op jit(solution)/shard_map/ppermute | solution.py:20
  130.9 1.0 collective-permute-done.10
  131.9 0.5 fusion.6
  132.3 0.4 scatter.4
  132.8 0.4 fusion.57
  133.2 0.6 fusion.5
  134.0 18.3 %all_to_all.30 = f32[16,8,1664]{2,1,0:T(8,128)S(1)} all-to-all(f32[16,8,1664]{2,1,0:T(8,128)S(1)} %maximum_bitcast_fusion), channel_id=1, replica_groups={{0,2,4,6,8,10,12,14,16,18,20,22,24,26,28,30},{1,3,5,7,9,11,13,15,17,19,..., dimensions={0} | all-to-all | bytes 1703936 | tf_op jit(solution)/shard_map/all_to_all | solution.py:218
  152.5 8.3 %all_to_all.31 = f32[4,8,416]{2,1,0:T(8,128)S(1)} all-to-all(f32[4,8,416]{2,1,0:T(8,128)S(1)} %copy.20), channel_id=1, replica_groups={{0,32,64,96},{128,160,192,224},{256,288,320,352},{384,416,448,480},{1,3..., dimensions={0} | all-to-all | bytes 106496 | tf_op jit(solution)/shard_map/all_to_all | solution.py:222
  160.8 18.4 %all_to_all.32 = f32[4,8,416]{2,1,0:T(8,128)S(1)} all-to-all(f32[4,8,416]{2,1,0:T(8,128)S(1)} %broadcast_in_dim.11), channel_id=1, replica_groups={{0,128,256,384},{32,160,288,416},{64,192,320,448},{96,224,352,480},{1,1..., dimensions={0} | all-to-all | bytes 106496 | tf_op jit(solution)/shard_map/all_to_all | solution.py:222
  179.3 7.0 %all_to_all.33 = f32[4,8,416]{2,1,0:T(8,128)S(1)} all-to-all(f32[4,8,416]{2,1,0:T(8,128)S(1)} %broadcast_in_dim.12), channel_id=1, replica_groups={{0,32,64,96},{128,160,192,224},{256,288,320,352},{384,416,448,480},{1,3..., dimensions={0} | all-to-all | bytes 106496 | tf_op jit(solution)/shard_map/all_to_all | solution.py:222
  186.4 14.2 %all_to_all.34 = f32[16,8,1664]{2,1,0:T(8,128)S(1)} all-to-all(f32[16,8,1664]{2,1,0:T(8,128)S(1)} %broadcast_in_dim.27), channel_id=1, replica_groups={{0,2,4,6,8,10,12,14,16,18,20,22,24,26,28,30},{1,3,5,7,9,11,13,15,17,19,..., dimensions={0} | all-to-all | bytes 1703936 | tf_op jit(solution)/shard_map/all_to_all | solution.py:218
  200.6 9.0 %collective-permute-start.11 = (f32[128,1664]{1,0:T(8,128)S(1)}, f32[128,1664]{1,0:T(8,128)S(1)}, u32[]{:S(2)}, u32[]{:S(2)}) collective-permute-start(f32[128,1664]{1,0:T(8,128)S(1)} %bitcast.54), channel_id=1, source_target_pairs={{0,1},{1,0},{2,3},{3,2},{4,5},{5,4},{6,7},{7,6},{8,9},{9,8},{10,11... | collective-permute-start | bytes 2555912 | tf_op jit(solution)/shard_map/ppermute | solution.py:20
  209.7 2.0 collective-permute-done.11.theirs
  211.7 21.4 %eliminate.1 = (f32[128,512]{1,0:T(8,128)}, f32[1,512]{1,0:T(1,128)}) custom-call(s32[1]{0:T(128)} %bitcast.core, f32[128,1664]{1,0:T(8,128)S(1)} %bitcast.55, f32[128,1664]{1,0:T(8,128)S(1)} %collective-permute-done.11.theirs, f32[128,512]{1,0:T(8,128)S(1)} %fusion.4.image_in, f32[128,512]{1,0:T(8,128)S(1)} %copy-done), custom_call_target="tpu_custom_call" | custom-call | tf_op jit(solution)/shard_map/eliminate/pallas_call | solution.py:194
  (51 shorter events, 1.5 us)
Async XLA Ops:
  0.6 35.6 %copy-start.1 = (f32[256,1280]{1,0:T(8,128)S(1)}, f32[256,1280]{1,0:T(8,128)}, u32[]{:S(2)}) copy-start(f32[256,1280]{1,0:T(8,128)} %param.16) | copy-start | bytes 3932164
  0.6 48.4 %collective-permute-start.2 = (f32[128,512]{1,0:T(8,128)}, f32[128,512]{1,0:T(8,128)S(1)}, u32[]{:S(2)}, u32[]{:S(2)}) collective-permute-start(f32[128,512]{1,0:T(8,128)} %own_in.1), channel_id=1, source_target_pairs={{0,128},{32,160},{64,192},{96,224},{128,0},{160,32},{192,64},{224,... | collective-permute-start | bytes 786440 | tf_op jit(solution)/shard_map/ppermute | solution.py:20
  10.4 54.2 %collective-permute-start.8 = (f32[128,512]{1,0:T(8,128)}, f32[128,512]{1,0:T(8,128)S(1)}, u32[]{:S(2)}, u32[]{:S(2)}) collective-permute-start(f32[128,512]{1,0:T(8,128)} %own_in.1), channel_id=1, source_target_pairs={{0,384},{32,416},{64,448},{96,480},{128,256},{160,288},{192,320},{... | collective-permute-start | bytes 786440 | tf_op jit(solution)/shard_map/ppermute | solution.py:20
  22.6 15.2 %copy-start.5 = (f32[1,1280]{1,0:T(1,128)S(1)}, f32[1,1280]{1,0:T(1,128)}, u32[]{:S(2)}) copy-start(f32[1,1280]{1,0:T(1,128)} %param.15) | copy-start | bytes 15364
  22.7 15.2 %copy-start.2 = (f32[128,256]{1,0:T(8,128)S(1)}, f32[128,256]{1,0:T(8,128)}, u32[]{:S(2)}) copy-start(f32[128,256]{1,0:T(8,128)} %param.14) | copy-start | bytes 393220
  22.7 15.4 %collective-permute-start.4 = (f32[128,256]{0,1:T(8,128)S(1)}, f32[128,256]{0,1:T(8,128)S(1)}, u32[]{:S(2)}, u32[]{:S(2)}) collective-permute-start(f32[128,256]{0,1:T(8,128)S(1)} %convolution_bitcast_fusion), channel_id=1, source_target_pairs={{0,4},{1,5},{2,6},{3,7},{4,0},{5,1},{6,2},{7,3},{8,12},{9,13},{10,... | collective-permute-start | bytes 393224 | tf_op jit(solution)/shard_map/ppermute | solution.py:20
  27.6 21.4 %collective-permute-start.3 = (f32[128,256]{1,0:T(8,128)}, f32[128,256]{1,0:T(8,128)S(1)}, u32[]{:S(2)}, u32[]{:S(2)}) collective-permute-start(f32[128,256]{1,0:T(8,128)} %param.13), channel_id=1, source_target_pairs={{0,256},{32,288},{64,320},{96,352},{128,384},{160,416},{192,448},{... | collective-permute-start | bytes 393224 | tf_op jit(solution)/shard_map/ppermute | solution.py:20
  32.4 5.6 %copy-start.3 = (f32[128,256]{1,0:T(8,128)S(1)}, f32[128,256]{1,0:T(8,128)}, u32[]{:S(2)}) copy-start(f32[128,256]{1,0:T(8,128)} %param.13) | copy-start | bytes 393220
  32.4 79.5 %collective-permute-start = (f32[136,512]{1,0:T(8,128)S(1)}, f32[136,512]{1,0:T(8,128)S(1)}, u32[]{:S(2)}, u32[]{:S(2)}) collective-permute-start(f32[136,512]{1,0:T(8,128)S(1)} %select_maximum_fusion), channel_id=1, source_target_pairs={{0,1},{1,2},{2,3},{3,4},{4,5},{5,6},{6,7},{7,8},{8,9},{9,10},{10,1... | collective-permute-start | bytes 835592 | tf_op jit(solution)/shard_map/ppermute | solution.py:26
  37.9 47.2 %copy-start = (f32[128,512]{1,0:T(8,128)S(1)}, f32[128,512]{1,0:T(8,128)}, u32[]{:S(2)}) copy-start(f32[128,512]{1,0:T(8,128)} %own_in.1) | copy-start | bytes 786436
  38.0 73.8 %collective-permute-start.1 = (f32[136,512]{1,0:T(8,128)S(1)}, f32[136,512]{1,0:T(8,128)S(1)}, u32[]{:S(2)}, u32[]{:S(2)}) collective-permute-start(f32[136,512]{1,0:T(8,128)S(1)} %select_maximum_fusion), channel_id=1, source_target_pairs={{1,0},{2,1},{3,2},{4,3},{5,4},{6,5},{7,6},{8,7},{9,8},{10,9},{11,1... | collective-permute-start | bytes 835592 | tf_op jit(solution)/shard_map/ppermute | solution.py:26
  49.4 18.6 %collective-permute-start.7 = (f32[256,256]{0,1:T(8,128)S(1)}, f32[256,256]{0,1:T(8,128)S(1)}, u32[]{:S(2)}, u32[]{:S(2)}) collective-permute-start(f32[256,256]{0,1:T(8,128)S(1)} %pad_maximum_fusion.6), channel_id=1, source_target_pairs={{0,128},{32,160},{64,192},{96,224},{128,0},{160,32},{192,64},{224,... | collective-permute-start | bytes 786440 | tf_op jit(solution)/shard_map/ppermute | solution.py:20
  57.7 27.4 %collective-permute-start.6 = (f32[128,512]{1,0:T(8,128)S(1)}, f32[128,512]{1,0:T(8,128)S(1)}, u32[]{:S(2)}, u32[]{:S(2)}) collective-permute-start(f32[128,512]{1,0:T(8,128)S(1)} %collective-permute-done.2), channel_id=1, source_target_pairs={{0,384},{32,416},{64,448},{96,480},{128,256},{160,288},{192,320},{... | collective-permute-start | bytes 786440 | tf_op jit(solution)/shard_map/ppermute | solution.py:20
  64.7 27.8 %collective-permute-start.5 = (f32[256,256]{0,1:T(8,128)}, f32[256,256]{0,1:T(8,128)S(1)}, u32[]{:S(2)}, u32[]{:S(2)}) collective-permute-start(f32[256,256]{0,1:T(8,128)} %fusion.24), channel_id=1, source_target_pairs={{0,8},{1,9},{2,10},{3,11},{4,12},{5,13},{6,14},{7,15},{8,0},{9,1},... | collective-permute-start | bytes 786440 | tf_op jit(solution)/shard_map/ppermute | solution.py:20
  85.8 5.9 %copy-start.4 = (f32[3,128]{1,0:T(4,128)S(1)}, f32[3,128]{1,0:T(4,128)}, u32[]{:S(2)}) copy-start(f32[3,128]{1,0:T(4,128)} %param.10) | copy-start | bytes 4612
  85.8 6.0 %copy-start.6 = (s32[1,2]{1,0:T(1,128)S(1)}, s32[1,2]{1,0:T(1,128)}, u32[]{:S(2)}) copy-start(s32[1,2]{1,0:T(1,128)} %param.12) | copy-start | bytes 28
  87.0 16.4 %collective-permute-start.9 = (f32[256,512]{1,0:T(8,128)S(1)}, f32[256,512]{1,0:T(8,128)S(1)}, u32[]{:S(2)}, u32[]{:S(2)}) collective-permute-start(f32[256,512]{1,0:T(8,128)S(1)} %convolution_add_fusion.1), channel_id=1, source_target_pairs={{0,16},{1,17},{2,18},{3,19},{4,20},{5,21},{6,22},{7,23},{8,24},{9,... | collective-permute-start | bytes 1572872 | tf_op jit(solution)/shard_map/ppermute | solution.py:20
  106.1 19.8 %all-to-all-start = ((f32[4,128,512]{2,1,0:T(8,128)}), f32[4,128,512]{2,1,0:T(8,128)S(1)}, u32[]{:S(2)}, u32[]{:S(2)}) async-start(f32[4,128,512]{2,1,0:T(8,128)} %bitcast.24), calls=%async_computation | async-start | bytes 2097152 | tf_op jit(solution)/shard_map/all_to_all | solution.py:329
  127.4 4.5 %collective-permute-start.10 = (f32[128,512]{1,0:T(8,128)S(1)}, f32[128,512]{1,0:T(8,128)S(1)}, u32[]{:S(2)}, u32[]{:S(2)}) collective-permute-start(f32[128,512]{1,0:T(8,128)S(1)} %fusion.4.image_in), channel_id=1, source_target_pairs={{0,1},{1,0},{2,3},{3,2},{4,5},{5,4},{6,7},{7,6},{8,9},{9,8},{10,11... | collective-permute-start | bytes 786440 | tf_op jit(solution)/shard_map/ppermute | solution.py:20
  200.6 11.0 %collective-permute-start.11 = (f32[128,1664]{1,0:T(8,128)S(1)}, f32[128,1664]{1,0:T(8,128)S(1)}, u32[]{:S(2)}, u32[]{:S(2)}) collective-permute-start(f32[128,1664]{1,0:T(8,128)S(1)} %bitcast.54), channel_id=1, source_target_pairs={{0,1},{1,0},{2,3},{3,2},{4,5},{5,4},{6,7},{7,6},{8,9},{9,8},{10,11... | collective-permute-start | bytes 2555912 | tf_op jit(solution)/shard_map/ppermute | solution.py:20

commit v6 on v5

--- a/solution.py
+++ b/solution.py
@@ -246,18 +246,23 @@
 
 def half_of_sums(core, image, own, pair_image, pair_own, own_squares):
     odd = core == 1
-    images = jnp.concatenate([image, pair_image], axis=0)
-    owns = jnp.concatenate([own, pair_own], axis=0)
-    blocks = [images[:, k * 128 : k * 128 + 128] for k in range(4)]
-    wide = matmul_hi(jnp.where(odd, blocks[1], blocks[0]), images, 0, 0)
+
+    def part(one, other):
+        blocks = [one[:, k * 128 : k * 128 + 128] for k in range(4)]
+        return (
+            matmul_hi(jnp.where(odd, blocks[1], blocks[0]), one, 0, 0),
+            matmul_hi(jnp.where(odd, blocks[2], blocks[3]), one[:, 256:], 0, 0),
+            matmul_hi(jnp.where(odd, one[:, 256:], one[:, :256]), other, 0, 0),
+        )
+
+    parts = zip(part(image, own), part(pair_image, pair_own))
+    wide, narrow, cross_part = (first + second for first, second in parts)
     wide = wide.at[120:, :64].set(own_squares.reshape(8, 64))
-    narrow = matmul_hi(jnp.where(odd, blocks[2], blocks[3]), images[:, 256:], 0, 0)
     gram_part = jnp.where(
         odd,
         jnp.concatenate([wide[:, 128:], narrow], axis=1),
         jnp.concatenate([wide, narrow[:, 128:]], axis=1),
     )
-    cross_part = matmul_hi(jnp.where(odd, images[:, 256:], images[:, :256]), owns, 0, 0)
     return jnp.concatenate([gram_part, cross_part[:128], cross_part[128:]], axis=1)
 
 

time: 234 us -> 235 us (level)
  waiting for transfers between devices: 52.8 us -> 49 us
  matrix products: 15.1 us -> 17.9 us
    ppermute x10, waiting for transfers between devices: 40.2 us -> 35.8 us  [swapped(): lax.ppermute(block, axis, [(i, i ^ bits) for i in range(lax.axis_size(axi...]
    dot_general x19 -> x22, matrix products: 15.1 us -> 17.9 us  [matmul_hi(): return lax.dot_general(left, right, dims, precision=lax.Precision.HIGHEST)]
  transfers between devices with their start and end apart: 13 -> 13, of which waited for: 7 -> 6; matrix products, arithmetic and copies ran while one was open for 6% -> 9% of each run, Pallas kernels for 0% -> 0%
where the time goes in v6:
time: 235 us; the launch traced here: 234 us
  starting transfers between devices  72.2 us (31%)
  blocking collectives  66.4 us (28%)
  waiting for transfers between devices  49 us (21%)
  Pallas kernels  21.3 us (9%)
  matrix products  17.9 us (8%)
  other arithmetic  3.32 us (1%)
  local copies, waits for them, and re-layouts  3.09 us (1%)
    ppermute x10, starting transfers between devices, swapped(): lax.ppermute(block, axis, [(i, i ^ bits) for i in range(lax.axis_size(axi...  61.3 us
    ppermute x10, waiting for transfers between devices, swapped(): lax.ppermute(block, axis, [(i, i ^ bits) for i in range(lax.axis_size(axi...  35.8 us
    all_to_all x3, blocking collectives, in_quads(): lax.all_to_all(tiles, 'row', 0, 0, axis_index_groups=groups, tiled=True)  33.7 us
    all_to_all x2, blocking collectives, within_plane(): lax.all_to_all(tiles, 'col', 0, 0, axis_index_groups=plane_groups(), tile...  32.7 us
    pallas_call x1, Pallas kernels, project_out(): pl.pallas_call(functools.partial(eliminate, points_total), in_specs=[pl.B...  21.3 us
    dot_general x22, matrix products, matmul_hi(): return lax.dot_general(left, right, dims, precision=lax.Precision.HIGHEST)  17.9 us
    all_to_all x1, waiting for transfers between devices, shards(): lax.all_to_all(given, 'col', 0, 0, axis_index_groups=quads, tiled=True)  13.2 us
    ppermute x2, starting transfers between devices, from_behind(): return lax.ppermute(block, axis, route)  5.62 us
  transfers between devices with their start and end apart: 13, of which 6 were waited for; matrix products, arithmetic and copies ran while one was open for 9% of the time, Pallas kernels for 0%

profile of v6, /device:TPU:1, one launch (start us, length us, event | category | flops | bytes accessed | tf_op | source)
XLA Modules:
  0.0 234.4 jit_solution(8128795716488210964)
XLA Ops:
  0.7 9.8 %collective-permute-start.2 = (f32[128,512]{1,0:T(8,128)}, f32[128,512]{1,0:T(8,128)}, u32[]{:S(2)}, u32[]{:S(2)}) collective-permute-start(f32[128,512]{1,0:T(8,128)} %own_in.1), channel_id=1, source_target_pairs={{0,128},{32,160},{64,192},{96,224},{128,0},{160,32},{192,64},{224,... | collective-permute-start | bytes 786440 | tf_op jit(solution)/shard_map/ppermute | solution.py:20
  10.5 8.8 %collective-permute-start.8 = (f32[128,512]{1,0:T(8,128)}, f32[128,512]{1,0:T(8,128)}, u32[]{:S(2)}, u32[]{:S(2)}) collective-permute-start(f32[128,512]{1,0:T(8,128)} %own_in.1), channel_id=1, source_target_pairs={{0,384},{32,416},{64,448},{96,480},{128,256},{160,288},{192,320},{... | collective-permute-start | bytes 786440 | tf_op jit(solution)/shard_map/ppermute | solution.py:20
  19.3 0.7 fusion.146
  20.0 1.3 fusion.31
  21.4 1.9 convolution_bitcast_fusion
  23.3 4.8 %collective-permute-start.4 = (f32[128,256]{0,1:T(8,128)}, f32[128,256]{0,1:T(8,128)S(1)}, u32[]{:S(2)}, u32[]{:S(2)}) collective-permute-start(f32[128,256]{0,1:T(8,128)} %convolution_bitcast_fusion), channel_id=1, source_target_pairs={{0,4},{1,5},{2,6},{3,7},{4,0},{5,1},{6,2},{7,3},{8,12},{9,13},{10,... | collective-permute-start | bytes 393224 | tf_op jit(solution)/shard_map/ppermute | solution.py:20
  28.2 3.7 %collective-permute-start.3 = (f32[128,256]{1,0:T(8,128)}, f32[128,256]{1,0:T(8,128)S(1)}, u32[]{:S(2)}, u32[]{:S(2)}) collective-permute-start(f32[128,256]{1,0:T(8,128)} %param.13), channel_id=1, source_target_pairs={{0,256},{32,288},{64,320},{96,352},{128,384},{160,416},{192,448},{... | collective-permute-start | bytes 393224 | tf_op jit(solution)/shard_map/ppermute | solution.py:20
  31.9 1.7 select_maximum_fusion
  33.6 3.7 %collective-permute-start = (f32[136,512]{1,0:T(8,128)}, f32[136,512]{1,0:T(8,128)S(1)}, u32[]{:S(2)}, u32[]{:S(2)}) collective-permute-start(f32[136,512]{1,0:T(8,128)} %select_maximum_fusion), channel_id=1, source_target_pairs={{0,1},{1,2},{2,3},{3,4},{4,5},{5,6},{6,7},{7,8},{8,9},{9,10},{10,1... | collective-permute-start | bytes 835592 | tf_op jit(solution)/shard_map/ppermute | solution.py:26
  37.5 0.4 fusion.27
  37.9 0.6 fusion.145
  38.5 0.4 fusion.25
  38.9 0.4 fusion.23
  39.9 1.9 collective-permute-start.1
  41.8 7.2 %collective-permute-done.3 = f32[128,256]{1,0:T(8,128)S(1)} collective-permute-done((f32[128,256]{1,0:T(8,128)}, f32[128,256]{1,0:T(8,128)S(1)}, u32[]{:S(2)}, u32[]{:S(2)}) %collective-permute-start.3) | collective-permute-done | bytes 131104 | tf_op jit(solution)/shard_map/ppermute | solution.py:20
  49.4 8.3 %collective-permute-start.7 = (f32[256,256]{0,1:T(8,128)S(1)}, f32[256,256]{0,1:T(8,128)S(1)}, u32[]{:S(2)}, u32[]{:S(2)}) collective-permute-start(f32[256,256]{0,1:T(8,128)S(1)} %pad_maximum_fusion), channel_id=1, source_target_pairs={{0,128},{32,160},{64,192},{96,224},{128,0},{160,32},{192,64},{224,... | collective-permute-start | bytes 786440 | tf_op jit(solution)/shard_map/ppermute | solution.py:20
  57.6 5.8 %collective-permute-start.6 = (f32[128,512]{1,0:T(8,128)}, f32[128,512]{1,0:T(8,128)S(1)}, u32[]{:S(2)}, u32[]{:S(2)}) collective-permute-start(f32[128,512]{1,0:T(8,128)} %collective-permute-done.2), channel_id=1, source_target_pairs={{0,384},{32,416},{64,448},{96,480},{128,256},{160,288},{192,320},{... | collective-permute-start | bytes 786440 | tf_op jit(solution)/shard_map/ppermute | solution.py:20
  63.5 1.1 fusion.19
  64.6 3.1 %collective-permute-start.5 = (f32[256,256]{0,1:T(8,128)}, f32[256,256]{0,1:T(8,128)}, u32[]{:S(2)}, u32[]{:S(2)}) collective-permute-start(f32[256,256]{0,1:T(8,128)} %fusion.19), channel_id=1, source_target_pairs={{0,8},{1,9},{2,10},{3,11},{4,12},{5,13},{6,14},{7,15},{8,0},{9,1},... | collective-permute-start | bytes 786440 | tf_op jit(solution)/shard_map/ppermute | solution.py:20
  67.8 17.9 %collective-permute-done.6 = f32[128,512]{1,0:T(8,128)S(1)} collective-permute-done((f32[128,512]{1,0:T(8,128)}, f32[128,512]{1,0:T(8,128)S(1)}, u32[]{:S(2)}, u32[]{:S(2)}) %collective-permute-start.6) | collective-permute-done | bytes 262176 | tf_op jit(solution)/shard_map/ppermute | solution.py:20
  85.7 0.6 convolution_multiply_fusion
  86.3 0.6 fusion.149
  87.0 1.7 convolution_add_fusion.2
  88.6 4.7 %collective-permute-start.9 = (f32[256,512]{1,0:T(8,128)S(1)}, f32[256,512]{1,0:T(8,128)S(1)}, u32[]{:S(2)}, u32[]{:S(2)}) collective-permute-start(f32[256,512]{1,0:T(8,128)S(1)} %convolution_add_fusion.2), channel_id=1, source_target_pairs={{0,16},{1,17},{2,18},{3,19},{4,20},{5,21},{6,22},{7,23},{8,24},{9,... | collective-permute-start | bytes 1572872 | tf_op jit(solution)/shard_map/ppermute | solution.py:20
  93.3 0.6 fusion.147
  93.9 0.7 fusion.89
  94.7 1.1 broadcast_select_fusion.3
  95.8 8.7 %collective-permute-done.9 = f32[256,512]{1,0:T(8,128)S(1)} collective-permute-done((f32[256,512]{1,0:T(8,128)S(1)}, f32[256,512]{1,0:T(8,128)S(1)}, u32[]{:S(2)}, u32[]{:S(2)}) %collective-permute-start.9) | collective-permute-done | bytes 524320 | tf_op jit(solution)/shard_map/ppermute | solution.py:20
  104.4 0.7 convolution_add_fusion.1
  105.1 2.0 fusion.5
  107.1 5.3 %all-to-all-start = ((f32[4,128,512]{2,1,0:T(8,128)}), f32[4,128,512]{2,1,0:T(8,128)S(1)}, u32[]{:S(2)}, u32[]{:S(2)}) async-start(f32[4,128,512]{2,1,0:T(8,128)} %bitcast.24), calls=%async_computation | async-start | bytes 2097152 | tf_op jit(solution)/shard_map/all_to_all | solution.py:334
  112.6 1.3 fusion.2
  113.9 13.2 %all-to-all-done = f32[4,128,512]{2,1,0:T(8,128)S(1)} async-done(((f32[4,128,512]{2,1,0:T(8,128)}), f32[4,128,512]{2,1,0:T(8,128)S(1)}, u32[]{:S(2)}, u32[]{:S(2)}) %all-to-all-start) | async-done | bytes 1048608 | tf_op jit(solution)/shard_map/all_to_all | solution.py:334
  127.1 1.4 fusion.4.image_in
  128.5 3.5 %collective-permute-start.10 = (f32[128,512]{1,0:T(8,128)S(1)}, f32[128,512]{1,0:T(8,128)S(1)}, u32[]{:S(2)}, u32[]{:S(2)}) collective-permute-start(f32[128,512]{1,0:T(8,128)S(1)} %fusion.4.image_in), channel_id=1, source_target_pairs={{0,1},{1,0},{2,3},{3,2},{4,5},{5,4},{6,7},{7,6},{8,9},{9,8},{10,11... | collective-permute-start | bytes 786440 | tf_op jit(solution)/shard_map/ppermute | solution.py:20
  132.1 0.4 fusion.59
  132.8 0.6 fusion.45
  133.5 0.4 convolution_add_fusion.3
  133.9 0.4 scatter.4
  134.7 0.6 convolution_add_fusion
  135.5 18.5 %all_to_all.30 = f32[16,8,1664]{2,1,0:T(8,128)S(1)} all-to-all(f32[16,8,1664]{2,1,0:T(8,128)S(1)} %maximum_bitcast_fusion), channel_id=1, replica_groups={{0,2,4,6,8,10,12,14,16,18,20,22,24,26,28,30},{1,3,5,7,9,11,13,15,17,19,..., dimensions={0} | all-to-all | bytes 1703936 | tf_op jit(solution)/shard_map/all_to_all | solution.py:218
  154.2 8.5 %all_to_all.31 = f32[4,8,416]{2,1,0:T(8,128)S(1)} all-to-all(f32[4,8,416]{2,1,0:T(8,128)S(1)} %copy.20), channel_id=1, replica_groups={{0,32,64,96},{128,160,192,224},{256,288,320,352},{384,416,448,480},{1,3..., dimensions={0} | all-to-all | bytes 106496 | tf_op jit(solution)/shard_map/all_to_all | solution.py:222
  162.7 18.3 %all_to_all.32 = f32[4,8,416]{2,1,0:T(8,128)S(1)} all-to-all(f32[4,8,416]{2,1,0:T(8,128)S(1)} %broadcast_in_dim.11), channel_id=1, replica_groups={{0,128,256,384},{32,160,288,416},{64,192,320,448},{96,224,352,480},{1,1..., dimensions={0} | all-to-all | bytes 106496 | tf_op jit(solution)/shard_map/all_to_all | solution.py:222
  181.0 7.0 %all_to_all.33 = f32[4,8,416]{2,1,0:T(8,128)S(1)} all-to-all(f32[4,8,416]{2,1,0:T(8,128)S(1)} %broadcast_in_dim.12), channel_id=1, replica_groups={{0,32,64,96},{128,160,192,224},{256,288,320,352},{384,416,448,480},{1,3..., dimensions={0} | all-to-all | bytes 106496 | tf_op jit(solution)/shard_map/all_to_all | solution.py:222
  188.2 14.2 %all_to_all.34 = f32[16,8,1664]{2,1,0:T(8,128)S(1)} all-to-all(f32[16,8,1664]{2,1,0:T(8,128)S(1)} %broadcast_in_dim.27), channel_id=1, replica_groups={{0,2,4,6,8,10,12,14,16,18,20,22,24,26,28,30},{1,3,5,7,9,11,13,15,17,19,..., dimensions={0} | all-to-all | bytes 1703936 | tf_op jit(solution)/shard_map/all_to_all | solution.py:218
  202.4 8.8 %collective-permute-start.11 = (f32[128,1664]{1,0:T(8,128)S(1)}, f32[128,1664]{1,0:T(8,128)S(1)}, u32[]{:S(2)}, u32[]{:S(2)}) collective-permute-start(f32[128,1664]{1,0:T(8,128)S(1)} %bitcast.57), channel_id=1, source_target_pairs={{0,1},{1,0},{2,3},{3,2},{4,5},{5,4},{6,7},{7,6},{8,9},{9,8},{10,11... | collective-permute-start | bytes 2555912 | tf_op jit(solution)/shard_map/ppermute | solution.py:20
  211.2 2.0 collective-permute-done.11.theirs
  213.2 21.3 %eliminate.1 = (f32[128,512]{1,0:T(8,128)}, f32[1,512]{1,0:T(1,128)}) custom-call(s32[1]{0:T(128)} %bitcast.core, f32[128,1664]{1,0:T(8,128)S(1)} %bitcast.58, f32[128,1664]{1,0:T(8,128)S(1)} %collective-permute-done.11.theirs, f32[128,512]{1,0:T(8,128)S(1)} %fusion.4.image_in, f32[128,512]{1,0:T(8,128)S(1)} %copy-done), custom_call_target="tpu_custom_call" | custom-call | tf_op jit(solution)/shard_map/eliminate/pallas_call | solution.py:194
  (62 shorter events, 2.5 us)
Async XLA Ops:
  0.6 36.8 %copy-start.1 = (f32[256,1280]{1,0:T(8,128)S(1)}, f32[256,1280]{1,0:T(8,128)}, u32[]{:S(2)}) copy-start(f32[256,1280]{1,0:T(8,128)} %param.16) | copy-start | bytes 3932164
  0.6 36.7 %copy-start.2 = (f32[128,256]{1,0:T(8,128)S(1)}, f32[128,256]{1,0:T(8,128)}, u32[]{:S(2)}) copy-start(f32[128,256]{1,0:T(8,128)} %param.14) | copy-start | bytes 393220
  0.7 37.8 %copy-start.3 = (f32[128,256]{1,0:T(8,128)S(1)}, f32[128,256]{1,0:T(8,128)}, u32[]{:S(2)}) copy-start(f32[128,256]{1,0:T(8,128)} %param.13) | copy-start | bytes 393220
  0.7 37.2 %copy-start.7 = (f32[1,1280]{1,0:T(1,128)S(1)}, f32[1,1280]{1,0:T(1,128)}, u32[]{:S(2)}) copy-start(f32[1,1280]{1,0:T(1,128)} %param.15) | copy-start | bytes 15364
  0.7 48.3 %collective-permute-start.2 = (f32[128,512]{1,0:T(8,128)}, f32[128,512]{1,0:T(8,128)}, u32[]{:S(2)}, u32[]{:S(2)}) collective-permute-start(f32[128,512]{1,0:T(8,128)} %own_in.1), channel_id=1, source_target_pairs={{0,128},{32,160},{64,192},{96,224},{128,0},{160,32},{192,64},{224,... | collective-permute-start | bytes 786440 | tf_op jit(solution)/shard_map/ppermute | solution.py:20
  10.5 54.1 %collective-permute-start.8 = (f32[128,512]{1,0:T(8,128)}, f32[128,512]{1,0:T(8,128)}, u32[]{:S(2)}, u32[]{:S(2)}) collective-permute-start(f32[128,512]{1,0:T(8,128)} %own_in.1), channel_id=1, source_target_pairs={{0,384},{32,416},{64,448},{96,480},{128,256},{160,288},{192,320},{... | collective-permute-start | bytes 786440 | tf_op jit(solution)/shard_map/ppermute | solution.py:20
  23.3 16.5 %collective-permute-start.4 = (f32[128,256]{0,1:T(8,128)}, f32[128,256]{0,1:T(8,128)S(1)}, u32[]{:S(2)}, u32[]{:S(2)}) collective-permute-start(f32[128,256]{0,1:T(8,128)} %convolution_bitcast_fusion), channel_id=1, source_target_pairs={{0,4},{1,5},{2,6},{3,7},{4,0},{5,1},{6,2},{7,3},{8,12},{9,13},{10,... | collective-permute-start | bytes 393224 | tf_op jit(solution)/shard_map/ppermute | solution.py:20
  28.2 20.9 %collective-permute-start.3 = (f32[128,256]{1,0:T(8,128)}, f32[128,256]{1,0:T(8,128)S(1)}, u32[]{:S(2)}, u32[]{:S(2)}) collective-permute-start(f32[128,256]{1,0:T(8,128)} %param.13), channel_id=1, source_target_pairs={{0,256},{32,288},{64,320},{96,352},{128,384},{160,416},{192,448},{... | collective-permute-start | bytes 393224 | tf_op jit(solution)/shard_map/ppermute | solution.py:20
  33.6 78.8 %collective-permute-start = (f32[136,512]{1,0:T(8,128)}, f32[136,512]{1,0:T(8,128)S(1)}, u32[]{:S(2)}, u32[]{:S(2)}) collective-permute-start(f32[136,512]{1,0:T(8,128)} %select_maximum_fusion), channel_id=1, source_target_pairs={{0,1},{1,2},{2,3},{3,4},{4,5},{5,6},{6,7},{7,8},{8,9},{9,10},{10,1... | collective-permute-start | bytes 835592 | tf_op jit(solution)/shard_map/ppermute | solution.py:26
  37.4 2.4 %copy-start.6 = (f32[3,128]{1,0:T(4,128)S(1)}, f32[3,128]{1,0:T(4,128)}, u32[]{:S(2)}) copy-start(f32[3,128]{1,0:T(4,128)} %param.10) | copy-start | bytes 4612
  38.5 10.9 %copy-start.4 = (f32[1,256]{1,0:T(1,128)}, f32[1,256]{1,0:T(1,128)S(1)}, u32[]{:S(2)}) copy-start(f32[1,256]{1,0:T(1,128)S(1)} %get-tuple-element.44) | copy-start | bytes 3076
  38.9 24.5 %copy-start = (f32[128,512]{1,0:T(8,128)S(1)}, f32[128,512]{1,0:T(8,128)}, u32[]{:S(2)}) copy-start(f32[128,512]{1,0:T(8,128)} %own_in.1) | copy-start | bytes 786436
  38.9 24.6 %copy-start.10 = (s32[1,2]{1,0:T(1,128)S(1)}, s32[1,2]{1,0:T(1,128)}, u32[]{:S(2)}) copy-start(s32[1,2]{1,0:T(1,128)} %param.12) | copy-start | bytes 28
  39.9 72.6 %collective-permute-start.1 = (f32[136,512]{1,0:T(8,128)}, f32[136,512]{1,0:T(8,128)S(1)}, u32[]{:S(2)}, u32[]{:S(2)}) collective-permute-start(f32[136,512]{1,0:T(8,128)} %select_maximum_fusion), channel_id=1, source_target_pairs={{1,0},{2,1},{3,2},{4,3},{5,4},{6,5},{7,6},{8,7},{9,8},{10,9},{11,1... | collective-permute-start | bytes 835592 | tf_op jit(solution)/shard_map/ppermute | solution.py:26
  49.4 18.4 %collective-permute-start.7 = (f32[256,256]{0,1:T(8,128)S(1)}, f32[256,256]{0,1:T(8,128)S(1)}, u32[]{:S(2)}, u32[]{:S(2)}) collective-permute-start(f32[256,256]{0,1:T(8,128)S(1)} %pad_maximum_fusion), channel_id=1, source_target_pairs={{0,128},{32,160},{64,192},{96,224},{128,0},{160,32},{192,64},{224,... | collective-permute-start | bytes 786440 | tf_op jit(solution)/shard_map/ppermute | solution.py:20
  57.6 28.0 %collective-permute-start.6 = (f32[128,512]{1,0:T(8,128)}, f32[128,512]{1,0:T(8,128)S(1)}, u32[]{:S(2)}, u32[]{:S(2)}) collective-permute-start(f32[128,512]{1,0:T(8,128)} %collective-permute-done.2), channel_id=1, source_target_pairs={{0,384},{32,416},{64,448},{96,480},{128,256},{160,288},{192,320},{... | collective-permute-start | bytes 786440 | tf_op jit(solution)/shard_map/ppermute | solution.py:20
  64.6 30.0 %collective-permute-start.5 = (f32[256,256]{0,1:T(8,128)}, f32[256,256]{0,1:T(8,128)}, u32[]{:S(2)}, u32[]{:S(2)}) collective-permute-start(f32[256,256]{0,1:T(8,128)} %fusion.19), channel_id=1, source_target_pairs={{0,8},{1,9},{2,10},{3,11},{4,12},{5,13},{6,14},{7,15},{8,0},{9,1},... | collective-permute-start | bytes 786440 | tf_op jit(solution)/shard_map/ppermute | solution.py:20
  86.9 7.7 %copy-start.5 = (f32[1,256]{1,0:T(1,128)S(1)}, f32[1,256]{1,0:T(1,128)}, u32[]{:S(2)}) copy-start(f32[1,256]{1,0:T(1,128)} %copy-done.4) | copy-start | bytes 3076
  86.9 7.7 %copy-start.9 = (f32[1,256]{1,0:T(1,128)S(1)}, f32[1,256]{1,0:T(1,128)}, u32[]{:S(2)}) copy-start(f32[1,256]{1,0:T(1,128)} %get-tuple-element.42) | copy-start | bytes 3076
  86.9 17.5 %copy-start.8 = (f32[1,256]{1,0:T(1,128)S(1)}, f32[1,256]{1,0:T(1,128)}, u32[]{:S(2)}) copy-start(f32[1,256]{1,0:T(1,128)} %get-tuple-element.43) | copy-start | bytes 3076
  88.6 15.8 %collective-permute-start.9 = (f32[256,512]{1,0:T(8,128)S(1)}, f32[256,512]{1,0:T(8,128)S(1)}, u32[]{:S(2)}, u32[]{:S(2)}) collective-permute-start(f32[256,512]{1,0:T(8,128)S(1)} %convolution_add_fusion.2), channel_id=1, source_target_pairs={{0,16},{1,17},{2,18},{3,19},{4,20},{5,21},{6,22},{7,23},{8,24},{9,... | collective-permute-start | bytes 1572872 | tf_op jit(solution)/shard_map/ppermute | solution.py:20
  107.1 19.9 %all-to-all-start = ((f32[4,128,512]{2,1,0:T(8,128)}), f32[4,128,512]{2,1,0:T(8,128)S(1)}, u32[]{:S(2)}, u32[]{:S(2)}) async-start(f32[4,128,512]{2,1,0:T(8,128)} %bitcast.24), calls=%async_computation | async-start | bytes 2097152 | tf_op jit(solution)/shard_map/all_to_all | solution.py:334
  128.5 4.9 %collective-permute-start.10 = (f32[128,512]{1,0:T(8,128)S(1)}, f32[128,512]{1,0:T(8,128)S(1)}, u32[]{:S(2)}, u32[]{:S(2)}) collective-permute-start(f32[128,512]{1,0:T(8,128)S(1)} %fusion.4.image_in), channel_id=1, source_target_pairs={{0,1},{1,0},{2,3},{3,2},{4,5},{5,4},{6,7},{7,6},{8,9},{9,8},{10,11... | collective-permute-start | bytes 786440 | tf_op jit(solution)/shard_map/ppermute | solution.py:20
  202.4 10.8 %collective-permute-start.11 = (f32[128,1664]{1,0:T(8,128)S(1)}, f32[128,1664]{1,0:T(8,128)S(1)}, u32[]{:S(2)}, u32[]{:S(2)}) collective-permute-start(f32[128,1664]{1,0:T(8,128)S(1)} %bitcast.57), channel_id=1, source_target_pairs={{0,1},{1,0},{2,3},{3,2},{4,5},{5,4},{6,7},{7,6},{8,9},{9,8},{10,11... | collective-permute-start | bytes 2555912 | tf_op jit(solution)/shard_map/ppermute | solution.py:20
